TPU v7x, 32 devices: a whole 2x2x4 slice. The times are simulated.
32 devices in a mesh: dev: 32 (over z, y, x, core).
Axes of the slice: x: 2, y: 2, z: 4, core: 2. Of those that a mesh axis runs over, the one named last changes fastest.
Arguments:
- params: float32 [9, 32768], P(None, 'dev')
- moment: float32 [9, 32768], P(None, 'dev'), may hold values from -3 to 3
- second: float32 [9, 32768], P(None, 'dev'), may hold values from 0.05 to 1
- fetch_ids: int32 [32, 32, 8], P('dev'), may hold values from 0 to 1023
- seg_ids: int32 [128, 256], P('dev'), may hold values from 0 to 255
- seg_count: int32 [128], P('dev'), may hold values from 1 to 256, 24576 in all
- seg_perm: int32 [128], replicated, may hold values from 0 to 127, as said below
- target: float32 [32, 3, 256], P('dev'), may hold values from 0 to 1
Outputs:
- image: float32 [32, 3, 256], P('dev')
- new_params: float32 [9, 32768], P(None, 'dev')
- new_moment: float32 [9, 32768], P(None, 'dev')
- new_second: float32 [9, 32768], P(None, 'dev')
Inputs may be any that keep to these rules, and one draw needn't show every extreme that they name: `seg_count`: segments that exceed their count hold unused slots; some segment is full. `seg_perm`: each number appears once.
All inputs are finite; a program needn't handle non-finite values. No bound on the sum of `seg_count` on one device may be relied on, other than what follows from the above.
Results may differ from a plain program's by a relative error of at most 0.0003.
Values sent between devices are 32-bit elements; how exact they have to be, the bound alone decides.
No kernel may reach another device: no remote copies, remote signals or barrier semaphores. Data moves between devices by JAX's collectives and lax.ppermute only.
A program may use at most 192 MiB of HBM per device.

v0:
```python
import jax
import jax.numpy as jnp
from jax import lax
from jax.sharding import PartitionSpec as P

TILES_X = 8
KSEG = 4


def segment(par, count, tile):
    span = par.shape[1]
    pidx = jnp.arange(256, dtype=jnp.int32)
    fine_x = ((pidx % 16).astype(jnp.float32) + 0.5) / 16.0
    fine_y = ((pidx // 16).astype(jnp.float32) + 0.5) / 16.0
    pos_x = (tile % TILES_X).astype(jnp.float32) + fine_x
    pos_y = (tile // TILES_X).astype(jnp.float32) + fine_y
    steps = jnp.arange(span, dtype=jnp.int32)
    live = (steps < count).astype(jnp.float32)
    delta_x = pos_x[None, :] - par[0][:, None]
    delta_y = pos_y[None, :] - par[1][:, None]
    scale_a = jnp.exp(par[2])
    scale_c = jnp.exp(par[3])
    cross = 0.8 * jnp.tanh(par[4]) * scale_a * scale_c
    power = -0.5 * (
        (scale_a * scale_a)[:, None] * delta_x * delta_x
        + 2.0 * cross[:, None] * delta_x * delta_y
        + (scale_c * scale_c)[:, None] * delta_y * delta_y
    )
    alpha = (0.95 * jax.nn.sigmoid(par[5]) * live)[:, None] * jnp.exp(power)
    logt = jnp.log1p(-alpha)
    lower = (steps[:, None] > steps[None, :]).astype(jnp.float32)
    earlier = jnp.dot(lower, logt, precision=lax.Precision.HIGHEST)
    weight = jnp.exp(earlier) * alpha
    colour = jnp.dot(par[6:9], weight, precision=lax.Precision.HIGHEST)
    return (colour, jnp.sum(logt, axis=0))


def per_device(params, moment, second, fetch_ids, seg_ids, seg_count, seg_perm, target):
    ndev = lax.axis_size("dev")
    me = lax.axis_index("dev")
    nparam, owned = params.shape
    segs, span = seg_ids.shape
    tiles_dev = target.shape[0]
    pixels = target.shape[2]
    wanted = fetch_ids[0]
    cap = wanted.shape[1]
    received = lax.all_to_all(wanted, "dev", split_axis=0, concat_axis=0, tiled=True)
    buckets = jnp.take(params, received, axis=1)
    arrived = lax.all_to_all(buckets, "dev", split_axis=1, concat_axis=1, tiled=True)
    buffer = arrived.reshape(nparam, ndev * cap)
    first = me * segs
    own_perm = lax.dynamic_slice_in_dim(seg_perm, first, segs, 0)
    own_tile = own_perm // KSEG
    own_rank = own_perm % KSEG
    gathered_par = jnp.moveaxis(jnp.take(buffer, seg_ids, axis=1), 1, 0)

    def partials(values):
        return jax.vmap(segment)(values, seg_count, own_tile)

    (colours, logs), back = jax.vjp(partials, gathered_par)
    all_colours, all_logs, all_target = (
        lax.all_gather(colours, "dev", axis=0, tiled=True),
        lax.all_gather(logs, "dev", axis=0, tiled=True),
        lax.all_gather(target, "dev", axis=0, tiled=True),
    )
    total = all_logs.shape[0]
    ntiles = all_target.shape[0]
    tile_all = seg_perm // KSEG
    rank_all = seg_perm % KSEG
    same = tile_all[:, None] == tile_all[None, :]
    before = (same & (rank_all[None, :] < rank_all[:, None])).astype(jnp.float32)
    prefix = jnp.exp(jnp.dot(before, all_logs, precision=lax.Precision.HIGHEST))
    contrib = (prefix[:, None, :] * all_colours).reshape(total, 3 * pixels)
    onehot = (jnp.arange(ntiles, dtype=jnp.int32)[:, None] == tile_all[None, :]).astype(jnp.float32)
    image = jnp.dot(onehot, contrib, precision=lax.Precision.HIGHEST)
    misfit = image - all_target.reshape(ntiles, 3 * pixels)
    later = (
        (own_tile[:, None] == tile_all[None, :]) & (rank_all[None, :] > own_rank[:, None])
    ).astype(jnp.float32)
    behind = jnp.dot(later, contrib, precision=lax.Precision.HIGHEST).reshape(segs, 3, pixels)
    picker = (own_tile[:, None] == jnp.arange(ntiles, dtype=jnp.int32)[None, :]).astype(jnp.float32)
    error = jnp.dot(picker, misfit, precision=lax.Precision.HIGHEST).reshape(segs, 3, pixels)
    own_prefix = lax.dynamic_slice_in_dim(prefix, first, segs, 0)
    d_colour = own_prefix[:, None, :] * error
    d_log = jnp.sum(error * behind, axis=1)
    (d_par,) = back((d_colour, d_log))
    slot_grad = (
        jnp.zeros((nparam, ndev * cap), jnp.float32)
        .at[:, seg_ids.reshape(-1)]
        .add(jnp.moveaxis(d_par, 1, 0).reshape(nparam, segs * span))
    )
    returned = lax.all_to_all(
        slot_grad.reshape(nparam, ndev, cap), "dev", split_axis=1, concat_axis=1, tiled=True
    )
    grad = (
        jnp.zeros((nparam, owned), jnp.float32)
        .at[:, received.reshape(-1)]
        .add(returned.reshape(nparam, ndev * cap))
    )
    new_moment = 0.9 * moment + 0.1 * grad
    new_second = 0.99 * second + 0.01 * grad * grad
    new_params = params - 0.05 * new_moment / (jnp.sqrt(new_second) + 1e-08)
    my_image = lax.dynamic_slice_in_dim(image, me * tiles_dev, tiles_dev, 0).reshape(
        tiles_dev, 3, pixels
    )
    return (my_image, new_params, new_moment, new_second)


def solution(mesh):
    placed = (
        P(None, "dev"),
        P(None, "dev"),
        P(None, "dev"),
        P("dev", None, None),
        P("dev", None),
        P("dev"),
        P(),
        P("dev", None, None),
    )
    return jax.shard_map(
        per_device,
        mesh=mesh,
        in_specs=placed,
        out_specs=(P("dev", None, None), P(None, "dev"), P(None, "dev"), P(None, "dev")),
        check_vma=False,
    )
```

profile of v0, /device:TPU:0, one launch (start us, length us, event | category | flops | bytes accessed | tf_op | source)
XLA Modules:
  0.0 180.7 jit_solution(15948701933116835159)
XLA Ops:
  0.6 1.4 copy.70
  2.0 7.3 %all-to-all-start = ((s32[32,1,8]{2,1,0:T(1,128)}), s32[32,1,8]{2,1,0:T(1,128)S(1)}, u32[]{:S(2)}, u32[]{:S(2)}) async-start(s32[32,1,8]{2,1,0:T(1,128)} %bitcast), calls=%async_computation | async-start | bytes 32768 | tf_op jit(solution)/shard_map/all_to_all | solution.py:47
  9.3 0.7 copy-done.3
  10.0 0.6 copy-done.6
  10.9 0.6 copy-done.4
  11.6 42.1 %all_gather.11 = f32[32,3,256]{2,1,0:T(4,128)S(1)} all-gather(f32[1,3,256]{2,1,0:T(4,128)S(1)} %copy.77), channel_id=1, replica_groups=mesh['dev'=32] {'dev'}, dimensions={0}, use_global_device_ids=true | all-gather | bytes 101376 | tf_op jit(solution)/shard_map/all_gather | solution.py:64
  53.7 0.8 copy-done
  54.7 0.5 broadcast.479
  55.3 0.7 reduce.3
  56.1 0.7 gather_fusion
  56.9 0.7 fusion.51
  57.6 2.6 %all-to-all-start.1 = ((f32[9,32,8]{0,2,1:T(8,128)}), f32[9,32,8]{0,2,1:T(8,128)S(1)}, u32[]{:S(2)}, u32[]{:S(2)}) async-start(f32[9,32,8]{0,2,1:T(8,128)} %fusion.51), calls=%async_computation.1 | async-start | bytes 262144 | tf_op jit(solution)/shard_map/all_to_all | solution.py:49
  60.2 8.2 %all-to-all-done.1 = f32[9,32,8]{0,2,1:T(8,128)S(1)} async-done(((f32[9,32,8]{0,2,1:T(8,128)}), f32[9,32,8]{0,2,1:T(8,128)S(1)}, u32[]{:S(2)}, u32[]{:S(2)}) %all-to-all-start.1) | async-done | bytes 9248 | tf_op jit(solution)/shard_map/all_to_all | solution.py:49
  68.4 2.8 %gather_fusion.1 = f32[1024,9]{1,0:T(8,128)S(1)} fusion(f32[9,256]{0,1:T(8,128)S(1)} %bitcast.112, s32[1024]{0:T(1024)S(1)} %broadcast_clamp_fusion), kind=kCustom, calls=%fused_computation.1 | custom fusion | bytes 77824 | tf_op jit(solution)/shard_map/jit(_take)/gather | solution.py:55
  71.5 0.6 copy-done.5
  72.3 1.0 log-plus-one_reduce_fusion
  73.3 38.2 %all-gather = f32[32,4,256]{2,1,0:T(4,128)S(1)} all-gather(f32[1,4,256]{2,1,0:T(4,128)S(1)} %bitcast.126), channel_id=1, replica_groups=mesh['dev'=32] {'dev'}, dimensions={0}, use_global_device_ids=true | all-gather | bytes 135168 | tf_op jit(solution)/shard_map/all_gather | solution.py:63
  111.9 1.5 convolution_exponential_fusion
  113.4 1.5 fusion.43
  114.8 38.4 %all_gather.10 = f32[128,3,256]{2,1,0:T(4,128)S(1)} all-gather(f32[4,3,256]{2,1,0:T(4,128)S(1)} %fusion.43), channel_id=1, replica_groups=mesh['dev'=32] {'dev'}, dimensions={0}, use_global_device_ids=true | all-gather | bytes 405504 | tf_op jit(solution)/shard_map/all_gather | solution.py:62
  153.5 0.3 fusion.67
  154.0 1.2 fusion.42
  155.2 1.0 fusion.64
  156.3 0.3 fusion.7
  156.6 3.0 %fusion.26 = (f32[4,256]{1,0:T(4,128)S(1)}, f32[4,256]{1,0:T(4,128)S(1)}, f32[4,256]{1,0:T(4,128)S(1)}, f32[4,256]{1,0:T(4,128)S(1)}, f32[4,256]{1,0:T(4,128)S(1)}, /*index=5*/f32[4,256]{1,0:T(4,128)S(1)}) fusion(f32[4,256]{1,0:T(4,128)S(1)} %get-tuple-element.51, f32[4,256]{1,0:T(4,128)S(1)} %get-tuple-element.56, f32[4,256]{1,0:T(4,128)S(1)} %get-tuple-element.48, ...), kind=kOutput, calls=%fused_computation.50 | convolution fusion | flops 820570112 | bytes 2183168 | tf_op jit(solution)/shard_map/transpose(jvp(vmap()))/dot_general | solution.py:32
  160.1 6.6 %scatter_custom_fusion = f32[9,256]{0,1:T(8,128)} fusion(s32[1024]{0:T(1024)S(1)} %bitcast.127, f32[1024,9]{1,0:T(8,128)S(1)} %copy.82, f32[]{:T(128)} %constant.154.clone.1), kind=kCustom, calls=%fused_computation.90 | custom fusion | flops 9216 | bytes 9220 | tf_op jit(solution)/shard_map/scatter-add | solution.py:90
  166.8 2.6 %all-to-all-start.2 = ((f32[9,32,8]{0,2,1:T(8,128)}), f32[9,32,8]{0,2,1:T(8,128)S(1)}, u32[]{:S(2)}, u32[]{:S(2)}) async-start(f32[9,32,8]{0,2,1:T(8,128)} %bitcast.29), calls=%async_computation.2 | async-start | bytes 262144 | tf_op jit(solution)/shard_map/all_to_all | solution.py:92
  169.3 0.6 constant_dynamic-slice_fusion.1
  169.9 7.6 %all-to-all-done.2 = f32[9,32,8]{0,2,1:T(8,128)S(1)} async-done(((f32[9,32,8]{0,2,1:T(8,128)}), f32[9,32,8]{0,2,1:T(8,128)S(1)}, u32[]{:S(2)}, u32[]{:S(2)}) %all-to-all-start.2) | async-done | bytes 9248 | tf_op jit(solution)/shard_map/all_to_all | solution.py:92
  177.6 1.6 scatter_custom_fusion.1
  179.3 0.6 copy-done.1
  180.0 0.7 divide_subtract_fusion
  (59 shorter events, 2.6 us)
Async XLA Ops:
  2.0 52.7 %all-to-all-start = ((s32[32,1,8]{2,1,0:T(1,128)}), s32[32,1,8]{2,1,0:T(1,128)S(1)}, u32[]{:S(2)}, u32[]{:S(2)}) async-start(s32[32,1,8]{2,1,0:T(1,128)} %bitcast), calls=%async_computation | async-start | bytes 32768 | tf_op jit(solution)/shard_map/all_to_all | solution.py:47
  9.3 0.7 copy-start.3
  10.0 0.7 copy-start.6
  10.8 0.7 copy-start.4
  53.7 0.8 copy-start
  57.6 10.8 %all-to-all-start.1 = ((f32[9,32,8]{0,2,1:T(8,128)}), f32[9,32,8]{0,2,1:T(8,128)S(1)}, u32[]{:S(2)}, u32[]{:S(2)}) async-start(f32[9,32,8]{0,2,1:T(8,128)} %fusion.51), calls=%async_computation.1 | async-start | bytes 262144 | tf_op jit(solution)/shard_map/all_to_all | solution.py:49
  71.5 0.7 copy-start.5
  166.8 10.8 %all-to-all-start.2 = ((f32[9,32,8]{0,2,1:T(8,128)}), f32[9,32,8]{0,2,1:T(8,128)S(1)}, u32[]{:S(2)}, u32[]{:S(2)}) async-start(f32[9,32,8]{0,2,1:T(8,128)} %bitcast.29), calls=%async_computation.2 | async-start | bytes 262144 | tf_op jit(solution)/shard_map/all_to_all | solution.py:92
  179.1 0.8 copy-start.1
  179.1 0.9 copy-start.2
where the time goes:
time: 181 us
  blocking collectives  119 us (66%)
  waiting for transfers between devices  15.9 us (9%)
  starting transfers between devices  12.4 us (7%)
  other arithmetic  12 us (7%)
  local copies, waits for them, and re-layouts  11.5 us (6%)
  matrix products  9.3 us (5%)
    all_gather x1, blocking collectives, per_device(): lax.all_gather(target, 'dev', axis=0, tiled=True)  42.1 us
    all_gather x1, blocking collectives, per_device(): lax.all_gather(colours, 'dev', axis=0, tiled=True)  38.4 us
    all_gather x1, blocking collectives, per_device(): lax.all_gather(logs, 'dev', axis=0, tiled=True)  38.2 us
    all_to_all x1, waiting for transfers between devices, per_device(): lax.all_to_all(buckets, 'dev', split_axis=1, concat_axis=1, tiled=True)  8.22 us
    all_to_all x1, waiting for transfers between devices, per_device(): lax.all_to_all(slot_grad.reshape(nparam, ndev, cap), 'dev', split_axis=1,...  7.64 us
    all_to_all x1, starting transfers between devices, per_device(): lax.all_to_all(wanted, 'dev', split_axis=0, concat_axis=0, tiled=True)  7.3 us
    scatter-add x1, other arithmetic, per_device(): slot_grad = jnp.zeros((nparam, ndev * cap), jnp.float32).at[:, seg_ids.re...  6.62 us
    unnamed x24, local copies, waits for them, and re-layouts  5.71 us
  transfers between devices with their start and end apart: 3, of which 2 were waited for; matrix products, arithmetic and copies ran while one was open for 1% of the time, Pallas kernels for 0%

commit v1 on v0

v1 whole, which is shorter than its diff:
```python
import functools

import jax
import jax.numpy as jnp
from jax import lax
from jax.experimental import pallas as pl
from jax.experimental.pallas import tpu as pltpu
from jax.sharding import PartitionSpec as P

TILES_X = 8
KSEG = 4
SIDE = 16
LANES = 128
GROUP = 32
ROWS = 16
F32 = jnp.float32
BF16 = jnp.bfloat16
SMEM = pl.BlockSpec(memory_space=pltpu.SMEM)
VMEM = pl.BlockSpec(memory_space=pltpu.VMEM)
PARAMS = pltpu.CompilerParams(vmem_limit_bytes=40 * 2**20)


def split2(x):
    high = x.astype(BF16)
    return high, (x - high.astype(F32)).astype(BF16)


def split3(x):
    high = x.astype(BF16)
    rest = x - high.astype(F32)
    mid = rest.astype(BF16)
    return high, mid, (rest - mid.astype(F32)).astype(BF16)


def iota(shape, dim):
    return lax.broadcasted_iota(jnp.int32, shape, dim)


def dot(a, b, dims=((1,), (0,))):
    return lax.dot_general(a, b, (dims, ((), ())), preferred_element_type=F32)


def one_hot_rows(ids, cap, width):
    cols = iota((ids.shape[0], width), 1)
    return jnp.concatenate([(ids[:, k : k + 1] == cols).astype(F32).astype(BF16) for k in range(cap)], 0)


def request_kernel(cap, count, seg, fetch, out, moved, base):
    segs, span = seg.shape
    ndev, rows, _ = out.shape
    halves = span // LANES
    lane = iota((1, LANES), 1)
    for s in range(segs):
        for h in range(halves):
            live = lane + h * LANES < count[s]
            row = s * halves + h
            base[row : row + 1, :] = jnp.where(live, seg[s : s + 1, h * LANES : (h + 1) * LANES], -1)
    block = base[...]
    sub, lanes = iota((rows, LANES), 0), iota((rows, LANES), 1)
    slot = (sub == rows - 1) & (lanes < cap)
    for d in range(ndev):
        wide = jnp.broadcast_to(fetch[d : d + 1, :], (rows, LANES))
        out[d] = jnp.where(slot, wide, block)
    last = jnp.broadcast_to(block[rows - 1 : rows, :], (rows, LANES)).astype(F32)
    column = jnp.sum(jnp.where(sub == lanes, last, 0.0), axis=1, keepdims=True)
    moved[...] = jnp.where(lanes == LANES - 1, column, 0.0)


def send_kernel(segs, cap, perm, ids_in, params, moved, out, order, wide, picked):
    ndev, rows, _ = ids_in.shape
    nparam, owned = params.shape
    total = perm.shape[0]

    def place(j, carry):
        order[perm[j]] = j
        return carry

    lax.fori_loop(0, total, place, 0, unroll=8)
    hot = one_hot_rows(ids_in[:, rows - 1, :], cap, owned)
    wide[...] = jnp.zeros(wide.shape, F32)
    for q in range(KSEG):
        wide[q * GROUP : q * GROUP + nparam, :] = params[...]
    picked[...] = sum(dot(hot, part, ((1,), (1,))) for part in split3(wide[...]))
    group = iota((cap, LANES), 1) // GROUP
    extra = moved[...]

    def send(t, carry):
        block = extra
        for q in range(KSEG):
            r = order[t * KSEG + q] // segs
            block = block + jnp.where(group == q, picked[pl.ds(r, cap, stride=ndev), :], 0.0)
        out[t] = block
        return carry

    lax.fori_loop(0, ndev, send, 0, unroll=4)


def render_kernel(
    segs, cap, nparam, me, order, arrived, lists, target, image, grads,
    bufs, hots, coef, ids, alpha, trans, logs, weights, backs, lower, dys, dpar, gback,
):
    ndev, rows, _ = lists.shape
    slots = ndev * cap
    pixels = SIDE * SIDE
    span = hots.shape[2]
    halves = span // LANES
    tile = me[0]
    bufs[...] = arrived[...].reshape(slots, LANES).T
    src, dst = iota((span, span), 0), iota((span, span), 1)
    before = (src < dst).astype(F32).astype(BF16)
    after = (src > dst).astype(F32).astype(BF16)
    lower[0, :span, :] = before
    lower[0, span:, :] = before
    lower[1, :span, :] = after
    lower[1, span:, :] = after
    slot_row = iota((slots, span), 0)
    fine = (iota((SIDE, span), 0).astype(F32) + 0.5) / SIDE
    pos_x = (tile % TILES_X).astype(F32) + fine
    pos_y = (tile // TILES_X).astype(F32) + fine
    sub8, lane8 = iota((cap, LANES), 0), iota((cap, LANES), 1)

    par, dxs, rates = [], [], []
    for q in range(KSEG):
        j = order[tile * KSEG + q]
        r, s = j // segs, j % segs
        tail = jnp.broadcast_to(arrived[r][:, LANES - 1 : LANES], (cap, LANES))
        tail = jnp.sum(jnp.where(sub8 == lane8, tail, 0.0), axis=0, keepdims=True).astype(jnp.int32)
        for h in range(halves):
            row = lists[r, pl.ds(s * halves + h, 1), :]
            if h == halves - 1:
                fix = (iota((1, LANES), 1) < cap) & (s == segs - 1)
                row = jnp.where(fix, tail, row)
            ids[q : q + 1, h * LANES : (h + 1) * LANES] = row
        own = ids[q : q + 1, :]
        hot = (slot_row == own).astype(F32).astype(BF16)
        hots[q] = hot
        parts = jnp.concatenate(split3(bufs[q * GROUP : q * GROUP + ROWS, :]), 0)
        got = dot(parts, hot)
        got = got[:ROWS] + got[ROWS : 2 * ROWS] + got[2 * ROWS :]
        coef[q] = got
        mx, my = got[0:1], got[1:2]
        ex, ey = jnp.exp(got[2:3]), jnp.exp(got[3:4])
        th = jnp.tanh(got[4:5])
        sa, sc, cross = ex * ex, ey * ey, 0.8 * th * ex * ey
        live = (own >= 0).astype(F32)
        peak = 0.95 / (1.0 + jnp.exp(-got[5:6])) * live
        dx = pos_x - mx
        dy = pos_y - my
        xa = -0.5 * sa * dx * dx
        xb = -cross * dx
        dys[q, 0] = dy
        dys[q, 1] = -0.5 * sc * dy * dy
        par.append((sa, sc, cross, ex, ey, th))
        dxs.append(dx)
        for y in range(SIDE):
            power = xa + dys[q, 0, y : y + 1, :] * xb + dys[q, 1, y : y + 1, :]
            al = peak * jnp.exp(power)
            at = slice(y * SIDE, (y + 1) * SIDE)
            alpha[q, at, :] = al
            hi, mid = split2(jnp.log(1.0 - al))
            logs[q, at, :span] = hi
            logs[q, at, span:] = mid
        trans[q] = dot(logs[q], lower[0])

    ahead = jnp.zeros((pixels, 1), F32)
    shown = jnp.zeros((pixels, LANES), F32)
    lane = iota((pixels, LANES), 1)
    for q in range(KSEG):
        front = jnp.broadcast_to(ahead, (pixels, LANES))
        gback[...] = front
        ahead = ahead + trans[q, :, span - 1 : span] + jnp.log(1.0 - alpha[q, :, span - 1 : span])
        for y in range(SIDE):
            at = slice(y * SIDE, (y + 1) * SIDE)
            both = jnp.concatenate([gback[at, :]] * halves, 1)
            t = jnp.exp(trans[q, at, :] + both)
            trans[q, at, :] = t
            hi, mid = split2(t * alpha[q, at, :])
            weights[q, at, :] = hi
            weights[KSEG + q, at, :] = mid
        colour = jnp.concatenate([coef[q, 6:9, :]] * 3 + [jnp.zeros((LANES - 9, span), F32)], 0).T
        c_hi, c_mid = split2(colour)
        shown = shown + dot(weights[q], c_hi) + dot(weights[q], c_mid) + dot(weights[KSEG + q], c_hi)
    shot = shown.T
    image[0] = shot[0:3, :]
    goal = jnp.concatenate([target[0]] * 3 + [jnp.zeros((LANES - 9, pixels), F32)], 0)
    err_rows = (shot - goal)[:ROWS]
    err = shown - goal.T
    e_hi, e_mid = split2(err)
    e_cols = jnp.where(lane < 6, e_hi.astype(F32), e_mid.astype(F32)).astype(BF16)
    er_hi, er_mid = split2(err_rows)
    behind = jnp.zeros((pixels, 1), F32)
    for q in range(KSEG):
        col = coef[q, 6:9, :]
        hi, mid = split2(col)
        hi, mid = hi.astype(F32), mid.astype(F32)
        c_rows = jnp.concatenate([hi, mid, hi, jnp.zeros((LANES - 9, span), F32)], 0).astype(BF16)
        gback2 = dot(e_cols, c_rows)
        w_hi, w_mid = weights[q], weights[KSEG + q]
        dcol = dot(er_hi, w_hi) + dot(er_hi, w_mid) + dot(er_mid, w_hi)
        dpar[q, 6:9, :] = dcol[0:3]
        for y in range(SIDE):
            at = slice(y * SIDE, (y + 1) * SIDE)
            gt = gback2[at] * trans[q, at, :]
            trans[q, at, :] = gt
            hi, mid = split2(gt * alpha[q, at, :])
            logs[q, at, :span] = hi
            logs[q, at, span:] = mid
        backs[q] = dot(logs[q], lower[1])
    for q in reversed(range(KSEG)):
        gback[...] = jnp.broadcast_to(behind, (pixels, LANES))
        behind = behind + backs[q, :, 0:1] + trans[q, :, 0:1] * alpha[q, :, 0:1]
        sa, sc, cross, ex, ey, th = par[q]
        dx = dxs[q]
        d0 = jnp.zeros((SIDE, span), F32)
        d1 = jnp.zeros((SIDE, span), F32)
        d2 = jnp.zeros((SIDE, span), F32)
        for y in range(SIDE):
            at = slice(y * SIDE, (y + 1) * SIDE)
            both = jnp.concatenate([gback[at, :]] * halves, 1)
            al = alpha[q, at, :]
            d = (trans[q, at, :] - (backs[q, at, :] + both) / (1.0 - al)) * al
            ddy = d * dys[q, 0, y : y + 1, :]
            d0 = d0 + d
            d1 = d1 + ddy
            d2 = d2 + ddy * dys[q, 0, y : y + 1, :]
        m0 = jnp.sum(d0, 0, keepdims=True)
        m_x = jnp.sum(d0 * dx, 0, keepdims=True)
        m_y = jnp.sum(d1, 0, keepdims=True)
        m_xx = jnp.sum(d0 * dx * dx, 0, keepdims=True)
        m_xy = jnp.sum(d1 * dx, 0, keepdims=True)
        m_yy = jnp.sum(d2, 0, keepdims=True)
        dpar[q, 0:1, :] = sa * m_x + cross * m_y
        dpar[q, 1:2, :] = cross * m_x + sc * m_y
        dpar[q, 2:3, :] = -(sa * m_xx + cross * m_xy)
        dpar[q, 3:4, :] = -(sc * m_yy + cross * m_xy)
        dpar[q, 4:5, :] = -0.8 * (1.0 - th) * (1.0 + th) * ex * ey * m_xy
        dpar[q, 5:6, :] = m0 / (1.0 + jnp.exp(coef[q, 5:6, :]))
        dpar[q, nparam:, :] = jnp.zeros((ROWS - nparam, span), F32)
        parts = jnp.concatenate(split3(dpar[q]), 0)
        back = dot(parts, hots[q], ((1,), (1,)))
        back = back[:ROWS] + back[ROWS : 2 * ROWS] + back[2 * ROWS :]
        bufs[q * GROUP : q * GROUP + ROWS, :] = back
        bufs[q * GROUP + ROWS : (q + 1) * GROUP, :] = jnp.zeros((GROUP - ROWS, slots), F32)
    grads[...] = bufs[...].T.reshape(ndev, cap, LANES)


def update_kernel(
    segs, cap, perm, returned, ids_in, params, moment, second, new_params, new_moment, new_second, gathered
):
    ndev, rows, _ = ids_in.shape
    nparam, owned = params.shape
    group = iota((cap, LANES), 1) // GROUP

    def collect(r, carry):
        block = jnp.zeros((cap, LANES), F32)
        for s in range(segs):
            v = perm[r * segs + s]
            block = block + jnp.where(group == v % KSEG, returned[v // KSEG], 0.0)
        gathered[pl.ds(r, cap, stride=ndev), :] = block
        return carry

    lax.fori_loop(0, ndev, collect, 0, unroll=4)
    hot = one_hot_rows(ids_in[:, rows - 1, :], cap, owned)
    flat = gathered[...].T
    values = sum(flat[q * GROUP : q * GROUP + ROWS] for q in range(KSEG))
    parts = jnp.concatenate(split3(values), 0)
    grad = dot(parts, hot)
    grad = (grad[:ROWS] + grad[ROWS : 2 * ROWS] + grad[2 * ROWS :])[:nparam]
    m = 0.9 * moment[...] + 0.1 * grad
    v = 0.99 * second[...] + 0.01 * grad * grad
    new_moment[...] = m
    new_second[...] = v
    new_params[...] = params[...] - 0.05 * m / (jnp.sqrt(v) + 1e-08)


def per_device(params, moment, second, fetch_ids, seg_ids, seg_count, seg_perm, target):
    ndev = lax.axis_size("dev")
    nparam, owned = params.shape
    segs, span = seg_ids.shape
    cap = fetch_ids.shape[2]
    pixels = target.shape[2]
    slots = ndev * cap
    rows = segs * span // LANES
    assert target.shape[0] == 1 and segs == KSEG and rows == cap and pixels == SIDE * SIDE
    fetch = jnp.pad(fetch_ids[0], ((0, 0), (0, LANES - cap)))
    block = jax.ShapeDtypeStruct((ndev, rows, LANES), F32)
    swap = functools.partial(lax.all_to_all, axis_name="dev", split_axis=0, concat_axis=0, tiled=True)

    requests, moved = pl.pallas_call(
        functools.partial(request_kernel, cap),
        out_shape=(jax.ShapeDtypeStruct((ndev, rows, LANES), jnp.int32), jax.ShapeDtypeStruct((rows, LANES), F32)),
        in_specs=[SMEM, VMEM, VMEM],
        out_specs=(VMEM, VMEM),
        scratch_shapes=[pltpu.VMEM((rows, LANES), jnp.int32)],
        compiler_params=PARAMS,
        name="requests",
    )(seg_count, seg_ids, fetch)
    lists = swap(requests)
    outgoing, order = pl.pallas_call(
        functools.partial(send_kernel, segs, cap),
        out_shape=(block, jax.ShapeDtypeStruct(seg_perm.shape, jnp.int32)),
        in_specs=[SMEM, VMEM, VMEM, VMEM],
        out_specs=(VMEM, SMEM),
        scratch_shapes=[pltpu.VMEM((LANES, owned), F32), pltpu.VMEM((slots, LANES), F32)],
        compiler_params=PARAMS,
        name="send",
    )(seg_perm, lists, params, moved)
    arrived = swap(outgoing)
    me = lax.axis_index("dev").astype(jnp.int32).reshape(1)
    image, grads = pl.pallas_call(
        functools.partial(render_kernel, segs, cap, nparam),
        out_shape=(jax.ShapeDtypeStruct(target.shape, F32), block),
        in_specs=[SMEM, SMEM, VMEM, VMEM, VMEM],
        out_specs=(VMEM, VMEM),
        scratch_shapes=[
            pltpu.VMEM((LANES, slots), F32),
            pltpu.VMEM((KSEG, slots, span), BF16),
            pltpu.VMEM((KSEG, ROWS, span), F32),
            pltpu.VMEM((KSEG, span), jnp.int32),
            pltpu.VMEM((KSEG, pixels, span), F32),
            pltpu.VMEM((KSEG, pixels, span), F32),
            pltpu.VMEM((KSEG, pixels, 2 * span), BF16),
            pltpu.VMEM((2 * KSEG, pixels, span), BF16),
            pltpu.VMEM((KSEG, pixels, span), F32),
            pltpu.VMEM((2, 2 * span, span), BF16),
            pltpu.VMEM((KSEG, 2, SIDE, span), F32),
            pltpu.VMEM((KSEG, ROWS, span), F32),
            pltpu.VMEM((pixels, LANES), F32),
        ],
        compiler_params=PARAMS,
        name="render",
    )(me, order, arrived, lists, target)
    returned = swap(grads)
    new = jax.ShapeDtypeStruct(params.shape, F32)
    new_params, new_moment, new_second = pl.pallas_call(
        functools.partial(update_kernel, segs, cap),
        out_shape=(new, new, new),
        in_specs=[SMEM] + [VMEM] * 5,
        out_specs=(VMEM, VMEM, VMEM),
        scratch_shapes=[pltpu.VMEM((slots, LANES), F32)],
        compiler_params=PARAMS,
        name="update",
    )(seg_perm, returned, lists, params, moment, second)
    return (image, new_params, new_moment, new_second)


def solution(mesh):
    placed = (
        P(None, "dev"),
        P(None, "dev"),
        P(None, "dev"),
        P("dev", None, None),
        P("dev", None),
        P("dev"),
        P(),
        P("dev", None, None),
    )
    return jax.shard_map(
        per_device,
        mesh=mesh,
        in_specs=placed,
        out_specs=(P("dev", None, None), P(None, "dev"), P(None, "dev"), P(None, "dev")),
        check_vma=False,
    )
```

time: 181 us -> 50.8 us (0.28)
  blocking collectives: 119 us -> 15.3 us
  other arithmetic: 12 us -> 0 us
  Pallas kernels: 0 us -> 10.5 us
  matrix products: 9.3 us -> 0 us
  local copies, waits for them, and re-layouts: 11.5 us -> 3.37 us
  starting transfers between devices: 12.4 us -> 5.28 us
    all_gather x3 -> x0, blocking collectives: 119 us -> none  [the longest x1 42.1 us: per_device(): lax.all_gather(target, 'dev', axis=0, tiled=True)]
    all_to_all x0 -> x1, blocking collectives: none -> 15.3 us  [per_device(): lists = swap(requests)]
    pallas_call x0 -> x4, Pallas kernels: none -> 10.5 us  [the longest x1 4.29 us: per_device(): pl.pallas_call(functools.partial(render_kernel, segs, cap, nparam), out_s...]
    dot_general x9 -> x0, matrix products: 9.3 us -> none  [the longest x2 4.49 us: segment(): earlier = jnp.dot(lower, logt, precision=lax.Precision.HIGHEST)]
    scatter-add x2 -> x0, other arithmetic: 8.17 us -> none  [the longest x1 6.62 us: per_device(): slot_grad = jnp.zeros((nparam, ndev * cap), jnp.float32).at[:, seg_ids.re...]
    all_to_all x3 -> x2, starting transfers between devices: 12.4 us -> 5.28 us  [the longest x1 2.7 us: per_device(): returned = swap(grads)]
    gather x3 -> x0, local copies, waits for them, and re-layouts: 3.72 us -> none  [the longest x2 2.99 us: per_device(): gathered_par = jnp.moveaxis(jnp.take(buffer, seg_ids, axis=1), 1, 0)]
    unnamed x24 -> x17, local copies, waits for them, and re-layouts: 5.71 us -> 3.37 us
  transfers between devices with their start and end apart: 3 -> 2, of which waited for: 2 -> 2; matrix products, arithmetic and copies ran while one was open for 1% -> 1% of each run, Pallas kernels for 0% -> 0%
where the time goes in v1:
time: 50.8 us; the launch traced here: 50.4 us
  blocking collectives  15.3 us (30%)
  waiting for transfers between devices  15.2 us (30%)
  Pallas kernels  10.5 us (21%)
  starting transfers between devices  5.28 us (10%)
  local copies, waits for them, and re-layouts  3.37 us (7%)
  between operations  0.68 us (1%)
    all_to_all x1, blocking collectives, per_device(): lists = swap(requests)  15.3 us
    all_to_all x1, waiting for transfers between devices, per_device(): returned = swap(grads)  7.65 us
    all_to_all x1, waiting for transfers between devices, per_device(): arrived = swap(outgoing)  7.54 us
    pallas_call x1, Pallas kernels, per_device(): pl.pallas_call(functools.partial(render_kernel, segs, cap, nparam), out_s...  4.29 us
    unnamed x17, local copies, waits for them, and re-layouts  3.37 us
    pallas_call x1, Pallas kernels, per_device(): pl.pallas_call(functools.partial(send_kernel, segs, cap), out_shape=(bloc...  2.98 us
    all_to_all x1, starting transfers between devices, per_device(): returned = swap(grads)  2.7 us
    pallas_call x1, Pallas kernels, per_device(): pl.pallas_call(functools.partial(update_kernel, segs, cap), out_shape=(ne...  2.65 us
  transfers between devices with their start and end apart: 2, of which 2 were waited for; matrix products, arithmetic and copies ran while one was open for 1% of the time, Pallas kernels for 0%

profile of v1, /device:TPU:0, one launch (start us, length us, event | category | flops | bytes accessed | tf_op | source)
XLA Modules:
  0.0 50.4 jit_solution(8177339225433257643)
XLA Ops:
  0.6 0.8 %copy.12 = s32[1,32,8]{2,1,0:T(8,128)S(1)} copy(s32[1,32,8]{1,2,0:T(8,128)} %param.11) | data formatting | bytes 2048 | tf_op args[3]
  1.4 0.0 copy-start.3
  1.4 0.0 copy-start.5
  1.4 0.7 %copy-done.3 = s32[4,256]{1,0:T(4,128)S(1)} copy-done((s32[4,256]{1,0:T(4,128)S(1)}, s32[4,256]{1,0:T(4,128)}, u32[]{:S(2)}) %copy-start.3) | copy-done | bytes 4120
  2.1 0.0 copy-done.5
  2.1 0.6 %requests.1 = (s32[32,8,128]{2,1,0:T(8,128)S(1)}, f32[8,128]{1,0:T(8,128)S(1)}) custom-call(s32[4]{0:T(128)S(1)} %copy-done.5, s32[4,256]{1,0:T(4,128)S(1)} %copy-done.3, s32[32,128]{1,0:T(8,128)S(1)} %pad.4.fetch), custom_call_target="tpu_custom_call" | custom-call | tf_op jit(solution)/shard_map/requests/pallas_call | solution.py:289
  2.7 0.0 copy-start
  2.7 15.3 %all_to_all.15.ids_in.lists = s32[32,8,128]{2,1,0:T(8,128)S(1)} all-to-all(s32[32,8,128]{2,1,0:T(8,128)S(1)} %get-tuple-element.13), channel_id=1, replica_groups=mesh['dev'=32] {'dev'}, dimensions={0} | all-to-all | bytes 262144 | tf_op jit(solution)/shard_map/all_to_all | solution.py:298
  18.0 0.0 copy-start.4
  18.0 0.0 copy-done
  18.0 0.7 %copy-done.4 = s32[128]{0:T(128)S(1)} copy-done((s32[128]{0:T(128)S(1)}, s32[128]{0:T(128)}, u32[]{:S(2)}) %copy-start.4) | copy-done | bytes 536
  18.7 3.0 %send.1 = (f32[32,8,128]{2,1,0:T(8,128)}, s32[128]{0:T(128)S(1)}) custom-call(s32[128]{0:T(128)S(1)} %copy-done.4, s32[32,8,128]{2,1,0:T(8,128)S(1)} %all_to_all.15.ids_in.lists, f32[9,1024]{1,0:T(8,128)S(1)} %copy-done, f32[8,128]{1,0:T(8,128)S(1)} %get-tuple-element.14.moved), custom_call_target="tpu_custom_call" | custom-call | tf_op jit(solution)/shard_map/send/pallas_call | solution.py:299
  21.7 2.6 %all-to-all-start.1 = ((f32[32,8,128]{2,1,0:T(8,128)}), f32[32,8,128]{2,1,0:T(8,128)S(1)}, u32[]{:S(2)}, u32[]{:S(2)}) async-start(f32[32,8,128]{2,1,0:T(8,128)} %get-tuple-element.16), calls=%async_computation.1 | async-start | bytes 262144 | tf_op jit(solution)/shard_map/all_to_all | solution.py:308
  24.3 0.0 copy-start.6
  24.3 0.7 %copy-done.6 = f32[1,3,256]{2,0,1:T(1,128)S(1)} copy-done((f32[1,3,256]{2,0,1:T(1,128)S(1)}, f32[1,3,256]{2,0,1:T(1,128)}, u32[]{:S(2)}) %copy-start.6) | copy-done | bytes 3096
  25.0 7.5 %all-to-all-done.1.arrived = f32[32,8,128]{2,1,0:T(8,128)S(1)} async-done(((f32[32,8,128]{2,1,0:T(8,128)}), f32[32,8,128]{2,1,0:T(8,128)S(1)}, u32[]{:S(2)}, u32[]{:S(2)}) %all-to-all-start.1) | async-done | bytes 131104 | tf_op jit(solution)/shard_map/all_to_all | solution.py:308
  32.5 4.3 %render.1 = (f32[1,3,256]{2,1,0:T(4,128)S(1)}, f32[32,8,128]{2,1,0:T(8,128)}) custom-call(s32[1]{0:T(128)} %bitcast.me, s32[128]{0:T(128)S(1)} %get-tuple-element.15.order, f32[32,8,128]{2,1,0:T(8,128)S(1)} %all-to-all-done.1.arrived, s32[32,8,128]{2,1,0:T(8,128)S(1)} %all_to_all.15.ids_in.lists, f32[1,3,256]{2,1,0:T(4,128)S(1)} %copy.13.target), custom_call_target="tpu_custom_call" | custom-call | tf_op jit(solution)/shard_map/render/pallas_call | solution.py:310
  36.8 0.0 copy-start.1
  36.8 0.0 copy-start.2
  36.8 2.7 %all-to-all-start.2 = ((f32[32,8,128]{2,1,0:T(8,128)}), f32[32,8,128]{2,1,0:T(8,128)S(1)}, u32[]{:S(2)}, u32[]{:S(2)}) async-start(f32[32,8,128]{2,1,0:T(8,128)} %get-tuple-element.18), calls=%async_computation.2 | async-start | bytes 262144 | tf_op jit(solution)/shard_map/all_to_all | solution.py:333
  39.5 0.6 %copy.14 = f32[1,3,256]{2,0,1:T(1,128)} copy(f32[1,3,256]{2,1,0:T(4,128)S(1)} %get-tuple-element.22) | data formatting | bytes 6144
  40.1 7.6 %all-to-all-done.2.returned = f32[32,8,128]{2,1,0:T(8,128)S(1)} async-done(((f32[32,8,128]{2,1,0:T(8,128)}), f32[32,8,128]{2,1,0:T(8,128)S(1)}, u32[]{:S(2)}, u32[]{:S(2)}) %all-to-all-start.2) | async-done | bytes 131104 | tf_op jit(solution)/shard_map/all_to_all | solution.py:333
  47.7 0.0 copy-done.1
  47.7 0.0 copy-done.2
  47.7 2.7 %update.1 = (f32[9,1024]{1,0:T(8,128)}, f32[9,1024]{1,0:T(8,128)}, f32[9,1024]{1,0:T(8,128)}) custom-call(s32[128]{0:T(128)S(1)} %copy-done.4, f32[32,8,128]{2,1,0:T(8,128)S(1)} %all-to-all-done.2.returned, s32[32,8,128]{2,1,0:T(8,128)S(1)} %all_to_all.15.ids_in.lists, f32[9,1024]{1,0:T(8,128)S(1)} %copy-done, f32[9,1024]{1,0:T(8,128)S(1)} %copy-done.1, ...), custom_call_target="tpu_custom_call" | custom-call | tf_op jit(solution)/shard_map/update/pallas_call | solution.py:335
  (2 shorter events, 0.0 us)
Async XLA Ops:
  1.4 0.7 %copy-start.3 = (s32[4,256]{1,0:T(4,128)S(1)}, s32[4,256]{1,0:T(4,128)}, u32[]{:S(2)}) copy-start(s32[4,256]{1,0:T(4,128)} %seg.1) | copy-start | bytes 12292
  1.4 0.7 %copy-start.5 = (s32[4]{0:T(128)S(1)}, s32[4]{0:T(128)}, u32[]{:S(2)}) copy-start(s32[4]{0:T(128)} %count.1) | copy-start | bytes 52
  2.7 15.3 %copy-start = (f32[9,1024]{1,0:T(8,128)S(1)}, f32[9,1024]{1,0:T(8,128)}, u32[]{:S(2)}) copy-start(f32[9,1024]{1,0:T(8,128)} %params.3) | copy-start | bytes 110596
  18.0 0.7 %copy-start.4 = (s32[128]{0:T(128)S(1)}, s32[128]{0:T(128)}, u32[]{:S(2)}) copy-start(s32[128]{0:T(128)} %perm.3) | copy-start | bytes 1540
  21.7 10.8 %all-to-all-start.1 = ((f32[32,8,128]{2,1,0:T(8,128)}), f32[32,8,128]{2,1,0:T(8,128)S(1)}, u32[]{:S(2)}, u32[]{:S(2)}) async-start(f32[32,8,128]{2,1,0:T(8,128)} %get-tuple-element.16), calls=%async_computation.1 | async-start | bytes 262144 | tf_op jit(solution)/shard_map/all_to_all | solution.py:308
  24.3 0.7 %copy-start.6 = (f32[1,3,256]{2,0,1:T(1,128)S(1)}, f32[1,3,256]{2,0,1:T(1,128)}, u32[]{:S(2)}) copy-start(f32[1,3,256]{2,0,1:T(1,128)} %param.15) | copy-start | bytes 9220
  36.8 10.9 %copy-start.1 = (f32[9,1024]{1,0:T(8,128)S(1)}, f32[9,1024]{1,0:T(8,128)}, u32[]{:S(2)}) copy-start(f32[9,1024]{1,0:T(8,128)} %moment.1) | copy-start | bytes 110596
  36.8 10.9 %copy-start.2 = (f32[9,1024]{1,0:T(8,128)S(1)}, f32[9,1024]{1,0:T(8,128)}, u32[]{:S(2)}) copy-start(f32[9,1024]{1,0:T(8,128)} %second.1) | copy-start | bytes 110596
  36.8 10.9 %all-to-all-start.2 = ((f32[32,8,128]{2,1,0:T(8,128)}), f32[32,8,128]{2,1,0:T(8,128)S(1)}, u32[]{:S(2)}, u32[]{:S(2)}) async-start(f32[32,8,128]{2,1,0:T(8,128)} %get-tuple-element.18), calls=%async_computation.2 | async-start | bytes 262144 | tf_op jit(solution)/shard_map/all_to_all | solution.py:333

commit v2 on v1

v2 whole, which is shorter than its diff:
```python
import functools

import jax
import jax.numpy as jnp
from jax import lax
from jax.experimental import pallas as pl
from jax.experimental.pallas import tpu as pltpu
from jax.sharding import PartitionSpec as P

TILES_X = 8
KSEG = 4
SIDE = 16
LANES = 128
SUB = 8
ROWS = 16
F32 = jnp.float32
BF16 = jnp.bfloat16
SMEM = pl.BlockSpec(memory_space=pltpu.SMEM)
VMEM = pl.BlockSpec(memory_space=pltpu.VMEM)
HBM = pl.BlockSpec(memory_space=pltpu.HBM)
PARAMS = pltpu.CompilerParams(vmem_limit_bytes=40 * 2**20)


def split2(x):
    high = x.astype(BF16)
    return high, (x - high.astype(F32)).astype(BF16)


def split3(x):
    high = x.astype(BF16)
    rest = x - high.astype(F32)
    mid = rest.astype(BF16)
    return high, mid, (rest - mid.astype(F32)).astype(BF16)


def iota(shape, dim):
    return lax.broadcasted_iota(jnp.int32, shape, dim)


def dot(a, b, dims=((1,), (0,))):
    return lax.dot_general(a, b, (dims, ((), ())), preferred_element_type=F32)


def stages(ndev):
    top, place, out = ndev.bit_length() - 1, 0, []
    assert ndev == 1 << top and top >= 3
    while top > 1:
        bits = min(2, top - 1)
        top -= bits
        out.append((top, bits, place))
        place += bits
    return out + [(0, 1, place)]


def position(ndev, offset):
    return sum(((offset >> bit) & ((1 << bits) - 1)) << place for bit, bits, place in stages(ndev))


def offset_at(ndev, pos):
    return sum(((pos >> place) & ((1 << bits) - 1)) << bit for bit, bits, place in stages(ndev))


def gather_blocks(block, ndev, beside):
    def pull(x, change):
        return lax.ppermute(x, "dev", [(d, d ^ change) for d in range(ndev)])

    held, steps = [block[None]], stages(ndev)
    for number, (bit, bits, _) in enumerate(steps[:-1]):
        whole = held[0] if len(held) == 1 else jnp.concatenate(held, 0)
        if number == 1:
            whole, beside = lax.optimization_barrier((whole, beside))
        held = [whole] + [pull(whole, change << bit) for change in range(1, 1 << bits)]
    return held + [pull(x, 1) for x in held], beside


def pick(source, lanes):
    return jnp.take_along_axis(source, lanes, axis=1)


def pack_kernel(count_in, seg_in, fetch_in, params_in, out, count, seg, fetch, params, sems):
    segs, span = seg.shape
    nparam, owned = params.shape
    chunks, halves = owned // LANES, span // LANES
    lane = iota((1, LANES), 1)
    pairs = ((params_in, params), (seg_in, seg), (fetch_in, fetch), (count_in, count))
    copies = [pltpu.make_async_copy(a, b, sems.at[i]) for i, (a, b) in enumerate(pairs)]
    for copy in copies:
        copy.start()
    for copy in copies:
        copy.wait()
    for p in range(nparam):
        for c in range(chunks):
            out[p * chunks + c : p * chunks + c + 1, :] = params[p : p + 1, c * LANES : (c + 1) * LANES]
    at = nparam * chunks
    for s in range(segs):
        for h in range(halves):
            row = jnp.where(lane + h * LANES < count[s], seg[s : s + 1, h * LANES : (h + 1) * LANES], -1)
            out[at : at + 1, :] = row.astype(F32)
            at += 1
    out[at : at + SUB, :] = jnp.zeros((SUB, LANES), F32)
    out[at : at + SUB, : fetch.shape[1]] = fetch[...].astype(F32)


def layout_kernel(perm, target, order, tri, goal, goal_cols):
    def place(j, carry):
        order[perm[j]] = j
        return carry

    lax.fori_loop(0, perm.shape[0], place, 0, unroll=8)
    span = tri.shape[2]
    src, dst = iota((span, span), 0), iota((span, span), 1)
    before = (src < dst).astype(F32).astype(BF16)
    after = (src > dst).astype(F32).astype(BF16)
    for half in range(2):
        tri[0, half * span : (half + 1) * span, :] = before
        tri[1, half * span : (half + 1) * span, :] = after
    rows = target[0]
    pixels = rows.shape[1]
    wide = jnp.concatenate([rows] * 3 + [jnp.zeros((LANES - 9, pixels), F32)], 0)
    goal[...] = wide[:ROWS]
    goal_cols[...] = wide.T


def render_kernel(segs, cap, nparam, chunks, ndev, *refs):
    me_ref, order, tri, goal, goal_cols = refs[:5]
    narr = 2 << stages(ndev)[-2][1]
    arrays = refs[5 : 5 + narr]
    image, grads = refs[5 + narr : 7 + narr]
    (idrows, table, hots, coef, alpha, trans, logs, weights, backs, dys, dpar, gback, flat) = refs[7 + narr :]
    per = arrays[0].shape[0]
    slots = ndev * cap
    quarter = slots // 2
    pixels = SIDE * SIDE
    span = hots.shape[2]
    halves = span // LANES
    me = me_ref[0]
    base = nparam * chunks

    def block(j):
        return arrays[j // per], j % per

    for j in range(ndev):
        ref, at = block(j)
        idrows[j] = ref[at, base : base + 2 * SUB, :]
    fetched, listed = [], []
    for q in range(KSEG):
        slot = order[me * KSEG + q]
        j = position(ndev, (slot // segs) ^ me)
        fetched.append(idrows[j, SUB : 2 * SUB, :])
        s = slot % segs
        listed.append([idrows[j, pl.ds(s * halves + h, 1), :].astype(jnp.int32) for h in range(halves)])
    sub, lane = iota((SUB, LANES), 0), iota((SUB, LANES), 1)
    rank, which = (lane // cap) % KSEG, lane // (cap * KSEG)
    for g in range(ndev // 4):
        offs = [offset_at(ndev, 4 * g + b) for b in range(4)]
        off = jnp.where(which == 0, offs[0], jnp.where(which == 1, offs[1], jnp.where(which == 2, offs[2], offs[3])))
        owner = off ^ me
        found = jnp.zeros((SUB, LANES), F32)
        for q in range(KSEG):
            found = jnp.where(rank == q, pick(fetched[q], owner), found)
        local = jnp.sum(jnp.where(sub == lane % cap, found, 0.0), 0, keepdims=True).astype(jnp.int32)
        local = jnp.broadcast_to(local, (SUB, LANES))
        inside, chunk = local % LANES, local // LANES
        for p in range(nparam):
            got = jnp.zeros((SUB, LANES), F32)
            for b in range(4):
                ref, at = block(4 * g + b)
                got = jnp.where(which == b, pick(ref[at, p * chunks : (p + 1) * chunks, :], inside), got)
            table[g, p : p + 1, :] = jnp.sum(jnp.where(sub == chunk, got, 0.0), 0, keepdims=True)
    slot_row = iota((slots, span), 0)
    fine = (iota((SIDE, span), 0).astype(F32) + 0.5) / SIDE
    pos_x = (me % TILES_X).astype(F32) + fine
    pos_y = (me // TILES_X).astype(F32) + fine

    par, dxs = [], []
    for q in range(KSEG):
        for h in range(halves):
            row = listed[q][h]
            live = row >= 0
            row = jnp.maximum(row, 0)
            pos = position(ndev, (row // cap) ^ me)
            spot = jnp.broadcast_to((pos % 4) * (cap * KSEG) + q * cap + row % cap, (SUB, LANES))
            team = pos // 4
            low = jnp.zeros((SUB, LANES), F32)
            high = jnp.zeros((SUB, LANES), F32)
            for g in range(ndev // 4):
                low = jnp.where(team == g, pick(table[g, :SUB, :], spot), low)
                high = jnp.where(team == g, pick(table[g, SUB:, :], spot), high)
            cols = slice(h * LANES, (h + 1) * LANES)
            coef[q, :SUB, cols] = jnp.where(live, low, 0.0)
            coef[q, SUB:, cols] = jnp.where(live, high, 0.0)
        own = jnp.concatenate(listed[q], 1)
        live = (own >= 0).astype(F32)
        k = own % cap
        own = jnp.where(own >= 0, (k // 4) * quarter + (own // cap) * 4 + k % 4, -1)
        hots[q] = (slot_row == own).astype(F32).astype(BF16)
        got = coef[q]
        mx, my = got[0:1], got[1:2]
        ex, ey = jnp.exp(got[2:3]), jnp.exp(got[3:4])
        th = jnp.tanh(got[4:5])
        sa, sc, cross = ex * ex, ey * ey, 0.8 * th * ex * ey
        peak = 0.95 / (1.0 + jnp.exp(-got[5:6])) * live
        dx = pos_x - mx
        dy = pos_y - my
        xa = -0.5 * sa * dx * dx
        xb = -cross * dx
        dys[q, 0] = dy
        dys[q, 1] = -0.5 * sc * dy * dy
        par.append((sa, sc, cross, ex, ey, th))
        dxs.append(dx)
        for y in range(SIDE):
            power = xa + dys[q, 0, y : y + 1, :] * xb + dys[q, 1, y : y + 1, :]
            al = peak * jnp.exp(power)
            at = slice(y * SIDE, (y + 1) * SIDE)
            alpha[q, at, :] = al
            hi, mid = split2(jnp.log(1.0 - al))
            logs[q, at, :span] = hi
            logs[q, at, span:] = mid
        trans[q] = dot(logs[q], tri[0])

    ahead = jnp.zeros((pixels, 1), F32)
    shown = jnp.zeros((pixels, LANES), F32)
    lane = iota((pixels, LANES), 1)
    for q in range(KSEG):
        gback[...] = jnp.broadcast_to(ahead, (pixels, LANES))
        ahead = ahead + trans[q, :, span - 1 : span] + jnp.log(1.0 - alpha[q, :, span - 1 : span])
        for y in range(SIDE):
            at = slice(y * SIDE, (y + 1) * SIDE)
            both = jnp.concatenate([gback[at, :]] * halves, 1)
            t = jnp.exp(trans[q, at, :] + both)
            trans[q, at, :] = t
            hi, mid = split2(t * alpha[q, at, :])
            weights[q, at, :] = hi
            weights[KSEG + q, at, :] = mid
        colour = jnp.concatenate([coef[q, 6:9, :]] * 3 + [jnp.zeros((LANES - 9, span), F32)], 0).T
        c_hi, c_mid = split2(colour)
        shown = shown + dot(weights[q], c_hi) + dot(weights[q], c_mid) + dot(weights[KSEG + q], c_hi)
    shot = shown.T
    image[0] = shot[0:3, :]
    err = shown - goal_cols[...]
    e_hi, e_mid = split2(err)
    e_cols = jnp.where(lane < 6, e_hi.astype(F32), e_mid.astype(F32)).astype(BF16)
    er_hi, er_mid = split2(shot[:ROWS] - goal[...])
    behind = jnp.zeros((pixels, 1), F32)
    for q in range(KSEG):
        hi, mid = split2(coef[q, 6:9, :])
        hi, mid = hi.astype(F32), mid.astype(F32)
        c_rows = jnp.concatenate([hi, mid, hi, jnp.zeros((LANES - 9, span), F32)], 0).astype(BF16)
        slope = dot(e_cols, c_rows)
        w_hi, w_mid = weights[q], weights[KSEG + q]
        dcol = dot(er_hi, w_hi) + dot(er_hi, w_mid) + dot(er_mid, w_hi)
        dpar[q, 6:9, :] = dcol[0:3]
        for y in range(SIDE):
            at = slice(y * SIDE, (y + 1) * SIDE)
            gt = slope[at] * trans[q, at, :]
            trans[q, at, :] = gt
            hi, mid = split2(gt * alpha[q, at, :])
            logs[q, at, :span] = hi
            logs[q, at, span:] = mid
        backs[q] = dot(logs[q], tri[1])
    for q in reversed(range(KSEG)):
        gback[...] = jnp.broadcast_to(behind, (pixels, LANES))
        behind = behind + backs[q, :, 0:1] + trans[q, :, 0:1] * alpha[q, :, 0:1]
        sa, sc, cross, ex, ey, th = par[q]
        dx = dxs[q]
        d0 = jnp.zeros((SIDE, span), F32)
        d1 = jnp.zeros((SIDE, span), F32)
        d2 = jnp.zeros((SIDE, span), F32)
        for y in range(SIDE):
            at = slice(y * SIDE, (y + 1) * SIDE)
            both = jnp.concatenate([gback[at, :]] * halves, 1)
            al = alpha[q, at, :]
            d = (trans[q, at, :] - (backs[q, at, :] + both) / (1.0 - al)) * al
            ddy = d * dys[q, 0, y : y + 1, :]
            d0 = d0 + d
            d1 = d1 + ddy
            d2 = d2 + ddy * dys[q, 0, y : y + 1, :]
        m0 = jnp.sum(d0, 0, keepdims=True)
        m_x = jnp.sum(d0 * dx, 0, keepdims=True)
        m_y = jnp.sum(d1, 0, keepdims=True)
        m_xx = jnp.sum(d0 * dx * dx, 0, keepdims=True)
        m_xy = jnp.sum(d1 * dx, 0, keepdims=True)
        m_yy = jnp.sum(d2, 0, keepdims=True)
        dpar[q, 0:1, :] = sa * m_x + cross * m_y
        dpar[q, 1:2, :] = cross * m_x + sc * m_y
        dpar[q, 2:3, :] = -(sa * m_xx + cross * m_xy)
        dpar[q, 3:4, :] = -(sc * m_yy + cross * m_xy)
        dpar[q, 4:5, :] = -0.8 * (1.0 - th) * (1.0 + th) * ex * ey * m_xy
        dpar[q, 5:6, :] = m0 / (1.0 + jnp.exp(coef[q, 5:6, :]))
        dpar[q, nparam:, :] = jnp.zeros((ROWS - nparam, span), F32)
        parts = jnp.concatenate(split3(dpar[q]), 0)
        back = dot(parts, hots[q], ((1,), (1,)))
        back = back[:ROWS] + back[ROWS : 2 * ROWS] + back[2 * ROWS :]
        for half in range(2):
            row = half * KSEG * ROWS + q * ROWS
            flat[row : row + ROWS, :] = back[:, half * quarter : (half + 1) * quarter]
    turned = flat[...].T
    for o in range(ndev):
        grads[o] = turned[4 * o : 4 * o + 4, :]


def asked_kernel(cap, base, ndev, owned, me_ref, *refs):
    *arrays, hot, column = refs
    per = arrays[0].shape[0]
    rows = ndev * 4
    for j in range(ndev):
        wide = arrays[j // per][j % per, base : base + cap, :]
        column[4 * j : 4 * j + 4, :] = wide[:4]
        column[rows + 4 * j : rows + 4 * j + 4, :] = wide[4:]
    mine = iota(column.shape, 1) == me_ref[0]
    ids = jnp.sum(jnp.where(mine, column[...], 0.0), 1, keepdims=True).astype(jnp.int32)
    for c in range(owned // LANES):
        cols = iota(column.shape, 1) + c * LANES
        hot[:, c * LANES : (c + 1) * LANES] = (ids == cols).astype(F32).astype(BF16)


def update_kernel(segs, ndev, me_ref, perm, returned, hot, params, moment, second, new_params, new_moment, new_second, held):
    nparam = params.shape[0]
    rank = (iota((4, LANES), 1) // ROWS) % KSEG
    me = me_ref[0]
    for j in range(ndev):
        r = offset_at(ndev, j) ^ me
        block = jnp.zeros((4, LANES), F32)
        for s in range(segs):
            v = perm[r * segs + s]
            block = block + jnp.where(rank == v % KSEG, returned[v // KSEG], 0.0)
        held[4 * j : 4 * j + 4, :] = block
    flat = held[...].T
    half = KSEG * ROWS
    sides = [sum(flat[h * half + q * ROWS : h * half + (q + 1) * ROWS] for q in range(KSEG)) for h in range(2)]
    parts = jnp.concatenate(split3(jnp.concatenate(sides, 1)), 0)
    grad = dot(parts, hot[...])
    grad = (grad[:ROWS] + grad[ROWS : 2 * ROWS] + grad[2 * ROWS :])[:nparam]
    m = 0.9 * moment[...] + 0.1 * grad
    v = 0.99 * second[...] + 0.01 * grad * grad
    new_moment[...] = m
    new_second[...] = v
    new_params[...] = params[...] - 0.05 * m / (jnp.sqrt(v) + 1e-08)


def per_device(params, moment, second, fetch_ids, seg_ids, seg_count, seg_perm, target):
    ndev = lax.axis_size("dev")
    nparam, owned = params.shape
    segs, span = seg_ids.shape
    cap = fetch_ids.shape[2]
    pixels = target.shape[2]
    slots = ndev * cap
    chunks = owned // LANES
    lists = segs * span // LANES
    assert target.shape[0] == 1 and segs == KSEG and pixels == SIDE * SIDE
    assert cap == SUB and chunks == SUB and lists == SUB and ndev <= LANES
    base = nparam * chunks
    me = lax.axis_index("dev").astype(jnp.int32).reshape(1)

    in_hbm = functools.partial(pltpu.with_memory_space_constraint, memory_space=pltpu.HBM)

    packed = pl.pallas_call(
        pack_kernel,
        out_shape=jax.ShapeDtypeStruct((base + 2 * SUB, LANES), F32),
        in_specs=[HBM] * 4,
        out_specs=VMEM,
        scratch_shapes=[
            pltpu.SMEM(seg_count.shape, jnp.int32),
            pltpu.VMEM(seg_ids.shape, jnp.int32),
            pltpu.VMEM((cap, ndev), jnp.int32),
            pltpu.VMEM(params.shape, F32),
            pltpu.SemaphoreType.DMA((4,)),
        ],
        compiler_params=PARAMS,
        name="pack",
    )(*[in_hbm(x) for x in (seg_count, seg_ids, fetch_ids[0].T, params)])
    order, tri, goal, goal_cols = pl.pallas_call(
        layout_kernel,
        out_shape=(
            jax.ShapeDtypeStruct(seg_perm.shape, jnp.int32),
            jax.ShapeDtypeStruct((2, 2 * span, span), BF16),
            jax.ShapeDtypeStruct((ROWS, pixels), F32),
            jax.ShapeDtypeStruct((pixels, LANES), F32),
        ),
        in_specs=[SMEM, VMEM],
        out_specs=(SMEM, VMEM, VMEM, VMEM),
        compiler_params=PARAMS,
        cost_estimate=pl.CostEstimate(flops=0, bytes_accessed=4 * 2**20, transcendentals=0),
        name="layout",
    )(seg_perm, target)
    blocks, (order, tri, goal, goal_cols) = gather_blocks(packed, ndev, (order, tri, goal, goal_cols))
    image, grads = pl.pallas_call(
        functools.partial(render_kernel, segs, cap, nparam, chunks, ndev),
        out_shape=(jax.ShapeDtypeStruct(target.shape, F32), jax.ShapeDtypeStruct((ndev, 4, LANES), F32)),
        in_specs=[SMEM, SMEM] + [VMEM] * (3 + len(blocks)),
        out_specs=(VMEM, VMEM),
        scratch_shapes=[
            pltpu.VMEM((ndev, 2 * SUB, LANES), F32),
            pltpu.VMEM((ndev // 4, ROWS, LANES), F32),
            pltpu.VMEM((KSEG, slots, span), BF16),
            pltpu.VMEM((KSEG, ROWS, span), F32),
            pltpu.VMEM((KSEG, pixels, span), F32),
            pltpu.VMEM((KSEG, pixels, span), F32),
            pltpu.VMEM((KSEG, pixels, 2 * span), BF16),
            pltpu.VMEM((2 * KSEG, pixels, span), BF16),
            pltpu.VMEM((KSEG, pixels, span), F32),
            pltpu.VMEM((KSEG, 2, SIDE, span), F32),
            pltpu.VMEM((KSEG, ROWS, span), F32),
            pltpu.VMEM((pixels, LANES), F32),
            pltpu.VMEM((LANES, slots // 2), F32),
        ],
        compiler_params=PARAMS,
        name="render",
    )(me, order, tri, goal, goal_cols, *blocks)
    returned = lax.all_to_all(grads, "dev", split_axis=0, concat_axis=0, tiled=True)
    hot = pl.pallas_call(
        functools.partial(asked_kernel, cap, base + SUB, ndev, owned),
        out_shape=jax.ShapeDtypeStruct((slots, owned), BF16),
        in_specs=[SMEM] + [VMEM] * len(blocks),
        out_specs=VMEM,
        scratch_shapes=[pltpu.VMEM((slots, LANES), F32)],
        compiler_params=PARAMS,
        name="asked",
    )(me, *blocks)
    new = jax.ShapeDtypeStruct(params.shape, F32)
    new_params, new_moment, new_second = pl.pallas_call(
        functools.partial(update_kernel, segs, ndev),
        out_shape=(new, new, new),
        in_specs=[SMEM, SMEM] + [VMEM] * 5,
        out_specs=(VMEM, VMEM, VMEM),
        scratch_shapes=[pltpu.VMEM((slots // 2, LANES), F32)],
        compiler_params=PARAMS,
        name="update",
    )(me, seg_perm, returned, hot, params, moment, second)
    return (image, new_params, new_moment, new_second)


def solution(mesh):
    placed = (
        P(None, "dev"),
        P(None, "dev"),
        P(None, "dev"),
        P("dev", None, None),
        P("dev", None),
        P("dev"),
        P(),
        P("dev", None, None),
    )
    return jax.shard_map(
        per_device,
        mesh=mesh,
        in_specs=placed,
        out_specs=(P("dev", None, None), P(None, "dev"), P(None, "dev"), P(None, "dev")),
        check_vma=False,
    )
```

time: 50.8 us -> 41.3 us (0.81)
  blocking collectives: 15.3 us -> 0 us
  starting transfers between devices: 5.28 us -> 13.3 us
  local copies, waits for them, and re-layouts: 3.37 us -> 0.61 us
  waiting for transfers between devices: 15.2 us -> 16.9 us
  Pallas kernels: 10.5 us -> 9.52 us
    all_to_all x1 -> x0, blocking collectives: 15.3 us -> none  [per_device(): lists = swap(requests)]
    ppermute x0 -> x10, waiting for transfers between devices: none -> 10.3 us  [pull(): return lax.ppermute(x, 'dev', [(d, d ^ change) for d in range(ndev)])]
    ppermute x0 -> x10, starting transfers between devices: none -> 9.75 us  [pull(): return lax.ppermute(x, 'dev', [(d, d ^ change) for d in range(ndev)])]
    all_to_all x2 -> x1, waiting for transfers between devices: 15.2 us -> 6.62 us  [per_device(): lax.all_to_all(grads, 'dev', split_axis=0, concat_axis=0, tiled=True)]
    unnamed x17 -> x12, local copies, waits for them, and re-layouts: 3.37 us -> 0.61 us
    all_to_all x2 -> x1, starting transfers between devices: 5.28 us -> 3.58 us  [per_device(): lax.all_to_all(grads, 'dev', split_axis=0, concat_axis=0, tiled=True)]
    pallas_call x4 -> x5, Pallas kernels: 10.5 us -> 9.52 us  [the longest x1 4.8 us: per_device(): pl.pallas_call(functools.partial(render_kernel, segs, cap, nparam, chunks...]
  transfers between devices with their start and end apart: 2 -> 11, of which waited for: 2 -> 8; matrix products, arithmetic and copies ran while one was open for 1% -> 1% of each run, Pallas kernels for 0% -> 4%
where the time goes in v2:
time: 41.3 us; the launch traced here: 41.1 us
  waiting for transfers between devices  16.9 us (41%)
  starting transfers between devices  13.3 us (32%)
  Pallas kernels  9.52 us (23%)
  between operations  0.7 us (2%)
  local copies, waits for them, and re-layouts  0.61 us (1%)
    ppermute x10, waiting for transfers between devices, pull(): return lax.ppermute(x, 'dev', [(d, d ^ change) for d in range(ndev)])  10.3 us
    ppermute x10, starting transfers between devices, pull(): return lax.ppermute(x, 'dev', [(d, d ^ change) for d in range(ndev)])  9.75 us
    all_to_all x1, waiting for transfers between devices, per_device(): lax.all_to_all(grads, 'dev', split_axis=0, concat_axis=0, tiled=True)  6.62 us
    pallas_call x1, Pallas kernels, per_device(): pl.pallas_call(functools.partial(render_kernel, segs, cap, nparam, chunks...  4.8 us
    all_to_all x1, starting transfers between devices, per_device(): lax.all_to_all(grads, 'dev', split_axis=0, concat_axis=0, tiled=True)  3.58 us
    pallas_call x1, Pallas kernels, per_device(): pl.pallas_call(functools.partial(update_kernel, segs, ndev), out_shape=(n...  2.25 us
    pallas_call x1, Pallas kernels, per_device(): pl.pallas_call(layout_kernel, out_shape=(jax.ShapeDtypeStruct(seg_perm.sh...  1.34 us
    pallas_call x1, Pallas kernels, per_device(): pl.pallas_call(pack_kernel, out_shape=jax.ShapeDtypeStruct((base + 2 * SU...  0.93 us
  transfers between devices with their start and end apart: 11, of which 8 were waited for; matrix products, arithmetic and copies ran while one was open for 1% of the time, Pallas kernels for 4%

profile of v2, /device:TPU:0, one launch (start us, length us, event | category | flops | bytes accessed | tf_op | source)
XLA Modules:
  0.0 41.1 jit_solution(4230821589265348884)
XLA Ops:
  0.6 0.0 copy-start.4
  0.6 0.9 %pack.1 = f32[88,128]{1,0:T(8,128)S(1)} custom-call(s32[4]{0:T(128)} %count_in.1, s32[4,256]{1,0:T(4,128)} %seg_in.1, s32[8,32]{1,0:T(8,128)} %bitcast.9, f32[9,1024]{1,0:T(8,128)} %params.1), custom_call_target="tpu_custom_call" | custom-call | tf_op jit(solution)/shard_map/pack/pallas_call | solution.py:357
  1.6 0.0 copy-start.3
  1.6 5.1 %collective-permute-start.2 = (f32[1,88,128]{2,1,0:T(8,128)S(1)}, f32[1,88,128]{2,1,0:T(8,128)S(1)}, u32[]{:S(2)}, u32[]{:S(2)}) collective-permute-start(f32[1,88,128]{2,1,0:T(8,128)S(1)} %bitcast.5), channel_id=1, source_target_pairs={{0,24},{1,25},{2,26},{3,27},{4,28},{5,29},{6,30},{7,31},{8,16},{9,... | collective-permute-start | bytes 135176 | tf_op jit(solution)/shard_map/ppermute | solution.py:65
  6.7 0.0 collective-permute-start.1
  6.7 0.6 %collective-permute-start = (f32[1,88,128]{2,1,0:T(8,128)S(1)}, f32[1,88,128]{2,1,0:T(8,128)S(1)}, u32[]{:S(2)}, u32[]{:S(2)}) collective-permute-start(f32[1,88,128]{2,1,0:T(8,128)S(1)} %bitcast.7), channel_id=1, source_target_pairs={{0,8},{1,9},{2,10},{3,11},{4,12},{5,13},{6,14},{7,15},{8,0},{9,1},... | collective-permute-start | bytes 135176 | tf_op jit(solution)/shard_map/ppermute | solution.py:65
  7.3 0.0 copy-done.4
  7.4 1.3 %layout.1 = (s32[128]{0:T(128)S(1)}, bf16[2,512,256]{2,1,0:T(8,128)(2,1)S(1)}, f32[16,256]{1,0:T(8,128)S(1)}, f32[256,128]{1,0:T(8,128)S(1)}) custom-call(s32[128]{0:T(128)S(1)} %copy-done.3, f32[1,3,256]{2,1,0:T(4,128)S(1)} %copy.12.target), custom_call_target="tpu_custom_call" | custom-call | bytes 4194304 | tf_op jit(solution)/shard_map/layout/pallas_call | solution.py:372
  8.7 0.1 collective-permute-done.2
  8.8 2.9 %collective-permute-done.1 = f32[1,88,128]{2,1,0:T(8,128)S(1)} collective-permute-done((f32[1,88,128]{2,1,0:T(8,128)S(1)}, f32[1,88,128]{2,1,0:T(8,128)S(1)}, u32[]{:S(2)}, u32[]{:S(2)}) %collective-permute-start.1) | collective-permute-done | bytes 45088 | tf_op jit(solution)/shard_map/ppermute | solution.py:65
  11.6 0.0 collective-permute-done
  11.7 2.5 %collective-permute-start.5 = (f32[4,88,128]{2,1,0:T(8,128)S(1)}, f32[4,88,128]{2,1,0:T(8,128)S(1)}, u32[]{:S(2)}, u32[]{:S(2)}) collective-permute-start(f32[4,88,128]{2,1,0:T(8,128)S(1)} %pad_maximum_fusion.refs_5_.refs_0_), channel_id=1, source_target_pairs={{0,6},{1,7},{2,4},{3,5},{4,2},{5,3},{6,0},{7,1},{8,14},{9,15},{10,... | collective-permute-start | bytes 540680 | tf_op jit(solution)/shard_map/ppermute | solution.py:65
  14.2 0.5 %collective-permute-start.4 = (f32[4,88,128]{2,1,0:T(8,128)S(1)}, f32[4,88,128]{2,1,0:T(8,128)S(1)}, u32[]{:S(2)}, u32[]{:S(2)}) collective-permute-start(f32[4,88,128]{2,1,0:T(8,128)S(1)} %pad_maximum_fusion.refs_5_.refs_0_), channel_id=1, source_target_pairs={{0,4},{1,5},{2,6},{3,7},{4,0},{5,1},{6,2},{7,3},{8,12},{9,13},{10,... | collective-permute-start | bytes 540680 | tf_op jit(solution)/shard_map/ppermute | solution.py:65
  14.7 0.5 %collective-permute-start.3 = (f32[4,88,128]{2,1,0:T(8,128)S(1)}, f32[4,88,128]{2,1,0:T(8,128)S(1)}, u32[]{:S(2)}, u32[]{:S(2)}) collective-permute-start(f32[4,88,128]{2,1,0:T(8,128)S(1)} %pad_maximum_fusion.refs_5_.refs_0_), channel_id=1, source_target_pairs={{0,2},{1,3},{2,0},{3,1},{4,6},{5,7},{6,4},{7,5},{8,10},{9,11},{10,... | collective-permute-start | bytes 540680 | tf_op jit(solution)/shard_map/ppermute | solution.py:65
  15.2 0.0 collective-permute-start.6
  15.2 4.8 %collective-permute-done.5.refs_8_.refs_3_ = f32[4,88,128]{2,1,0:T(8,128)S(1)} collective-permute-done((f32[4,88,128]{2,1,0:T(8,128)S(1)}, f32[4,88,128]{2,1,0:T(8,128)S(1)}, u32[]{:S(2)}, u32[]{:S(2)}) %collective-permute-start.5) | collective-permute-done | bytes 180256 | tf_op jit(solution)/shard_map/ppermute | solution.py:65
  20.1 0.0 collective-permute-start.9
  20.1 1.3 %collective-permute-done.4.refs_7_.refs_2_ = f32[4,88,128]{2,1,0:T(8,128)S(1)} collective-permute-done((f32[4,88,128]{2,1,0:T(8,128)S(1)}, f32[4,88,128]{2,1,0:T(8,128)S(1)}, u32[]{:S(2)}, u32[]{:S(2)}) %collective-permute-start.4) | collective-permute-done | bytes 180256 | tf_op jit(solution)/shard_map/ppermute | solution.py:65
  21.4 0.0 collective-permute-start.8
  21.4 0.1 collective-permute-done.3.refs_6_.refs_1_
  21.4 0.4 %collective-permute-start.7 = (f32[4,88,128]{2,1,0:T(8,128)S(1)}, f32[4,88,128]{2,1,0:T(8,128)S(1)}, u32[]{:S(2)}, u32[]{:S(2)}) collective-permute-start(f32[4,88,128]{2,1,0:T(8,128)S(1)} %collective-permute-done.3.refs_6_.refs_1_), channel_id=1, source_target_pairs={{0,1},{1,0},{2,3},{3,2},{4,5},{5,4},{6,7},{7,6},{8,9},{9,8},{10,11... | collective-permute-start | bytes 540680 | tf_op jit(solution)/shard_map/ppermute | solution.py:65
  21.9 0.0 collective-permute-done.6.refs_9_.refs_4_
  21.9 0.0 collective-permute-done.9.refs_12_.refs_7_
  21.9 0.9 %collective-permute-done.8.refs_11_.refs_6_ = f32[4,88,128]{2,1,0:T(8,128)S(1)} collective-permute-done((f32[4,88,128]{2,1,0:T(8,128)S(1)}, f32[4,88,128]{2,1,0:T(8,128)S(1)}, u32[]{:S(2)}, u32[]{:S(2)}) %collective-permute-start.8) | collective-permute-done | bytes 180256 | tf_op jit(solution)/shard_map/ppermute | solution.py:65
  22.8 0.3 collective-permute-done.7.refs_10_.refs_5_
  23.0 4.8 %render.1 = (f32[1,3,256]{2,1,0:T(4,128)S(1)}, f32[32,4,128]{2,1,0:T(4,128)}) custom-call(s32[1]{0:T(128)} %bitcast.refs_0_.me_ref, s32[128]{0:T(128)S(1)} %get-tuple-element.22.refs_1_, bf16[2,512,256]{2,1,0:T(8,128)(2,1)S(1)} %get-tuple-element.23.refs_2_, f32[16,256]{1,0:T(8,128)S(1)} %get-tuple-element.24.refs_3_, ...), custom_call_target="tpu_custom_call" | custom-call | tf_op jit(solution)/shard_map/render/pallas_call | solution.py:387
  27.9 3.6 %all-to-all-start = ((f32[32,4,128]{2,1,0:T(4,128)}), f32[32,4,128]{2,1,0:T(4,128)S(1)}, u32[]{:S(2)}, u32[]{:S(2)}) async-start(f32[32,4,128]{2,1,0:T(4,128)} %get-tuple-element.28), calls=%async_computation | async-start | bytes 131072 | tf_op jit(solution)/shard_map/all_to_all | solution.py:410
  31.4 0.6 %copy.13 = f32[1,3,256]{2,0,1:T(1,128)} copy(f32[1,3,256]{2,1,0:T(4,128)S(1)} %get-tuple-element.32) | data formatting | bytes 6144
  32.0 0.2 asked.1.hot
  32.2 6.6 %all-to-all-done.returned = f32[32,4,128]{2,1,0:T(4,128)S(1)} async-done(((f32[32,4,128]{2,1,0:T(4,128)}), f32[32,4,128]{2,1,0:T(4,128)S(1)}, u32[]{:S(2)}, u32[]{:S(2)}) %all-to-all-start) | async-done | bytes 65568 | tf_op jit(solution)/shard_map/all_to_all | solution.py:410
  38.9 0.0 copy-done
  38.9 2.3 %update.1 = (f32[9,1024]{1,0:T(8,128)}, f32[9,1024]{1,0:T(8,128)}, f32[9,1024]{1,0:T(8,128)}) custom-call(s32[1]{0:T(128)} %bitcast.refs_0_.me_ref, s32[128]{0:T(128)S(1)} %copy-done.3, f32[32,4,128]{2,1,0:T(4,128)S(1)} %all-to-all-done.returned, bf16[256,1024]{1,0:T(8,128)(2,1)S(1)} %asked.1.hot, f32[9,1024]{1,0:T(8,128)S(1)} %copy-done, ...), custom_call_target="tpu_custom_call" | custom-call | tf_op jit(solution)/shard_map/update/pallas_call | solution.py:421
  (8 shorter events, 0.0 us)
Async XLA Ops:
  0.6 6.7 %copy-start.4 = (f32[1,3,256]{2,0,1:T(1,128)S(1)}, f32[1,3,256]{2,0,1:T(1,128)}, u32[]{:S(2)}) copy-start(f32[1,3,256]{2,0,1:T(1,128)} %param.15) | copy-start | bytes 9220
  1.6 5.8 %copy-start.3 = (s32[128]{0:T(128)S(1)}, s32[128]{0:T(128)}, u32[]{:S(2)}) copy-start(s32[128]{0:T(128)} %perm.3) | copy-start | bytes 1540
  1.6 7.2 %collective-permute-start.2 = (f32[1,88,128]{2,1,0:T(8,128)S(1)}, f32[1,88,128]{2,1,0:T(8,128)S(1)}, u32[]{:S(2)}, u32[]{:S(2)}) collective-permute-start(f32[1,88,128]{2,1,0:T(8,128)S(1)} %bitcast.5), channel_id=1, source_target_pairs={{0,24},{1,25},{2,26},{3,27},{4,28},{5,29},{6,30},{7,31},{8,16},{9,... | collective-permute-start | bytes 135176 | tf_op jit(solution)/shard_map/ppermute | solution.py:65
  6.7 4.9 %collective-permute-start.1 = (f32[1,88,128]{2,1,0:T(8,128)S(1)}, f32[1,88,128]{2,1,0:T(8,128)S(1)}, u32[]{:S(2)}, u32[]{:S(2)}) collective-permute-start(f32[1,88,128]{2,1,0:T(8,128)S(1)} %bitcast.6), channel_id=1, source_target_pairs={{0,16},{1,17},{2,18},{3,19},{4,20},{5,21},{6,22},{7,23},{8,24},{9,... | collective-permute-start | bytes 135176 | tf_op jit(solution)/shard_map/ppermute | solution.py:65
  6.7 4.9 %collective-permute-start = (f32[1,88,128]{2,1,0:T(8,128)S(1)}, f32[1,88,128]{2,1,0:T(8,128)S(1)}, u32[]{:S(2)}, u32[]{:S(2)}) collective-permute-start(f32[1,88,128]{2,1,0:T(8,128)S(1)} %bitcast.7), channel_id=1, source_target_pairs={{0,8},{1,9},{2,10},{3,11},{4,12},{5,13},{6,14},{7,15},{8,0},{9,1},... | collective-permute-start | bytes 135176 | tf_op jit(solution)/shard_map/ppermute | solution.py:65
  11.7 8.4 %collective-permute-start.5 = (f32[4,88,128]{2,1,0:T(8,128)S(1)}, f32[4,88,128]{2,1,0:T(8,128)S(1)}, u32[]{:S(2)}, u32[]{:S(2)}) collective-permute-start(f32[4,88,128]{2,1,0:T(8,128)S(1)} %pad_maximum_fusion.refs_5_.refs_0_), channel_id=1, source_target_pairs={{0,6},{1,7},{2,4},{3,5},{4,2},{5,3},{6,0},{7,1},{8,14},{9,15},{10,... | collective-permute-start | bytes 540680 | tf_op jit(solution)/shard_map/ppermute | solution.py:65
  14.2 7.2 %collective-permute-start.4 = (f32[4,88,128]{2,1,0:T(8,128)S(1)}, f32[4,88,128]{2,1,0:T(8,128)S(1)}, u32[]{:S(2)}, u32[]{:S(2)}) collective-permute-start(f32[4,88,128]{2,1,0:T(8,128)S(1)} %pad_maximum_fusion.refs_5_.refs_0_), channel_id=1, source_target_pairs={{0,4},{1,5},{2,6},{3,7},{4,0},{5,1},{6,2},{7,3},{8,12},{9,13},{10,... | collective-permute-start | bytes 540680 | tf_op jit(solution)/shard_map/ppermute | solution.py:65
  14.7 6.8 %collective-permute-start.3 = (f32[4,88,128]{2,1,0:T(8,128)S(1)}, f32[4,88,128]{2,1,0:T(8,128)S(1)}, u32[]{:S(2)}, u32[]{:S(2)}) collective-permute-start(f32[4,88,128]{2,1,0:T(8,128)S(1)} %pad_maximum_fusion.refs_5_.refs_0_), channel_id=1, source_target_pairs={{0,2},{1,3},{2,0},{3,1},{4,6},{5,7},{6,4},{7,5},{8,10},{9,11},{10,... | collective-permute-start | bytes 540680 | tf_op jit(solution)/shard_map/ppermute | solution.py:65
  15.2 6.7 %collective-permute-start.6 = (f32[4,88,128]{2,1,0:T(8,128)S(1)}, f32[4,88,128]{2,1,0:T(8,128)S(1)}, u32[]{:S(2)}, u32[]{:S(2)}) collective-permute-start(f32[4,88,128]{2,1,0:T(8,128)S(1)} %pad_maximum_fusion.refs_5_.refs_0_), channel_id=1, source_target_pairs={{0,1},{1,0},{2,3},{3,2},{4,5},{5,4},{6,7},{7,6},{8,9},{9,8},{10,11... | collective-permute-start | bytes 540680 | tf_op jit(solution)/shard_map/ppermute | solution.py:65
  20.1 1.8 %collective-permute-start.9 = (f32[4,88,128]{2,1,0:T(8,128)S(1)}, f32[4,88,128]{2,1,0:T(8,128)S(1)}, u32[]{:S(2)}, u32[]{:S(2)}) collective-permute-start(f32[4,88,128]{2,1,0:T(8,128)S(1)} %collective-permute-done.5.refs_8_.refs_3_), channel_id=1, source_target_pairs={{0,1},{1,0},{2,3},{3,2},{4,5},{5,4},{6,7},{7,6},{8,9},{9,8},{10,11... | collective-permute-start | bytes 540680 | tf_op jit(solution)/shard_map/ppermute | solution.py:65
  21.4 1.4 %collective-permute-start.8 = (f32[4,88,128]{2,1,0:T(8,128)S(1)}, f32[4,88,128]{2,1,0:T(8,128)S(1)}, u32[]{:S(2)}, u32[]{:S(2)}) collective-permute-start(f32[4,88,128]{2,1,0:T(8,128)S(1)} %collective-permute-done.4.refs_7_.refs_2_), channel_id=1, source_target_pairs={{0,1},{1,0},{2,3},{3,2},{4,5},{5,4},{6,7},{7,6},{8,9},{9,8},{10,11... | collective-permute-start | bytes 540680 | tf_op jit(solution)/shard_map/ppermute | solution.py:65
  21.4 1.6 %collective-permute-start.7 = (f32[4,88,128]{2,1,0:T(8,128)S(1)}, f32[4,88,128]{2,1,0:T(8,128)S(1)}, u32[]{:S(2)}, u32[]{:S(2)}) collective-permute-start(f32[4,88,128]{2,1,0:T(8,128)S(1)} %collective-permute-done.3.refs_6_.refs_1_), channel_id=1, source_target_pairs={{0,1},{1,0},{2,3},{3,2},{4,5},{5,4},{6,7},{7,6},{8,9},{9,8},{10,11... | collective-permute-start | bytes 540680 | tf_op jit(solution)/shard_map/ppermute | solution.py:65
  27.9 11.0 %all-to-all-start = ((f32[32,4,128]{2,1,0:T(4,128)}), f32[32,4,128]{2,1,0:T(4,128)S(1)}, u32[]{:S(2)}, u32[]{:S(2)}) async-start(f32[32,4,128]{2,1,0:T(4,128)} %get-tuple-element.28), calls=%async_computation | async-start | bytes 131072 | tf_op jit(solution)/shard_map/all_to_all | solution.py:410
  32.0 6.8 %copy-start = (f32[9,1024]{1,0:T(8,128)S(1)}, f32[9,1024]{1,0:T(8,128)}, u32[]{:S(2)}) copy-start(f32[9,1024]{1,0:T(8,128)} %params.1) | copy-start | bytes 110596
  32.0 6.8 %copy-start.1 = (f32[9,1024]{1,0:T(8,128)S(1)}, f32[9,1024]{1,0:T(8,128)}, u32[]{:S(2)}) copy-start(f32[9,1024]{1,0:T(8,128)} %moment.1) | copy-start | bytes 110596
  32.0 6.8 %copy-start.2 = (f32[9,1024]{1,0:T(8,128)S(1)}, f32[9,1024]{1,0:T(8,128)}, u32[]{:S(2)}) copy-start(f32[9,1024]{1,0:T(8,128)} %second.1) | copy-start | bytes 110596

commit v3 on v2

--- a/solution.py
+++ b/solution.py
@@ -75,6 +75,17 @@
 
 def pick(source, lanes):
     return jnp.take_along_axis(source, lanes, axis=1)
+
+
+def sum_rows(blocks):
+    row = iota((SUB, LANES), 0)
+    for step in (1, 2, 4):
+        first = row & step == 0
+        blocks = [
+            jnp.where(first, a, b) + pltpu.roll(jnp.where(first, b, a), step, 0)
+            for a, b in zip(blocks[::2], blocks[1::2], strict=True)
+        ]
+    return blocks[0]
 
 
 def pack_kernel(count_in, seg_in, fetch_in, params_in, out, count, seg, fetch, params, sems):
@@ -114,7 +125,7 @@
     for half in range(2):
         tri[0, half * span : (half + 1) * span, :] = before
         tri[1, half * span : (half + 1) * span, :] = after
-    rows = target[0]
+    rows = jnp.concatenate([target[c] for c in range(3)], 0)
     pixels = rows.shape[1]
     wide = jnp.concatenate([rows] * 3 + [jnp.zeros((LANES - 9, pixels), F32)], 0)
     goal[...] = wide[:ROWS]
@@ -126,12 +137,12 @@
     narr = 2 << stages(ndev)[-2][1]
     arrays = refs[5 : 5 + narr]
     image, grads = refs[5 + narr : 7 + narr]
-    (idrows, table, hots, coef, alpha, trans, logs, weights, backs, dys, dpar, gback, flat) = refs[7 + narr :]
+    (ids, lists, idrows, table, hots, coef, alpha, trans, logs, weights, colours, backs, dys, dpar, gback, flat) = refs[7 + narr :]
     per = arrays[0].shape[0]
     slots = ndev * cap
     quarter = slots // 2
     pixels = SIDE * SIDE
-    span = hots.shape[2]
+    span = hots.shape[1]
     halves = span // LANES
     me = me_ref[0]
     base = nparam * chunks
@@ -142,15 +153,17 @@
     for j in range(ndev):
         ref, at = block(j)
         idrows[j] = ref[at, base : base + 2 * SUB, :]
-    fetched, listed = [], []
+    fetched = []
     for q in range(KSEG):
         slot = order[me * KSEG + q]
         j = position(ndev, (slot // segs) ^ me)
         fetched.append(idrows[j, SUB : 2 * SUB, :])
-        s = slot % segs
-        listed.append([idrows[j, pl.ds(s * halves + h, 1), :].astype(jnp.int32) for h in range(halves)])
+        for h in range(halves):
+            lists[q * halves + h : q * halves + h + 1, :] = idrows[j, pl.ds((slot % segs) * halves + h, 1), :]
     sub, lane = iota((SUB, LANES), 0), iota((SUB, LANES), 1)
-    rank, which = (lane // cap) % KSEG, lane // (cap * KSEG)
+    low_bits = cap.bit_length() - 1
+    rank, which = (lane >> low_bits) & (KSEG - 1), lane >> (low_bits + 2)
+    extra = []
     for g in range(ndev // 4):
         offs = [offset_at(ndev, 4 * g + b) for b in range(4)]
         off = jnp.where(which == 0, offs[0], jnp.where(which == 1, offs[1], jnp.where(which == 2, offs[2], offs[3])))
@@ -158,48 +171,72 @@
         found = jnp.zeros((SUB, LANES), F32)
         for q in range(KSEG):
             found = jnp.where(rank == q, pick(fetched[q], owner), found)
-        local = jnp.sum(jnp.where(sub == lane % cap, found, 0.0), 0, keepdims=True).astype(jnp.int32)
-        local = jnp.broadcast_to(local, (SUB, LANES))
-        inside, chunk = local % LANES, local // LANES
+        found = jnp.where(sub == lane & (cap - 1), found, 0.0)
+        for step in (4, 2, 1):
+            found = found + pltpu.roll(found, step, 0)
+        local = found.astype(jnp.int32)
+        inside, chunk = local & (LANES - 1), local >> 7
+        got = []
         for p in range(nparam):
-            got = jnp.zeros((SUB, LANES), F32)
+            value = jnp.zeros((SUB, LANES), F32)
             for b in range(4):
                 ref, at = block(4 * g + b)
-                got = jnp.where(which == b, pick(ref[at, p * chunks : (p + 1) * chunks, :], inside), got)
-            table[g, p : p + 1, :] = jnp.sum(jnp.where(sub == chunk, got, 0.0), 0, keepdims=True)
-    slot_row = iota((slots, span), 0)
+                value = jnp.where(which == b, pick(ref[at, p * chunks : (p + 1) * chunks, :], inside), value)
+            got.append(jnp.where(sub == chunk, value, 0.0))
+        table[g] = sum_rows(got[:SUB])
+        last = got[SUB]
+        for step in (4, 2, 1):
+            last = last + pltpu.roll(last, step, 0)
+        extra.append(last)
+    listed = lists[...].astype(jnp.int32)
+    slot = jnp.maximum(listed, 0)
+    pos = position(ndev, (slot >> low_bits) ^ me)
+    spot = ((pos & 3) << (low_bits + 2)) + ((sub // halves) << low_bits) + (slot & (cap - 1))
+    team = pos >> 2
+    live = listed >= 0
+    ninth = jnp.zeros((SUB, LANES), F32)
+    for g in range(ndev // 4):
+        ninth = jnp.where(team == g, pick(extra[g], spot), ninth)
+    ninth = jnp.where(live, ninth, 0.0)
+    k = slot & (cap - 1)
+    into = jnp.where(live, (k >> 2) * quarter + (slot >> low_bits) * 4 + (k & 3), -1).astype(F32)
+    for q in range(KSEG):
+        for h in range(halves):
+            row = q * halves + h
+            cols = slice(h * LANES, (h + 1) * LANES)
+            spot_row = jnp.broadcast_to(spot[row : row + 1, :], (SUB, LANES))
+            team_row = jnp.broadcast_to(team[row : row + 1, :], (SUB, LANES))
+            value = jnp.zeros((SUB, LANES), F32)
+            for g in range(ndev // 4):
+                value = jnp.where(team_row == g, pick(table[g], spot_row), value)
+            coef[q, :SUB, cols] = jnp.where(live[row : row + 1, :], value, 0.0)
+            coef[q, SUB : SUB + 1, cols] = ninth[row : row + 1, :]
+            ids[q : q + 1, cols] = into[row : row + 1, :]
+    thin = iota((span, LANES), 1)
+    gap = jnp.zeros((ROWS - 9, span), F32)
+    groups = []
+    for q in range(KSEG):
+        hi, mid = split2(coef[q, 6:9, :])
+        groups += [hi.astype(F32)] * 3 + [gap] + [mid.astype(F32)] * 3 + [gap]
+    columns = jnp.concatenate(groups, 0).T
+    for q in range(KSEG):
+        both = pltpu.roll(columns, LANES - 2 * q * ROWS, 1) if q else columns
+        colours[2 * q * span : (2 * q + 1) * span, :] = jnp.where(thin < 2 * ROWS, both, 0.0).astype(BF16)
+        colours[(2 * q + 1) * span : 2 * (q + 1) * span, :] = jnp.where(thin < ROWS, both, 0.0).astype(BF16)
+    slot_lane = iota((span, slots), 1)
     fine = (iota((SIDE, span), 0).astype(F32) + 0.5) / SIDE
     pos_x = (me % TILES_X).astype(F32) + fine
     pos_y = (me // TILES_X).astype(F32) + fine
 
     par, dxs = [], []
     for q in range(KSEG):
-        for h in range(halves):
-            row = listed[q][h]
-            live = row >= 0
-            row = jnp.maximum(row, 0)
-            pos = position(ndev, (row // cap) ^ me)
-            spot = jnp.broadcast_to((pos % 4) * (cap * KSEG) + q * cap + row % cap, (SUB, LANES))
-            team = pos // 4
-            low = jnp.zeros((SUB, LANES), F32)
-            high = jnp.zeros((SUB, LANES), F32)
-            for g in range(ndev // 4):
-                low = jnp.where(team == g, pick(table[g, :SUB, :], spot), low)
-                high = jnp.where(team == g, pick(table[g, SUB:, :], spot), high)
-            cols = slice(h * LANES, (h + 1) * LANES)
-            coef[q, :SUB, cols] = jnp.where(live, low, 0.0)
-            coef[q, SUB:, cols] = jnp.where(live, high, 0.0)
-        own = jnp.concatenate(listed[q], 1)
-        live = (own >= 0).astype(F32)
-        k = own % cap
-        own = jnp.where(own >= 0, (k // 4) * quarter + (own // cap) * 4 + k % 4, -1)
-        hots[q] = (slot_row == own).astype(F32).astype(BF16)
+        alive = (ids[q : q + 1, :] >= 0.0).astype(F32)
         got = coef[q]
         mx, my = got[0:1], got[1:2]
         ex, ey = jnp.exp(got[2:3]), jnp.exp(got[3:4])
         th = jnp.tanh(got[4:5])
         sa, sc, cross = ex * ex, ey * ey, 0.8 * th * ex * ey
-        peak = 0.95 / (1.0 + jnp.exp(-got[5:6])) * live
+        peak = 0.95 / (1.0 + jnp.exp(-got[5:6])) * alive
         dx = pos_x - mx
         dy = pos_y - my
         xa = -0.5 * sa * dx * dx
@@ -218,8 +255,10 @@
             logs[q, at, span:] = mid
         trans[q] = dot(logs[q], tri[0])
 
+    places = ids[...].T.astype(jnp.int32)
+    for q in range(KSEG):
+        hots[q] = (slot_lane == places[:, q : q + 1]).astype(F32).astype(BF16)
     ahead = jnp.zeros((pixels, 1), F32)
-    shown = jnp.zeros((pixels, LANES), F32)
     lane = iota((pixels, LANES), 1)
     for q in range(KSEG):
         gback[...] = jnp.broadcast_to(ahead, (pixels, LANES))
@@ -230,25 +269,25 @@
             t = jnp.exp(trans[q, at, :] + both)
             trans[q, at, :] = t
             hi, mid = split2(t * alpha[q, at, :])
-            weights[q, at, :] = hi
-            weights[KSEG + q, at, :] = mid
-        colour = jnp.concatenate([coef[q, 6:9, :]] * 3 + [jnp.zeros((LANES - 9, span), F32)], 0).T
-        c_hi, c_mid = split2(colour)
-        shown = shown + dot(weights[q], c_hi) + dot(weights[q], c_mid) + dot(weights[KSEG + q], c_hi)
+            weights[at, 2 * q * span : (2 * q + 1) * span] = hi
+            weights[at, (2 * q + 1) * span : 2 * (q + 1) * span] = mid
+    shown = dot(weights[...], colours[...])
+    e_hi, e_mid = split2(shown - goal_cols[...])
+    e_cols = jnp.where((lane < 6) | (lane >= 9), e_hi.astype(F32), e_mid.astype(F32)).astype(BF16)
     shot = shown.T
-    image[0] = shot[0:3, :]
-    err = shown - goal_cols[...]
-    e_hi, e_mid = split2(err)
-    e_cols = jnp.where(lane < 6, e_hi.astype(F32), e_mid.astype(F32)).astype(BF16)
-    er_hi, er_mid = split2(shot[:ROWS] - goal[...])
+    shot = shot[:ROWS] + shot[ROWS : 2 * ROWS]
+    for c in range(3):
+        image[c] = shot[c : c + 1, :]
+    er_both = jnp.concatenate(split2(shot - goal[...]), 0)
     behind = jnp.zeros((pixels, 1), F32)
     for q in range(KSEG):
         hi, mid = split2(coef[q, 6:9, :])
         hi, mid = hi.astype(F32), mid.astype(F32)
-        c_rows = jnp.concatenate([hi, mid, hi, jnp.zeros((LANES - 9, span), F32)], 0).astype(BF16)
+        gap = jnp.zeros((ROWS - 9, span), F32)
+        c_rows = jnp.concatenate([hi, mid, hi, gap, hi, jnp.zeros((LANES - ROWS - 3, span), F32)], 0).astype(BF16)
         slope = dot(e_cols, c_rows)
-        w_hi, w_mid = weights[q], weights[KSEG + q]
-        dcol = dot(er_hi, w_hi) + dot(er_hi, w_mid) + dot(er_mid, w_hi)
+        dcol = dot(er_both, weights[:, 2 * q * span : (2 * q + 1) * span])
+        dcol = dcol[:ROWS] + dcol[ROWS:] + dot(er_both[:ROWS], weights[:, (2 * q + 1) * span : 2 * (q + 1) * span])
         dpar[q, 6:9, :] = dcol[0:3]
         for y in range(SIDE):
             at = slice(y * SIDE, (y + 1) * SIDE)
@@ -289,7 +328,7 @@
         dpar[q, 5:6, :] = m0 / (1.0 + jnp.exp(coef[q, 5:6, :]))
         dpar[q, nparam:, :] = jnp.zeros((ROWS - nparam, span), F32)
         parts = jnp.concatenate(split3(dpar[q]), 0)
-        back = dot(parts, hots[q], ((1,), (1,)))
+        back = dot(parts, hots[q])
         back = back[:ROWS] + back[ROWS : 2 * ROWS] + back[2 * ROWS :]
         for half in range(2):
             row = half * KSEG * ROWS + q * ROWS
@@ -316,14 +355,14 @@
 
 def update_kernel(segs, ndev, me_ref, perm, returned, hot, params, moment, second, new_params, new_moment, new_second, held):
     nparam = params.shape[0]
-    rank = (iota((4, LANES), 1) // ROWS) % KSEG
+    rank = (iota((4, LANES), 1) >> 4) & (KSEG - 1)
     me = me_ref[0]
     for j in range(ndev):
         r = offset_at(ndev, j) ^ me
         block = jnp.zeros((4, LANES), F32)
         for s in range(segs):
             v = perm[r * segs + s]
-            block = block + jnp.where(rank == v % KSEG, returned[v // KSEG], 0.0)
+            block = block + jnp.where(rank == v & (KSEG - 1), returned[v >> 2], 0.0)
         held[4 * j : 4 * j + 4, :] = block
     flat = held[...].T
     half = KSEG * ROWS
@@ -348,7 +387,7 @@
     chunks = owned // LANES
     lists = segs * span // LANES
     assert target.shape[0] == 1 and segs == KSEG and pixels == SIDE * SIDE
-    assert cap == SUB and chunks == SUB and lists == SUB and ndev <= LANES
+    assert cap == SUB and chunks == SUB and lists == SUB and ndev <= LANES and nparam == SUB + 1
     base = nparam * chunks
     me = lax.axis_index("dev").astype(jnp.int32).reshape(1)
 
@@ -382,22 +421,25 @@
         compiler_params=PARAMS,
         cost_estimate=pl.CostEstimate(flops=0, bytes_accessed=4 * 2**20, transcendentals=0),
         name="layout",
-    )(seg_perm, target)
+    )(seg_perm, target.transpose(1, 0, 2))
     blocks, (order, tri, goal, goal_cols) = gather_blocks(packed, ndev, (order, tri, goal, goal_cols))
     image, grads = pl.pallas_call(
         functools.partial(render_kernel, segs, cap, nparam, chunks, ndev),
-        out_shape=(jax.ShapeDtypeStruct(target.shape, F32), jax.ShapeDtypeStruct((ndev, 4, LANES), F32)),
+        out_shape=(jax.ShapeDtypeStruct((3, 1, pixels), F32), jax.ShapeDtypeStruct((ndev, 4, LANES), F32)),
         in_specs=[SMEM, SMEM] + [VMEM] * (3 + len(blocks)),
         out_specs=(VMEM, VMEM),
         scratch_shapes=[
+            pltpu.VMEM((SUB, span), F32),
+            pltpu.VMEM((SUB, LANES), F32),
             pltpu.VMEM((ndev, 2 * SUB, LANES), F32),
-            pltpu.VMEM((ndev // 4, ROWS, LANES), F32),
-            pltpu.VMEM((KSEG, slots, span), BF16),
+            pltpu.VMEM((ndev // 4, SUB, LANES), F32),
+            pltpu.VMEM((KSEG, span, slots), BF16),
             pltpu.VMEM((KSEG, ROWS, span), F32),
             pltpu.VMEM((KSEG, pixels, span), F32),
             pltpu.VMEM((KSEG, pixels, span), F32),
             pltpu.VMEM((KSEG, pixels, 2 * span), BF16),
-            pltpu.VMEM((2 * KSEG, pixels, span), BF16),
+            pltpu.VMEM((pixels, 2 * KSEG * span), BF16),
+            pltpu.VMEM((2 * KSEG * span, LANES), BF16),
             pltpu.VMEM((KSEG, pixels, span), F32),
             pltpu.VMEM((KSEG, 2, SIDE, span), F32),
             pltpu.VMEM((KSEG, ROWS, span), F32),
@@ -407,7 +449,6 @@
         compiler_params=PARAMS,
         name="render",
     )(me, order, tri, goal, goal_cols, *blocks)
-    returned = lax.all_to_all(grads, "dev", split_axis=0, concat_axis=0, tiled=True)
     hot = pl.pallas_call(
         functools.partial(asked_kernel, cap, base + SUB, ndev, owned),
         out_shape=jax.ShapeDtypeStruct((slots, owned), BF16),
@@ -417,6 +458,8 @@
         compiler_params=PARAMS,
         name="asked",
     )(me, *blocks)
+    grads, hot = lax.optimization_barrier((grads, hot))
+    returned = lax.all_to_all(grads, "dev", split_axis=0, concat_axis=0, tiled=True)
     new = jax.ShapeDtypeStruct(params.shape, F32)
     new_params, new_moment, new_second = pl.pallas_call(
         functools.partial(update_kernel, segs, ndev),
@@ -427,7 +470,7 @@
         compiler_params=PARAMS,
         name="update",
     )(me, seg_perm, returned, hot, params, moment, second)
-    return (image, new_params, new_moment, new_second)
+    return (image.transpose(1, 0, 2), new_params, new_moment, new_second)
 
 
 def solution(mesh):

time: 41.3 us -> 39.8 us (0.964)
  blocking collectives: 0 us -> 10.8 us
  waiting for transfers between devices: 16.9 us -> 10.3 us
  starting transfers between devices: 13.3 us -> 9.75 us
  Pallas kernels: 9.52 us -> 7.9 us
  local copies, waits for them, and re-layouts: 0.61 us -> 0.03 us
    all_to_all x0 -> x1, blocking collectives: none -> 10.8 us  [per_device(): lax.all_to_all(grads, 'dev', split_axis=0, concat_axis=0, tiled=True)]
    all_to_all x1 -> x0, waiting for transfers between devices: 6.62 us -> none  [per_device(): lax.all_to_all(grads, 'dev', split_axis=0, concat_axis=0, tiled=True)]
    all_to_all x1 -> x0, starting transfers between devices: 3.58 us -> none  [per_device(): lax.all_to_all(grads, 'dev', split_axis=0, concat_axis=0, tiled=True)]
    pallas_call x1, Pallas kernels: 4.8 us -> 3.74 us  [per_device(): pl.pallas_call(functools.partial(render_kernel, segs, cap, nparam, chunks...]
    unnamed x12 -> x10, local copies, waits for them, and re-layouts: 0.61 us -> 0.03 us
    pallas_call x1, Pallas kernels: 2.25 us -> 1.7 us  [per_device(): pl.pallas_call(functools.partial(update_kernel, segs, ndev), out_shape=(n...]
  transfers between devices with their start and end apart: 11 -> 10, of which waited for: 8 -> 7; matrix products, arithmetic and copies ran while one was open for 1% -> 0% of each run, Pallas kernels for 4% -> 3%
where the time goes in v3:
time: 39.8 us; the launch traced here: 39.6 us
  blocking collectives  10.8 us (27%)
  waiting for transfers between devices  10.3 us (26%)
  starting transfers between devices  9.75 us (24%)
  Pallas kernels  7.9 us (20%)
  between operations  0.72 us (2%)
    all_to_all x1, blocking collectives, per_device(): lax.all_to_all(grads, 'dev', split_axis=0, concat_axis=0, tiled=True)  10.8 us
    ppermute x10, waiting for transfers between devices, pull(): return lax.ppermute(x, 'dev', [(d, d ^ change) for d in range(ndev)])  10.3 us
    ppermute x10, starting transfers between devices, pull(): return lax.ppermute(x, 'dev', [(d, d ^ change) for d in range(ndev)])  9.75 us
    pallas_call x1, Pallas kernels, per_device(): pl.pallas_call(functools.partial(render_kernel, segs, cap, nparam, chunks...  3.74 us
    pallas_call x1, Pallas kernels, per_device(): pl.pallas_call(functools.partial(update_kernel, segs, ndev), out_shape=(n...  1.7 us
    pallas_call x1, Pallas kernels, per_device(): pl.pallas_call(layout_kernel, out_shape=(jax.ShapeDtypeStruct(seg_perm.sh...  1.33 us
    pallas_call x1, Pallas kernels, per_device(): pl.pallas_call(pack_kernel, out_shape=jax.ShapeDtypeStruct((base + 2 * SU...  0.92 us
  transfers between devices with their start and end apart: 10, of which 7 were waited for; matrix products, arithmetic and copies ran while one was open for 0% of the time, Pallas kernels for 3%

profile of v3, /device:TPU:0, one launch (start us, length us, event | category | flops | bytes accessed | tf_op | source)
XLA Modules:
  0.0 39.6 jit_solution(9503266915797863174)
XLA Ops:
  0.6 0.9 %pack.1 = f32[88,128]{1,0:T(8,128)S(1)} custom-call(s32[4]{0:T(128)} %count_in.1, s32[4,256]{1,0:T(4,128)} %seg_in.1, s32[8,32]{1,0:T(8,128)} %bitcast.12, f32[9,1024]{1,0:T(8,128)} %params.1), custom_call_target="tpu_custom_call" | custom-call | tf_op jit(solution)/shard_map/pack/pallas_call | solution.py:396
  1.6 0.0 copy-start.3
  1.6 0.0 copy-start.4
  1.6 5.1 %collective-permute-start.2 = (f32[1,88,128]{2,1,0:T(8,128)S(1)}, f32[1,88,128]{2,1,0:T(8,128)S(1)}, u32[]{:S(2)}, u32[]{:S(2)}) collective-permute-start(f32[1,88,128]{2,1,0:T(8,128)S(1)} %bitcast.7), channel_id=1, source_target_pairs={{0,24},{1,25},{2,26},{3,27},{4,28},{5,29},{6,30},{7,31},{8,16},{9,... | collective-permute-start | bytes 135176 | tf_op jit(solution)/shard_map/ppermute | solution.py:65
  6.7 0.0 collective-permute-start.1
  6.7 0.6 %collective-permute-start = (f32[1,88,128]{2,1,0:T(8,128)S(1)}, f32[1,88,128]{2,1,0:T(8,128)S(1)}, u32[]{:S(2)}, u32[]{:S(2)}) collective-permute-start(f32[1,88,128]{2,1,0:T(8,128)S(1)} %bitcast.9), channel_id=1, source_target_pairs={{0,8},{1,9},{2,10},{3,11},{4,12},{5,13},{6,14},{7,15},{8,0},{9,1},... | collective-permute-start | bytes 135176 | tf_op jit(solution)/shard_map/ppermute | solution.py:65
  7.3 0.0 copy-done.3
  7.3 1.3 %layout.1 = (s32[128]{0:T(128)S(1)}, bf16[2,512,256]{2,1,0:T(8,128)(2,1)S(1)}, f32[16,256]{1,0:T(8,128)S(1)}, f32[256,128]{1,0:T(8,128)S(1)}) custom-call(s32[128]{0:T(128)S(1)} %copy-done.4, f32[3,1,256]{2,1,0:T(1,128)S(1)} %bitcast.11), custom_call_target="tpu_custom_call" | custom-call | bytes 4194304 | tf_op jit(solution)/shard_map/layout/pallas_call | solution.py:411
  8.7 0.1 collective-permute-done.2
  8.8 2.9 %collective-permute-done.1 = f32[1,88,128]{2,1,0:T(8,128)S(1)} collective-permute-done((f32[1,88,128]{2,1,0:T(8,128)S(1)}, f32[1,88,128]{2,1,0:T(8,128)S(1)}, u32[]{:S(2)}, u32[]{:S(2)}) %collective-permute-start.1) | collective-permute-done | bytes 45088 | tf_op jit(solution)/shard_map/ppermute | solution.py:65
  11.6 0.0 collective-permute-done
  11.7 2.5 %collective-permute-start.5 = (f32[4,88,128]{2,1,0:T(8,128)S(1)}, f32[4,88,128]{2,1,0:T(8,128)S(1)}, u32[]{:S(2)}, u32[]{:S(2)}) collective-permute-start(f32[4,88,128]{2,1,0:T(8,128)S(1)} %pad_maximum_fusion.refs_5_.refs_0_), channel_id=1, source_target_pairs={{0,6},{1,7},{2,4},{3,5},{4,2},{5,3},{6,0},{7,1},{8,14},{9,15},{10,... | collective-permute-start | bytes 540680 | tf_op jit(solution)/shard_map/ppermute | solution.py:65
  14.2 0.5 %collective-permute-start.4 = (f32[4,88,128]{2,1,0:T(8,128)S(1)}, f32[4,88,128]{2,1,0:T(8,128)S(1)}, u32[]{:S(2)}, u32[]{:S(2)}) collective-permute-start(f32[4,88,128]{2,1,0:T(8,128)S(1)} %pad_maximum_fusion.refs_5_.refs_0_), channel_id=1, source_target_pairs={{0,4},{1,5},{2,6},{3,7},{4,0},{5,1},{6,2},{7,3},{8,12},{9,13},{10,... | collective-permute-start | bytes 540680 | tf_op jit(solution)/shard_map/ppermute | solution.py:65
  14.7 0.5 %collective-permute-start.3 = (f32[4,88,128]{2,1,0:T(8,128)S(1)}, f32[4,88,128]{2,1,0:T(8,128)S(1)}, u32[]{:S(2)}, u32[]{:S(2)}) collective-permute-start(f32[4,88,128]{2,1,0:T(8,128)S(1)} %pad_maximum_fusion.refs_5_.refs_0_), channel_id=1, source_target_pairs={{0,2},{1,3},{2,0},{3,1},{4,6},{5,7},{6,4},{7,5},{8,10},{9,11},{10,... | collective-permute-start | bytes 540680 | tf_op jit(solution)/shard_map/ppermute | solution.py:65
  15.2 0.0 collective-permute-start.6
  15.2 4.8 %collective-permute-done.5.refs_8_.refs_3_ = f32[4,88,128]{2,1,0:T(8,128)S(1)} collective-permute-done((f32[4,88,128]{2,1,0:T(8,128)S(1)}, f32[4,88,128]{2,1,0:T(8,128)S(1)}, u32[]{:S(2)}, u32[]{:S(2)}) %collective-permute-start.5) | collective-permute-done | bytes 180256 | tf_op jit(solution)/shard_map/ppermute | solution.py:65
  20.1 0.0 collective-permute-start.9
  20.1 1.3 %collective-permute-done.4.refs_7_.refs_2_ = f32[4,88,128]{2,1,0:T(8,128)S(1)} collective-permute-done((f32[4,88,128]{2,1,0:T(8,128)S(1)}, f32[4,88,128]{2,1,0:T(8,128)S(1)}, u32[]{:S(2)}, u32[]{:S(2)}) %collective-permute-start.4) | collective-permute-done | bytes 180256 | tf_op jit(solution)/shard_map/ppermute | solution.py:65
  21.4 0.0 collective-permute-start.8
  21.4 0.1 collective-permute-done.3.refs_6_.refs_1_
  21.4 0.4 %collective-permute-start.7 = (f32[4,88,128]{2,1,0:T(8,128)S(1)}, f32[4,88,128]{2,1,0:T(8,128)S(1)}, u32[]{:S(2)}, u32[]{:S(2)}) collective-permute-start(f32[4,88,128]{2,1,0:T(8,128)S(1)} %collective-permute-done.3.refs_6_.refs_1_), channel_id=1, source_target_pairs={{0,1},{1,0},{2,3},{3,2},{4,5},{5,4},{6,7},{7,6},{8,9},{9,8},{10,11... | collective-permute-start | bytes 540680 | tf_op jit(solution)/shard_map/ppermute | solution.py:65
  21.9 0.0 collective-permute-done.6.refs_9_.refs_4_
  21.9 0.0 collective-permute-done.9.refs_12_.refs_7_
  21.9 0.9 %collective-permute-done.8.refs_11_.refs_6_ = f32[4,88,128]{2,1,0:T(8,128)S(1)} collective-permute-done((f32[4,88,128]{2,1,0:T(8,128)S(1)}, f32[4,88,128]{2,1,0:T(8,128)S(1)}, u32[]{:S(2)}, u32[]{:S(2)}) %collective-permute-start.8) | collective-permute-done | bytes 180256 | tf_op jit(solution)/shard_map/ppermute | solution.py:65
  22.8 0.3 collective-permute-done.7.refs_10_.refs_5_
  23.0 0.2 asked.1.hot
  23.2 0.0 copy-start.2
  23.3 3.7 %render.1 = (f32[3,1,256]{2,1,0:T(1,128)}, f32[32,4,128]{2,1,0:T(4,128)S(1)}) custom-call(s32[1]{0:T(128)} %bitcast.refs_0_.me_ref, s32[128]{0:T(128)S(1)} %get-tuple-element.24.refs_1_, bf16[2,512,256]{2,1,0:T(8,128)(2,1)S(1)} %get-tuple-element.25.refs_2_, f32[16,256]{1,0:T(8,128)S(1)} %get-tuple-element.26.refs_3_, ...), custom_call_target="tpu_custom_call" | custom-call | tf_op jit(solution)/shard_map/render/pallas_call | solution.py:426
  27.0 0.0 copy-start
  27.0 0.0 copy-start.1
  27.0 10.8 %all_to_all.5.returned = f32[32,4,128]{2,1,0:T(4,128)S(1)} all-to-all(f32[32,4,128]{2,1,0:T(4,128)S(1)} %get-tuple-element.31), channel_id=1, replica_groups=mesh['dev'=32] {'dev'}, dimensions={0} | all-to-all | bytes 131072 | tf_op jit(solution)/shard_map/all_to_all | solution.py:462
  37.9 1.7 %update.1 = (f32[9,1024]{1,0:T(8,128)}, f32[9,1024]{1,0:T(8,128)}, f32[9,1024]{1,0:T(8,128)}) custom-call(s32[1]{0:T(128)} %bitcast.refs_0_.me_ref, s32[128]{0:T(128)S(1)} %copy-done.4, f32[32,4,128]{2,1,0:T(4,128)S(1)} %all_to_all.5.returned, bf16[256,1024]{1,0:T(8,128)(2,1)S(1)} %asked.1.hot, f32[9,1024]{1,0:T(8,128)S(1)} %copy-done, ...), custom_call_target="tpu_custom_call" | custom-call | tf_op jit(solution)/shard_map/update/pallas_call | solution.py:464
  (5 shorter events, 0.0 us)
Async XLA Ops:
  1.6 5.8 %copy-start.3 = (f32[1,3,256]{2,0,1:T(1,128)S(1)}, f32[1,3,256]{2,0,1:T(1,128)}, u32[]{:S(2)}) copy-start(f32[1,3,256]{2,0,1:T(1,128)} %param.15) | copy-start | bytes 9220
  1.6 5.8 %copy-start.4 = (s32[128]{0:T(128)S(1)}, s32[128]{0:T(128)}, u32[]{:S(2)}) copy-start(s32[128]{0:T(128)} %perm.3) | copy-start | bytes 1540
  1.6 7.2 %collective-permute-start.2 = (f32[1,88,128]{2,1,0:T(8,128)S(1)}, f32[1,88,128]{2,1,0:T(8,128)S(1)}, u32[]{:S(2)}, u32[]{:S(2)}) collective-permute-start(f32[1,88,128]{2,1,0:T(8,128)S(1)} %bitcast.7), channel_id=1, source_target_pairs={{0,24},{1,25},{2,26},{3,27},{4,28},{5,29},{6,30},{7,31},{8,16},{9,... | collective-permute-start | bytes 135176 | tf_op jit(solution)/shard_map/ppermute | solution.py:65
  6.7 4.9 %collective-permute-start.1 = (f32[1,88,128]{2,1,0:T(8,128)S(1)}, f32[1,88,128]{2,1,0:T(8,128)S(1)}, u32[]{:S(2)}, u32[]{:S(2)}) collective-permute-start(f32[1,88,128]{2,1,0:T(8,128)S(1)} %bitcast.8), channel_id=1, source_target_pairs={{0,16},{1,17},{2,18},{3,19},{4,20},{5,21},{6,22},{7,23},{8,24},{9,... | collective-permute-start | bytes 135176 | tf_op jit(solution)/shard_map/ppermute | solution.py:65
  6.7 4.9 %collective-permute-start = (f32[1,88,128]{2,1,0:T(8,128)S(1)}, f32[1,88,128]{2,1,0:T(8,128)S(1)}, u32[]{:S(2)}, u32[]{:S(2)}) collective-permute-start(f32[1,88,128]{2,1,0:T(8,128)S(1)} %bitcast.9), channel_id=1, source_target_pairs={{0,8},{1,9},{2,10},{3,11},{4,12},{5,13},{6,14},{7,15},{8,0},{9,1},... | collective-permute-start | bytes 135176 | tf_op jit(solution)/shard_map/ppermute | solution.py:65
  11.7 8.4 %collective-permute-start.5 = (f32[4,88,128]{2,1,0:T(8,128)S(1)}, f32[4,88,128]{2,1,0:T(8,128)S(1)}, u32[]{:S(2)}, u32[]{:S(2)}) collective-permute-start(f32[4,88,128]{2,1,0:T(8,128)S(1)} %pad_maximum_fusion.refs_5_.refs_0_), channel_id=1, source_target_pairs={{0,6},{1,7},{2,4},{3,5},{4,2},{5,3},{6,0},{7,1},{8,14},{9,15},{10,... | collective-permute-start | bytes 540680 | tf_op jit(solution)/shard_map/ppermute | solution.py:65
  14.2 7.2 %collective-permute-start.4 = (f32[4,88,128]{2,1,0:T(8,128)S(1)}, f32[4,88,128]{2,1,0:T(8,128)S(1)}, u32[]{:S(2)}, u32[]{:S(2)}) collective-permute-start(f32[4,88,128]{2,1,0:T(8,128)S(1)} %pad_maximum_fusion.refs_5_.refs_0_), channel_id=1, source_target_pairs={{0,4},{1,5},{2,6},{3,7},{4,0},{5,1},{6,2},{7,3},{8,12},{9,13},{10,... | collective-permute-start | bytes 540680 | tf_op jit(solution)/shard_map/ppermute | solution.py:65
  14.7 6.8 %collective-permute-start.3 = (f32[4,88,128]{2,1,0:T(8,128)S(1)}, f32[4,88,128]{2,1,0:T(8,128)S(1)}, u32[]{:S(2)}, u32[]{:S(2)}) collective-permute-start(f32[4,88,128]{2,1,0:T(8,128)S(1)} %pad_maximum_fusion.refs_5_.refs_0_), channel_id=1, source_target_pairs={{0,2},{1,3},{2,0},{3,1},{4,6},{5,7},{6,4},{7,5},{8,10},{9,11},{10,... | collective-permute-start | bytes 540680 | tf_op jit(solution)/shard_map/ppermute | solution.py:65
  15.2 6.7 %collective-permute-start.6 = (f32[4,88,128]{2,1,0:T(8,128)S(1)}, f32[4,88,128]{2,1,0:T(8,128)S(1)}, u32[]{:S(2)}, u32[]{:S(2)}) collective-permute-start(f32[4,88,128]{2,1,0:T(8,128)S(1)} %pad_maximum_fusion.refs_5_.refs_0_), channel_id=1, source_target_pairs={{0,1},{1,0},{2,3},{3,2},{4,5},{5,4},{6,7},{7,6},{8,9},{9,8},{10,11... | collective-permute-start | bytes 540680 | tf_op jit(solution)/shard_map/ppermute | solution.py:65
  20.1 1.8 %collective-permute-start.9 = (f32[4,88,128]{2,1,0:T(8,128)S(1)}, f32[4,88,128]{2,1,0:T(8,128)S(1)}, u32[]{:S(2)}, u32[]{:S(2)}) collective-permute-start(f32[4,88,128]{2,1,0:T(8,128)S(1)} %collective-permute-done.5.refs_8_.refs_3_), channel_id=1, source_target_pairs={{0,1},{1,0},{2,3},{3,2},{4,5},{5,4},{6,7},{7,6},{8,9},{9,8},{10,11... | collective-permute-start | bytes 540680 | tf_op jit(solution)/shard_map/ppermute | solution.py:65
  21.4 1.4 %collective-permute-start.8 = (f32[4,88,128]{2,1,0:T(8,128)S(1)}, f32[4,88,128]{2,1,0:T(8,128)S(1)}, u32[]{:S(2)}, u32[]{:S(2)}) collective-permute-start(f32[4,88,128]{2,1,0:T(8,128)S(1)} %collective-permute-done.4.refs_7_.refs_2_), channel_id=1, source_target_pairs={{0,1},{1,0},{2,3},{3,2},{4,5},{5,4},{6,7},{7,6},{8,9},{9,8},{10,11... | collective-permute-start | bytes 540680 | tf_op jit(solution)/shard_map/ppermute | solution.py:65
  21.4 1.6 %collective-permute-start.7 = (f32[4,88,128]{2,1,0:T(8,128)S(1)}, f32[4,88,128]{2,1,0:T(8,128)S(1)}, u32[]{:S(2)}, u32[]{:S(2)}) collective-permute-start(f32[4,88,128]{2,1,0:T(8,128)S(1)} %collective-permute-done.3.refs_6_.refs_1_), channel_id=1, source_target_pairs={{0,1},{1,0},{2,3},{3,2},{4,5},{5,4},{6,7},{7,6},{8,9},{9,8},{10,11... | collective-permute-start | bytes 540680 | tf_op jit(solution)/shard_map/ppermute | solution.py:65
  23.2 14.6 %copy-start.2 = (f32[9,1024]{1,0:T(8,128)S(1)}, f32[9,1024]{1,0:T(8,128)}, u32[]{:S(2)}) copy-start(f32[9,1024]{1,0:T(8,128)} %second.1) | copy-start | bytes 110596
  27.0 10.8 %copy-start = (f32[9,1024]{1,0:T(8,128)S(1)}, f32[9,1024]{1,0:T(8,128)}, u32[]{:S(2)}) copy-start(f32[9,1024]{1,0:T(8,128)} %params.1) | copy-start | bytes 110596
  27.0 10.8 %copy-start.1 = (f32[9,1024]{1,0:T(8,128)S(1)}, f32[9,1024]{1,0:T(8,128)}, u32[]{:S(2)}) copy-start(f32[9,1024]{1,0:T(8,128)} %moment.1) | copy-start | bytes 110596

commit v4 on v3

--- a/solution.py
+++ b/solution.py
@@ -112,12 +112,26 @@
     out[at : at + SUB, : fetch.shape[1]] = fetch[...].astype(F32)
 
 
-def layout_kernel(perm, target, order, tri, goal, goal_cols):
-    def place(j, carry):
-        order[perm[j]] = j
-        return carry
-
-    lax.fori_loop(0, perm.shape[0], place, 0, unroll=8)
+def layout_kernel(me_ref, perm, target, tri, goal, goal_cols, back):
+    width = back.shape[1]
+    ndev = width // 4
+    lane = iota((SUB, LANES), 1)
+    row = iota((KSEG * width, LANES), 0)
+    wanted = ((row & (width - 1)) >> 2) * KSEG + row // width
+    for part in range(width // LANES):
+        cols = lane + part * LANES
+        requester = offset_at(ndev, cols >> 2) ^ me_ref[0]
+        same_k = (iota((KSEG * width, LANES), 1) & 3) == (row & 3)
+        hit = jnp.zeros((KSEG * width, LANES), F32)
+        for s in range(KSEG):
+            at = requester * KSEG + s
+            held = jnp.zeros((SUB, LANES), F32)
+            for g in range(perm.shape[0]):
+                source = jnp.broadcast_to(perm[g : g + 1, :].astype(F32), (SUB, LANES))
+                held = jnp.where(at >> 7 == g, pick(source, at & (LANES - 1)), held)
+            held = held[:1, :].astype(jnp.int32)
+            hit = hit + jnp.where((wanted == held) & same_k, 1.0, 0.0)
+        back[:, part * LANES : (part + 1) * LANES] = hit.astype(BF16)
     span = tri.shape[2]
     src, dst = iota((span, span), 0), iota((span, span), 1)
     before = (src < dst).astype(F32).astype(BF16)
@@ -133,11 +147,11 @@
 
 
 def render_kernel(segs, cap, nparam, chunks, ndev, *refs):
-    me_ref, order, tri, goal, goal_cols = refs[:5]
+    me_ref, perm, tri, goal, goal_cols = refs[:5]
     narr = 2 << stages(ndev)[-2][1]
     arrays = refs[5 : 5 + narr]
-    image, grads = refs[5 + narr : 7 + narr]
-    (ids, lists, idrows, table, hots, coef, alpha, trans, logs, weights, colours, backs, dys, dpar, gback, flat) = refs[7 + narr :]
+    image, grads, asked = refs[5 + narr : 8 + narr]
+    (column, ids, lists, idrows, table, hots, coef, alpha, trans, logs, weights, colours, backs, dys, dpar, gback, flat) = refs[8 + narr :]
     per = arrays[0].shape[0]
     slots = ndev * cap
     quarter = slots // 2
@@ -154,12 +168,13 @@
         ref, at = block(j)
         idrows[j] = ref[at, base : base + 2 * SUB, :]
     fetched = []
-    for q in range(KSEG):
-        slot = order[me * KSEG + q]
-        j = position(ndev, (slot // segs) ^ me)
+    places = (iota(perm.shape, 0) * LANES + iota(perm.shape, 1)).astype(F32)
+    for q in range(KSEG):
+        slot = jnp.sum(jnp.where(perm[...] == me * KSEG + q, places, 0.0)).astype(jnp.int32)
+        j = position(ndev, (slot >> 2) ^ me)
         fetched.append(idrows[j, SUB : 2 * SUB, :])
         for h in range(halves):
-            lists[q * halves + h : q * halves + h + 1, :] = idrows[j, pl.ds((slot % segs) * halves + h, 1), :]
+            lists[q * halves + h : q * halves + h + 1, :] = idrows[j, pl.ds((slot & 3) * halves + h, 1), :]
     sub, lane = iota((SUB, LANES), 0), iota((SUB, LANES), 1)
     low_bits = cap.bit_length() - 1
     rank, which = (lane >> low_bits) & (KSEG - 1), lane >> (low_bits + 2)
@@ -255,9 +270,9 @@
             logs[q, at, span:] = mid
         trans[q] = dot(logs[q], tri[0])
 
-    places = ids[...].T.astype(jnp.int32)
-    for q in range(KSEG):
-        hots[q] = (slot_lane == places[:, q : q + 1]).astype(F32).astype(BF16)
+    rows_of = ids[...].T.astype(jnp.int32)
+    for q in range(KSEG):
+        hots[q] = (slot_lane == rows_of[:, q : q + 1]).astype(F32).astype(BF16)
     ahead = jnp.zeros((pixels, 1), F32)
     lane = iota((pixels, LANES), 1)
     for q in range(KSEG):
@@ -279,6 +294,14 @@
     for c in range(3):
         image[c] = shot[c : c + 1, :]
     er_both = jnp.concatenate(split2(shot - goal[...]), 0)
+    for j in range(ndev):
+        column[4 * j : 4 * j + 4, :] = idrows[j, SUB : SUB + 4, :]
+        column[quarter + 4 * j : quarter + 4 * j + 4, :] = idrows[j, SUB + 4 : 2 * SUB, :]
+    mine = iota(column.shape, 1) == me
+    wanted = jnp.sum(jnp.where(mine, column[...], 0.0), 1, keepdims=True).astype(jnp.int32)
+    for c in range(chunks):
+        cols = iota(column.shape, 1) + c * LANES
+        asked[:, c * LANES : (c + 1) * LANES] = (wanted == cols).astype(F32).astype(BF16)
     behind = jnp.zeros((pixels, 1), F32)
     for q in range(KSEG):
         hi, mid = split2(coef[q, 6:9, :])
@@ -338,36 +361,18 @@
         grads[o] = turned[4 * o : 4 * o + 4, :]
 
 
-def asked_kernel(cap, base, ndev, owned, me_ref, *refs):
-    *arrays, hot, column = refs
-    per = arrays[0].shape[0]
-    rows = ndev * 4
-    for j in range(ndev):
-        wide = arrays[j // per][j % per, base : base + cap, :]
-        column[4 * j : 4 * j + 4, :] = wide[:4]
-        column[rows + 4 * j : rows + 4 * j + 4, :] = wide[4:]
-    mine = iota(column.shape, 1) == me_ref[0]
-    ids = jnp.sum(jnp.where(mine, column[...], 0.0), 1, keepdims=True).astype(jnp.int32)
-    for c in range(owned // LANES):
-        cols = iota(column.shape, 1) + c * LANES
-        hot[:, c * LANES : (c + 1) * LANES] = (ids == cols).astype(F32).astype(BF16)
-
-
-def update_kernel(segs, ndev, me_ref, perm, returned, hot, params, moment, second, new_params, new_moment, new_second, held):
+def update_kernel(returned, back, hot, params, moment, second, new_params, new_moment, new_second):
     nparam = params.shape[0]
-    rank = (iota((4, LANES), 1) >> 4) & (KSEG - 1)
-    me = me_ref[0]
-    for j in range(ndev):
-        r = offset_at(ndev, j) ^ me
-        block = jnp.zeros((4, LANES), F32)
-        for s in range(segs):
-            v = perm[r * segs + s]
-            block = block + jnp.where(rank == v & (KSEG - 1), returned[v >> 2], 0.0)
-        held[4 * j : 4 * j + 4, :] = block
-    flat = held[...].T
+    flat = returned[...].T
     half = KSEG * ROWS
-    sides = [sum(flat[h * half + q * ROWS : h * half + (q + 1) * ROWS] for q in range(KSEG)) for h in range(2)]
-    parts = jnp.concatenate(split3(jnp.concatenate(sides, 1)), 0)
+    sides = [
+        jnp.concatenate([flat[h * half + q * ROWS : h * half + (q + 1) * ROWS] for q in range(KSEG)], 1)
+        for h in range(2)
+    ]
+    parts = jnp.concatenate(split3(jnp.concatenate(sides, 0)), 0)
+    asked = dot(parts, back[...])
+    asked = asked[: 2 * ROWS] + asked[2 * ROWS : 4 * ROWS] + asked[4 * ROWS :]
+    parts = jnp.concatenate(split3(jnp.concatenate([asked[:ROWS], asked[ROWS:]], 1)), 0)
     grad = dot(parts, hot[...])
     grad = (grad[:ROWS] + grad[ROWS : 2 * ROWS] + grad[2 * ROWS :])[:nparam]
     m = 0.9 * moment[...] + 0.1 * grad
@@ -389,6 +394,7 @@
     assert target.shape[0] == 1 and segs == KSEG and pixels == SIDE * SIDE
     assert cap == SUB and chunks == SUB and lists == SUB and ndev <= LANES and nparam == SUB + 1
     base = nparam * chunks
+    perm = seg_perm.reshape(-1, LANES)
     me = lax.axis_index("dev").astype(jnp.int32).reshape(1)
 
     in_hbm = functools.partial(pltpu.with_memory_space_constraint, memory_space=pltpu.HBM)
@@ -408,27 +414,32 @@
         compiler_params=PARAMS,
         name="pack",
     )(*[in_hbm(x) for x in (seg_count, seg_ids, fetch_ids[0].T, params)])
-    order, tri, goal, goal_cols = pl.pallas_call(
+    tri, goal, goal_cols, back = pl.pallas_call(
         layout_kernel,
         out_shape=(
-            jax.ShapeDtypeStruct(seg_perm.shape, jnp.int32),
             jax.ShapeDtypeStruct((2, 2 * span, span), BF16),
             jax.ShapeDtypeStruct((ROWS, pixels), F32),
             jax.ShapeDtypeStruct((pixels, LANES), F32),
+            jax.ShapeDtypeStruct((KSEG * 4 * ndev, 4 * ndev), BF16),
         ),
-        in_specs=[SMEM, VMEM],
-        out_specs=(SMEM, VMEM, VMEM, VMEM),
+        in_specs=[SMEM, VMEM, VMEM],
+        out_specs=(VMEM, VMEM, VMEM, VMEM),
         compiler_params=PARAMS,
         cost_estimate=pl.CostEstimate(flops=0, bytes_accessed=4 * 2**20, transcendentals=0),
         name="layout",
-    )(seg_perm, target.transpose(1, 0, 2))
-    blocks, (order, tri, goal, goal_cols) = gather_blocks(packed, ndev, (order, tri, goal, goal_cols))
-    image, grads = pl.pallas_call(
+    )(me, perm, target.transpose(1, 0, 2))
+    blocks, (tri, goal, goal_cols, back) = gather_blocks(packed, ndev, (tri, goal, goal_cols, back))
+    image, grads, hot = pl.pallas_call(
         functools.partial(render_kernel, segs, cap, nparam, chunks, ndev),
-        out_shape=(jax.ShapeDtypeStruct((3, 1, pixels), F32), jax.ShapeDtypeStruct((ndev, 4, LANES), F32)),
-        in_specs=[SMEM, SMEM] + [VMEM] * (3 + len(blocks)),
-        out_specs=(VMEM, VMEM),
+        out_shape=(
+            jax.ShapeDtypeStruct((3, 1, pixels), F32),
+            jax.ShapeDtypeStruct((ndev, 4, LANES), F32),
+            jax.ShapeDtypeStruct((slots, owned), BF16),
+        ),
+        in_specs=[SMEM] + [VMEM] * (4 + len(blocks)),
+        out_specs=(VMEM, VMEM, VMEM),
         scratch_shapes=[
+            pltpu.VMEM((slots, LANES), F32),
             pltpu.VMEM((SUB, span), F32),
             pltpu.VMEM((SUB, LANES), F32),
             pltpu.VMEM((ndev, 2 * SUB, LANES), F32),
@@ -448,28 +459,17 @@
         ],
         compiler_params=PARAMS,
         name="render",
-    )(me, order, tri, goal, goal_cols, *blocks)
-    hot = pl.pallas_call(
-        functools.partial(asked_kernel, cap, base + SUB, ndev, owned),
-        out_shape=jax.ShapeDtypeStruct((slots, owned), BF16),
-        in_specs=[SMEM] + [VMEM] * len(blocks),
-        out_specs=VMEM,
-        scratch_shapes=[pltpu.VMEM((slots, LANES), F32)],
-        compiler_params=PARAMS,
-        name="asked",
-    )(me, *blocks)
-    grads, hot = lax.optimization_barrier((grads, hot))
+    )(me, perm, tri, goal, goal_cols, *blocks)
     returned = lax.all_to_all(grads, "dev", split_axis=0, concat_axis=0, tiled=True)
     new = jax.ShapeDtypeStruct(params.shape, F32)
     new_params, new_moment, new_second = pl.pallas_call(
-        functools.partial(update_kernel, segs, ndev),
+        update_kernel,
         out_shape=(new, new, new),
-        in_specs=[SMEM, SMEM] + [VMEM] * 5,
+        in_specs=[VMEM] * 6,
         out_specs=(VMEM, VMEM, VMEM),
-        scratch_shapes=[pltpu.VMEM((slots // 2, LANES), F32)],
         compiler_params=PARAMS,
         name="update",
-    )(me, seg_perm, returned, hot, params, moment, second)
+    )(returned.reshape(4 * ndev, LANES), back, hot, params, moment, second)
     return (image.transpose(1, 0, 2), new_params, new_moment, new_second)
 
 

time: 39.8 us -> 38.6 us (0.970)
  Pallas kernels: 7.9 us -> 5.73 us
  local copies, waits for them, and re-layouts: 0.03 us -> 0.7 us
    pallas_call x3 -> x2, Pallas kernels: 3.23 us -> 1.44 us  [the longest x1 1.1 us: per_device(): pl.pallas_call(update_kernel, out_shape=(new, new, new), in_specs=[VMEM]...]
    unnamed x10, local copies, waits for them, and re-layouts: 0.03 us -> 0.7 us
  transfers between devices with their start and end apart: 10 -> 10, of which waited for: 7 -> 7; matrix products, arithmetic and copies ran while one was open for 0% -> 0% of each run, Pallas kernels for 3% -> 1%
where the time goes in v4:
time: 38.6 us; the launch traced here: 38.3 us
  blocking collectives  10.8 us (28%)
  waiting for transfers between devices  10.6 us (27%)
  starting transfers between devices  9.75 us (25%)
  Pallas kernels  5.73 us (15%)
  local copies, waits for them, and re-layouts  0.7 us (2%)
  between operations  0.68 us (2%)
    all_to_all x1, blocking collectives, per_device(): lax.all_to_all(grads, 'dev', split_axis=0, concat_axis=0, tiled=True)  10.8 us
    ppermute x10, waiting for transfers between devices, pull(): return lax.ppermute(x, 'dev', [(d, d ^ change) for d in range(ndev)])  10.6 us
    ppermute x10, starting transfers between devices, pull(): return lax.ppermute(x, 'dev', [(d, d ^ change) for d in range(ndev)])  9.75 us
    pallas_call x1, Pallas kernels, per_device(): pl.pallas_call(functools.partial(render_kernel, segs, cap, nparam, chunks...  3.37 us
    pallas_call x1, Pallas kernels, per_device(): pl.pallas_call(update_kernel, out_shape=(new, new, new), in_specs=[VMEM]...  1.1 us
    pallas_call x1, Pallas kernels, per_device(): pl.pallas_call(pack_kernel, out_shape=jax.ShapeDtypeStruct((base + 2 * SU...  0.92 us
  transfers between devices with their start and end apart: 10, of which 7 were waited for; matrix products, arithmetic and copies ran while one was open for 0% of the time, Pallas kernels for 1%

profile of v4, /device:TPU:0, one launch (start us, length us, event | category | flops | bytes accessed | tf_op | source)
XLA Modules:
  0.0 38.3 jit_solution(18262423565339912502)
XLA Ops:
  0.6 0.9 %pack.1 = f32[88,128]{1,0:T(8,128)S(1)} custom-call(s32[4]{0:T(128)} %count_in.1, s32[4,256]{1,0:T(4,128)} %seg_in.1, s32[8,32]{1,0:T(8,128)} %bitcast.17, f32[9,1024]{1,0:T(8,128)} %params.1), custom_call_target="tpu_custom_call" | custom-call | tf_op jit(solution)/shard_map/pack/pallas_call | solution.py:402
  1.6 5.1 %collective-permute-start.2 = (f32[1,88,128]{2,1,0:T(8,128)S(1)}, f32[1,88,128]{2,1,0:T(8,128)S(1)}, u32[]{:S(2)}, u32[]{:S(2)}) collective-permute-start(f32[1,88,128]{2,1,0:T(8,128)S(1)} %bitcast.10), channel_id=1, source_target_pairs={{0,24},{1,25},{2,26},{3,27},{4,28},{5,29},{6,30},{7,31},{8,16},{9,... | collective-permute-start | bytes 135176 | tf_op jit(solution)/shard_map/ppermute | solution.py:65
  6.7 0.0 collective-permute-start.1
  6.7 0.6 %collective-permute-start = (f32[1,88,128]{2,1,0:T(8,128)S(1)}, f32[1,88,128]{2,1,0:T(8,128)S(1)}, u32[]{:S(2)}, u32[]{:S(2)}) collective-permute-start(f32[1,88,128]{2,1,0:T(8,128)S(1)} %bitcast.12), channel_id=1, source_target_pairs={{0,8},{1,9},{2,10},{3,11},{4,12},{5,13},{6,14},{7,15},{8,0},{9,1},... | collective-permute-start | bytes 135176 | tf_op jit(solution)/shard_map/ppermute | solution.py:65
  7.3 0.7 %copy-done.3 = f32[1,3,256]{2,0,1:T(1,128)S(1)} copy-done((f32[1,3,256]{2,0,1:T(1,128)S(1)}, f32[1,3,256]{2,0,1:T(1,128)}, u32[]{:S(2)}) %copy-start.3) | copy-done | bytes 3096
  8.0 0.0 copy-done.4
  8.0 0.3 layout.1
  8.3 0.4 %collective-permute-done.2 = f32[1,88,128]{2,1,0:T(8,128)S(1)} collective-permute-done((f32[1,88,128]{2,1,0:T(8,128)S(1)}, f32[1,88,128]{2,1,0:T(8,128)S(1)}, u32[]{:S(2)}, u32[]{:S(2)}) %collective-permute-start.2) | collective-permute-done | bytes 45088 | tf_op jit(solution)/shard_map/ppermute | solution.py:65
  8.8 2.9 %collective-permute-done.1 = f32[1,88,128]{2,1,0:T(8,128)S(1)} collective-permute-done((f32[1,88,128]{2,1,0:T(8,128)S(1)}, f32[1,88,128]{2,1,0:T(8,128)S(1)}, u32[]{:S(2)}, u32[]{:S(2)}) %collective-permute-start.1) | collective-permute-done | bytes 45088 | tf_op jit(solution)/shard_map/ppermute | solution.py:65
  11.6 0.0 collective-permute-done
  11.6 2.5 %collective-permute-start.5 = (f32[4,88,128]{2,1,0:T(8,128)S(1)}, f32[4,88,128]{2,1,0:T(8,128)S(1)}, u32[]{:S(2)}, u32[]{:S(2)}) collective-permute-start(f32[4,88,128]{2,1,0:T(8,128)S(1)} %pad_maximum_fusion.refs_5_), channel_id=1, source_target_pairs={{0,6},{1,7},{2,4},{3,5},{4,2},{5,3},{6,0},{7,1},{8,14},{9,15},{10,... | collective-permute-start | bytes 540680 | tf_op jit(solution)/shard_map/ppermute | solution.py:65
  14.2 0.5 %collective-permute-start.4 = (f32[4,88,128]{2,1,0:T(8,128)S(1)}, f32[4,88,128]{2,1,0:T(8,128)S(1)}, u32[]{:S(2)}, u32[]{:S(2)}) collective-permute-start(f32[4,88,128]{2,1,0:T(8,128)S(1)} %pad_maximum_fusion.refs_5_), channel_id=1, source_target_pairs={{0,4},{1,5},{2,6},{3,7},{4,0},{5,1},{6,2},{7,3},{8,12},{9,13},{10,... | collective-permute-start | bytes 540680 | tf_op jit(solution)/shard_map/ppermute | solution.py:65
  14.7 0.5 %collective-permute-start.3 = (f32[4,88,128]{2,1,0:T(8,128)S(1)}, f32[4,88,128]{2,1,0:T(8,128)S(1)}, u32[]{:S(2)}, u32[]{:S(2)}) collective-permute-start(f32[4,88,128]{2,1,0:T(8,128)S(1)} %pad_maximum_fusion.refs_5_), channel_id=1, source_target_pairs={{0,2},{1,3},{2,0},{3,1},{4,6},{5,7},{6,4},{7,5},{8,10},{9,11},{10,... | collective-permute-start | bytes 540680 | tf_op jit(solution)/shard_map/ppermute | solution.py:65
  15.2 0.0 collective-permute-start.6
  15.2 4.8 %collective-permute-done.5.refs_8_ = f32[4,88,128]{2,1,0:T(8,128)S(1)} collective-permute-done((f32[4,88,128]{2,1,0:T(8,128)S(1)}, f32[4,88,128]{2,1,0:T(8,128)S(1)}, u32[]{:S(2)}, u32[]{:S(2)}) %collective-permute-start.5) | collective-permute-done | bytes 180256 | tf_op jit(solution)/shard_map/ppermute | solution.py:65
  20.0 0.0 collective-permute-start.9
  20.0 1.3 %collective-permute-done.4.refs_7_ = f32[4,88,128]{2,1,0:T(8,128)S(1)} collective-permute-done((f32[4,88,128]{2,1,0:T(8,128)S(1)}, f32[4,88,128]{2,1,0:T(8,128)S(1)}, u32[]{:S(2)}, u32[]{:S(2)}) %collective-permute-start.4) | collective-permute-done | bytes 180256 | tf_op jit(solution)/shard_map/ppermute | solution.py:65
  21.3 0.0 collective-permute-start.8
  21.3 0.1 collective-permute-done.3.refs_6_
  21.4 0.4 %collective-permute-start.7 = (f32[4,88,128]{2,1,0:T(8,128)S(1)}, f32[4,88,128]{2,1,0:T(8,128)S(1)}, u32[]{:S(2)}, u32[]{:S(2)}) collective-permute-start(f32[4,88,128]{2,1,0:T(8,128)S(1)} %collective-permute-done.3.refs_6_), channel_id=1, source_target_pairs={{0,1},{1,0},{2,3},{3,2},{4,5},{5,4},{6,7},{7,6},{8,9},{9,8},{10,11... | collective-permute-start | bytes 540680 | tf_op jit(solution)/shard_map/ppermute | solution.py:65
  21.9 0.0 collective-permute-done.6.refs_9_
  21.9 0.0 collective-permute-done.9.refs_12_
  21.9 0.9 %collective-permute-done.8.refs_11_ = f32[4,88,128]{2,1,0:T(8,128)S(1)} collective-permute-done((f32[4,88,128]{2,1,0:T(8,128)S(1)}, f32[4,88,128]{2,1,0:T(8,128)S(1)}, u32[]{:S(2)}, u32[]{:S(2)}) %collective-permute-start.8) | collective-permute-done | bytes 180256 | tf_op jit(solution)/shard_map/ppermute | solution.py:65
  22.8 0.3 collective-permute-done.7.refs_10_
  23.0 3.4 %render.1 = (f32[3,1,256]{2,1,0:T(1,128)}, f32[32,4,128]{2,1,0:T(4,128)S(1)}, bf16[256,1024]{1,0:T(8,128)(2,1)S(1)}) custom-call(s32[1]{0:T(128)} %bitcast.me_ref.refs_0_, s32[1,128]{1,0:T(1,128)S(1)} %bitcast.16, bf16[2,512,256]{2,1,0:T(8,128)(2,1)S(1)} %get-tuple-element.23.refs_2_, f32[16,256]{1,0:T(8,128)S(1)} %get-tuple-element.24.refs_3_, ...), custom_call_target="tpu_custom_call" | custom-call | tf_op jit(solution)/shard_map/render/pallas_call | solution.py:432
  26.4 0.0 copy-start
  26.4 0.0 copy-start.1
  26.4 10.8 %all_to_all.5 = f32[32,4,128]{2,1,0:T(4,128)S(1)} all-to-all(f32[32,4,128]{2,1,0:T(4,128)S(1)} %get-tuple-element.28), channel_id=1, replica_groups=mesh['dev'=32] {'dev'}, dimensions={0} | all-to-all | bytes 131072 | tf_op jit(solution)/shard_map/all_to_all | solution.py:463
  37.2 0.0 copy-done.2
  37.2 0.0 copy-done
  37.2 0.0 copy-done.1
  37.2 1.1 %update.1 = (f32[9,1024]{1,0:T(8,128)}, f32[9,1024]{1,0:T(8,128)}, f32[9,1024]{1,0:T(8,128)}) custom-call(f32[128,128]{1,0:T(8,128)S(1)} %bitcast.9, bf16[512,128]{1,0:T(8,128)(2,1)S(1)} %get-tuple-element.29.back, bf16[256,1024]{1,0:T(8,128)(2,1)S(1)} %get-tuple-element.30.hot, f32[9,1024]{1,0:T(8,128)S(1)} %copy-done, f32[9,1024]{1,0:T(8,128)S(1)} %copy-done.1, ...), custom_call_target="tpu_custom_call" | custom-call | tf_op jit(solution)/shard_map/update/pallas_call | solution.py:465
  (4 shorter events, 0.0 us)
Async XLA Ops:
  1.6 7.2 %collective-permute-start.2 = (f32[1,88,128]{2,1,0:T(8,128)S(1)}, f32[1,88,128]{2,1,0:T(8,128)S(1)}, u32[]{:S(2)}, u32[]{:S(2)}) collective-permute-start(f32[1,88,128]{2,1,0:T(8,128)S(1)} %bitcast.10), channel_id=1, source_target_pairs={{0,24},{1,25},{2,26},{3,27},{4,28},{5,29},{6,30},{7,31},{8,16},{9,... | collective-permute-start | bytes 135176 | tf_op jit(solution)/shard_map/ppermute | solution.py:65
  6.7 4.9 %collective-permute-start.1 = (f32[1,88,128]{2,1,0:T(8,128)S(1)}, f32[1,88,128]{2,1,0:T(8,128)S(1)}, u32[]{:S(2)}, u32[]{:S(2)}) collective-permute-start(f32[1,88,128]{2,1,0:T(8,128)S(1)} %bitcast.11), channel_id=1, source_target_pairs={{0,16},{1,17},{2,18},{3,19},{4,20},{5,21},{6,22},{7,23},{8,24},{9,... | collective-permute-start | bytes 135176 | tf_op jit(solution)/shard_map/ppermute | solution.py:65
  6.7 4.9 %collective-permute-start = (f32[1,88,128]{2,1,0:T(8,128)S(1)}, f32[1,88,128]{2,1,0:T(8,128)S(1)}, u32[]{:S(2)}, u32[]{:S(2)}) collective-permute-start(f32[1,88,128]{2,1,0:T(8,128)S(1)} %bitcast.12), channel_id=1, source_target_pairs={{0,8},{1,9},{2,10},{3,11},{4,12},{5,13},{6,14},{7,15},{8,0},{9,1},... | collective-permute-start | bytes 135176 | tf_op jit(solution)/shard_map/ppermute | solution.py:65
  7.3 0.7 %copy-start.3 = (f32[1,3,256]{2,0,1:T(1,128)S(1)}, f32[1,3,256]{2,0,1:T(1,128)}, u32[]{:S(2)}) copy-start(f32[1,3,256]{2,0,1:T(1,128)} %param.15) | copy-start | bytes 9220
  7.3 0.7 %copy-start.4 = (s32[128]{0:T(128)S(1)}, s32[128]{0:T(128)}, u32[]{:S(2)}) copy-start(s32[128]{0:T(128)} %param.14) | copy-start | bytes 1540
  11.6 8.4 %collective-permute-start.5 = (f32[4,88,128]{2,1,0:T(8,128)S(1)}, f32[4,88,128]{2,1,0:T(8,128)S(1)}, u32[]{:S(2)}, u32[]{:S(2)}) collective-permute-start(f32[4,88,128]{2,1,0:T(8,128)S(1)} %pad_maximum_fusion.refs_5_), channel_id=1, source_target_pairs={{0,6},{1,7},{2,4},{3,5},{4,2},{5,3},{6,0},{7,1},{8,14},{9,15},{10,... | collective-permute-start | bytes 540680 | tf_op jit(solution)/shard_map/ppermute | solution.py:65
  14.2 7.2 %collective-permute-start.4 = (f32[4,88,128]{2,1,0:T(8,128)S(1)}, f32[4,88,128]{2,1,0:T(8,128)S(1)}, u32[]{:S(2)}, u32[]{:S(2)}) collective-permute-start(f32[4,88,128]{2,1,0:T(8,128)S(1)} %pad_maximum_fusion.refs_5_), channel_id=1, source_target_pairs={{0,4},{1,5},{2,6},{3,7},{4,0},{5,1},{6,2},{7,3},{8,12},{9,13},{10,... | collective-permute-start | bytes 540680 | tf_op jit(solution)/shard_map/ppermute | solution.py:65
  14.7 6.8 %collective-permute-start.3 = (f32[4,88,128]{2,1,0:T(8,128)S(1)}, f32[4,88,128]{2,1,0:T(8,128)S(1)}, u32[]{:S(2)}, u32[]{:S(2)}) collective-permute-start(f32[4,88,128]{2,1,0:T(8,128)S(1)} %pad_maximum_fusion.refs_5_), channel_id=1, source_target_pairs={{0,2},{1,3},{2,0},{3,1},{4,6},{5,7},{6,4},{7,5},{8,10},{9,11},{10,... | collective-permute-start | bytes 540680 | tf_op jit(solution)/shard_map/ppermute | solution.py:65
  15.2 6.7 %collective-permute-start.6 = (f32[4,88,128]{2,1,0:T(8,128)S(1)}, f32[4,88,128]{2,1,0:T(8,128)S(1)}, u32[]{:S(2)}, u32[]{:S(2)}) collective-permute-start(f32[4,88,128]{2,1,0:T(8,128)S(1)} %pad_maximum_fusion.refs_5_), channel_id=1, source_target_pairs={{0,1},{1,0},{2,3},{3,2},{4,5},{5,4},{6,7},{7,6},{8,9},{9,8},{10,11... | collective-permute-start | bytes 540680 | tf_op jit(solution)/shard_map/ppermute | solution.py:65
  20.0 1.8 %collective-permute-start.9 = (f32[4,88,128]{2,1,0:T(8,128)S(1)}, f32[4,88,128]{2,1,0:T(8,128)S(1)}, u32[]{:S(2)}, u32[]{:S(2)}) collective-permute-start(f32[4,88,128]{2,1,0:T(8,128)S(1)} %collective-permute-done.5.refs_8_), channel_id=1, source_target_pairs={{0,1},{1,0},{2,3},{3,2},{4,5},{5,4},{6,7},{7,6},{8,9},{9,8},{10,11... | collective-permute-start | bytes 540680 | tf_op jit(solution)/shard_map/ppermute | solution.py:65
  21.3 1.4 %collective-permute-start.8 = (f32[4,88,128]{2,1,0:T(8,128)S(1)}, f32[4,88,128]{2,1,0:T(8,128)S(1)}, u32[]{:S(2)}, u32[]{:S(2)}) collective-permute-start(f32[4,88,128]{2,1,0:T(8,128)S(1)} %collective-permute-done.4.refs_7_), channel_id=1, source_target_pairs={{0,1},{1,0},{2,3},{3,2},{4,5},{5,4},{6,7},{7,6},{8,9},{9,8},{10,11... | collective-permute-start | bytes 540680 | tf_op jit(solution)/shard_map/ppermute | solution.py:65
  21.4 1.6 %collective-permute-start.7 = (f32[4,88,128]{2,1,0:T(8,128)S(1)}, f32[4,88,128]{2,1,0:T(8,128)S(1)}, u32[]{:S(2)}, u32[]{:S(2)}) collective-permute-start(f32[4,88,128]{2,1,0:T(8,128)S(1)} %collective-permute-done.3.refs_6_), channel_id=1, source_target_pairs={{0,1},{1,0},{2,3},{3,2},{4,5},{5,4},{6,7},{7,6},{8,9},{9,8},{10,11... | collective-permute-start | bytes 540680 | tf_op jit(solution)/shard_map/ppermute | solution.py:65
  23.0 14.2 %copy-start.2 = (f32[9,1024]{1,0:T(8,128)S(1)}, f32[9,1024]{1,0:T(8,128)}, u32[]{:S(2)}) copy-start(f32[9,1024]{1,0:T(8,128)} %second.1) | copy-start | bytes 110596
  26.4 10.8 %copy-start = (f32[9,1024]{1,0:T(8,128)S(1)}, f32[9,1024]{1,0:T(8,128)}, u32[]{:S(2)}) copy-start(f32[9,1024]{1,0:T(8,128)} %params.1) | copy-start | bytes 110596
  26.4 10.8 %copy-start.1 = (f32[9,1024]{1,0:T(8,128)S(1)}, f32[9,1024]{1,0:T(8,128)}, u32[]{:S(2)}) copy-start(f32[9,1024]{1,0:T(8,128)} %moment.1) | copy-start | bytes 110596

commit v5 on v4

--- a/solution.py
+++ b/solution.py
@@ -60,17 +60,36 @@
     return sum(((pos >> place) & ((1 << bits) - 1)) << bit for bit, bits, place in stages(ndev))
 
 
-def gather_blocks(block, ndev, beside):
+def gather_blocks(block, ndev, main, beside):
     def pull(x, change):
         return lax.ppermute(x, "dev", [(d, d ^ change) for d in range(ndev)])
 
-    held, steps = [block[None]], stages(ndev)
+    held, steps = [block], stages(ndev)
     for number, (bit, bits, _) in enumerate(steps[:-1]):
-        whole = held[0] if len(held) == 1 else jnp.concatenate(held, 0)
+        whole = block
         if number == 1:
-            whole, beside = lax.optimization_barrier((whole, beside))
+            held[-1], beside = lax.optimization_barrier((held[-1], beside))
+            whole = pl.pallas_call(
+                functools.partial(stack_kernel, main),
+                out_shape=jax.ShapeDtypeStruct((len(held) * block.shape[0], LANES), F32),
+                in_specs=[VMEM] * len(held),
+                out_specs=VMEM,
+                compiler_params=PARAMS,
+                name="stack",
+            )(*held)
+        elif number:
+            whole = jnp.concatenate(held, 0)
         held = [whole] + [pull(whole, change << bit) for change in range(1, 1 << bits)]
     return held + [pull(x, 1) for x in held], beside
+
+
+def stack_kernel(main, *refs):
+    *blocks, out = refs
+    rows = blocks[0].shape[0]
+    for i, block in enumerate(blocks):
+        out[i * main : (i + 1) * main, :] = block[:main, :]
+        at = len(blocks) * main + i * (rows - main)
+        out[at : at + rows - main, :] = block[main:, :]
 
 
 def pick(source, lanes):
@@ -88,12 +107,12 @@
     return blocks[0]
 
 
-def pack_kernel(count_in, seg_in, fetch_in, params_in, out, count, seg, fetch, params, sems):
+def pack_kernel(count_in, seg_in, fetch_in, params_in, out, count, seg, short, fetch, params, sems):
     segs, span = seg.shape
     nparam, owned = params.shape
     chunks, halves = owned // LANES, span // LANES
     lane = iota((1, LANES), 1)
-    pairs = ((params_in, params), (seg_in, seg), (fetch_in, fetch), (count_in, count))
+    pairs = ((params_in, params), (seg_in, seg), (fetch_in, short), (count_in, count))
     copies = [pltpu.make_async_copy(a, b, sems.at[i]) for i, (a, b) in enumerate(pairs)]
     for copy in copies:
         copy.start()
@@ -108,8 +127,18 @@
             row = jnp.where(lane + h * LANES < count[s], seg[s : s + 1, h * LANES : (h + 1) * LANES], -1)
             out[at : at + 1, :] = row.astype(F32)
             at += 1
-    out[at : at + SUB, :] = jnp.zeros((SUB, LANES), F32)
-    out[at : at + SUB, : fetch.shape[1]] = fetch[...].astype(F32)
+    ndev = fetch_in.shape[1]
+    rows = SUB * ndev // LANES
+    if ndev == LANES:
+        out[at : at + SUB, :] = short[...].astype(F32)
+        return
+    fetch[...] = jnp.zeros(fetch.shape, F32)
+    fetch[:, :ndev] = short[...].astype(F32)
+    lane, sub = iota((SUB, LANES), 1), iota((SUB, LANES), 0)
+    wide = pick(fetch[...], lane & (ndev - 1))
+    for r in range(rows):
+        own = jnp.where(sub == r * (SUB // rows) + lane // ndev, wide, 0.0)
+        out[at + r : at + r + 1, :] = jnp.sum(own, 0, keepdims=True)
 
 
 def layout_kernel(me_ref, perm, target, tri, goal, goal_cols, back):
@@ -152,7 +181,9 @@
     arrays = refs[5 : 5 + narr]
     image, grads, asked = refs[5 + narr : 8 + narr]
     (column, ids, lists, idrows, table, hots, coef, alpha, trans, logs, weights, colours, backs, dys, dpar, gback, flat) = refs[8 + narr :]
-    per = arrays[0].shape[0]
+    main, tail = nparam * chunks + SUB, SUB * ndev // LANES
+    unit = 4 * (main + tail)
+    per = arrays[0].shape[0] * 4 // unit
     slots = ndev * cap
     quarter = slots // 2
     pixels = SIDE * SIDE
@@ -162,33 +193,37 @@
     base = nparam * chunks
 
     def block(j):
-        return arrays[j // per], j % per
+        return arrays[j // per], j % per // 4 * unit + j % 4 * main
 
     for j in range(ndev):
         ref, at = block(j)
-        idrows[j] = ref[at, base : base + 2 * SUB, :]
+        idrows[j, :SUB, :] = ref[at + base : at + base + SUB, :]
+        at = j % per // 4 * unit + 4 * main + j % 4 * tail
+        idrows[j, SUB : SUB + tail, :] = ref[at : at + tail, :]
     fetched = []
     places = (iota(perm.shape, 0) * LANES + iota(perm.shape, 1)).astype(F32)
     for q in range(KSEG):
         slot = jnp.sum(jnp.where(perm[...] == me * KSEG + q, places, 0.0)).astype(jnp.int32)
         j = position(ndev, (slot >> 2) ^ me)
-        fetched.append(idrows[j, SUB : 2 * SUB, :])
+        fetched.append([jnp.broadcast_to(idrows[j, SUB + r : SUB + r + 1, :], (SUB, LANES)) for r in range(tail)])
         for h in range(halves):
             lists[q * halves + h : q * halves + h + 1, :] = idrows[j, pl.ds((slot & 3) * halves + h, 1), :]
     sub, lane = iota((SUB, LANES), 0), iota((SUB, LANES), 1)
     low_bits = cap.bit_length() - 1
     rank, which = (lane >> low_bits) & (KSEG - 1), lane >> (low_bits + 2)
+    kth, share = lane & (cap - 1), SUB // tail
     extra = []
     for g in range(ndev // 4):
         offs = [offset_at(ndev, 4 * g + b) for b in range(4)]
         off = jnp.where(which == 0, offs[0], jnp.where(which == 1, offs[1], jnp.where(which == 2, offs[2], offs[3])))
         owner = off ^ me
         found = jnp.zeros((SUB, LANES), F32)
-        for q in range(KSEG):
-            found = jnp.where(rank == q, pick(fetched[q], owner), found)
-        found = jnp.where(sub == lane & (cap - 1), found, 0.0)
-        for step in (4, 2, 1):
-            found = found + pltpu.roll(found, step, 0)
+        source = (kth & (share - 1)) * ndev + owner
+        for r in range(tail):
+            here = jnp.zeros((SUB, LANES), F32)
+            for q in range(KSEG):
+                here = jnp.where(rank == q, pick(fetched[q][r], source), here)
+            found = jnp.where(kth // share == r, here, found)
         local = found.astype(jnp.int32)
         inside, chunk = local & (LANES - 1), local >> 7
         got = []
@@ -196,7 +231,7 @@
             value = jnp.zeros((SUB, LANES), F32)
             for b in range(4):
                 ref, at = block(4 * g + b)
-                value = jnp.where(which == b, pick(ref[at, p * chunks : (p + 1) * chunks, :], inside), value)
+                value = jnp.where(which == b, pick(ref[at + p * chunks : at + (p + 1) * chunks, :], inside), value)
             got.append(jnp.where(sub == chunk, value, 0.0))
         table[g] = sum_rows(got[:SUB])
         last = got[SUB]
@@ -295,9 +330,12 @@
         image[c] = shot[c : c + 1, :]
     er_both = jnp.concatenate(split2(shot - goal[...]), 0)
     for j in range(ndev):
-        column[4 * j : 4 * j + 4, :] = idrows[j, SUB : SUB + 4, :]
-        column[quarter + 4 * j : quarter + 4 * j + 4, :] = idrows[j, SUB + 4 : 2 * SUB, :]
-    mine = iota(column.shape, 1) == me
+        for k in range(cap):
+            row = k // 4 * quarter + 4 * j + k % 4
+            column[row : row + 1, :] = idrows[j, SUB + k // share : SUB + k // share + 1, :]
+    line = iota(column.shape, 0)
+    spot_k = jnp.where(line < quarter, 0, 4) + (line & 3)
+    mine = iota(column.shape, 1) == (spot_k & (share - 1)) * ndev + me
     wanted = jnp.sum(jnp.where(mine, column[...], 0.0), 1, keepdims=True).astype(jnp.int32)
     for c in range(chunks):
         cols = iota(column.shape, 1) + c * LANES
@@ -401,13 +439,14 @@
 
     packed = pl.pallas_call(
         pack_kernel,
-        out_shape=jax.ShapeDtypeStruct((base + 2 * SUB, LANES), F32),
+        out_shape=jax.ShapeDtypeStruct((base + SUB + slots // LANES, LANES), F32),
         in_specs=[HBM] * 4,
         out_specs=VMEM,
         scratch_shapes=[
             pltpu.SMEM(seg_count.shape, jnp.int32),
             pltpu.VMEM(seg_ids.shape, jnp.int32),
             pltpu.VMEM((cap, ndev), jnp.int32),
+            pltpu.VMEM((cap, LANES), F32),
             pltpu.VMEM(params.shape, F32),
             pltpu.SemaphoreType.DMA((4,)),
         ],
@@ -428,7 +467,7 @@
         cost_estimate=pl.CostEstimate(flops=0, bytes_accessed=4 * 2**20, transcendentals=0),
         name="layout",
     )(me, perm, target.transpose(1, 0, 2))
-    blocks, (tri, goal, goal_cols, back) = gather_blocks(packed, ndev, (tri, goal, goal_cols, back))
+    blocks, (tri, goal, goal_cols, back) = gather_blocks(packed, ndev, base + SUB, (tri, goal, goal_cols, back))
     image, grads, hot = pl.pallas_call(
         functools.partial(render_kernel, segs, cap, nparam, chunks, ndev),
         out_shape=(

time: 38.6 us -> 38.1 us (0.987)
  waiting for transfers between devices: 10.6 us -> 10.1 us
    ppermute x10, waiting for transfers between devices: 10.6 us -> 10.1 us  [pull(): return lax.ppermute(x, 'dev', [(d, d ^ change) for d in range(ndev)])]
    pallas_call x1 -> x2, Pallas kernels: 0.92 us -> 0.98 us  [the longest x1 0.97 us: per_device(): pl.pallas_call(pack_kernel, out_shape=jax.ShapeDtypeStruct((base + SUB +...]
where the time goes in v5:
time: 38.1 us; the launch traced here: 37.9 us
  blocking collectives  10.8 us (28%)
  waiting for transfers between devices  10.1 us (27%)
  starting transfers between devices  9.77 us (26%)
  Pallas kernels  5.83 us (15%)
  local copies, waits for them, and re-layouts  0.7 us (2%)
  between operations  0.69 us (2%)
    all_to_all x1, blocking collectives, per_device(): lax.all_to_all(grads, 'dev', split_axis=0, concat_axis=0, tiled=True)  10.8 us
    ppermute x10, waiting for transfers between devices, pull(): return lax.ppermute(x, 'dev', [(d, d ^ change) for d in range(ndev)])  10.1 us
    ppermute x10, starting transfers between devices, pull(): return lax.ppermute(x, 'dev', [(d, d ^ change) for d in range(ndev)])  9.77 us
    pallas_call x1, Pallas kernels, per_device(): pl.pallas_call(functools.partial(render_kernel, segs, cap, nparam, chunks...  3.42 us
    pallas_call x1, Pallas kernels, per_device(): pl.pallas_call(update_kernel, out_shape=(new, new, new), in_specs=[VMEM]...  1.1 us
    pallas_call x1, Pallas kernels, per_device(): pl.pallas_call(pack_kernel, out_shape=jax.ShapeDtypeStruct((base + SUB +...  0.97 us
  transfers between devices with their start and end apart: 10, of which 7 were waited for; matrix products, arithmetic and copies ran while one was open for 0% of the time, Pallas kernels for 1%

profile of v5, /device:TPU:0, one launch (start us, length us, event | category | flops | bytes accessed | tf_op | source)
XLA Modules:
  0.0 37.9 jit_solution(7511864605413697406)
XLA Ops:
  0.6 1.0 %pack.1.refs_0_ = f32[82,128]{1,0:T(8,128)S(1)} custom-call(s32[4]{0:T(128)} %count_in.1, s32[4,256]{1,0:T(4,128)} %seg_in.1, s32[8,32]{1,0:T(8,128)} %bitcast.12, f32[9,1024]{1,0:T(8,128)} %params.1), custom_call_target="tpu_custom_call" | custom-call | tf_op jit(solution)/shard_map/pack/pallas_call | solution.py:440
  1.6 5.1 %collective-permute-start = (f32[82,128]{1,0:T(8,128)S(1)}, f32[82,128]{1,0:T(8,128)S(1)}, u32[]{:S(2)}, u32[]{:S(2)}) collective-permute-start(f32[82,128]{1,0:T(8,128)S(1)} %pack.1.refs_0_), channel_id=1, source_target_pairs={{0,24},{1,25},{2,26},{3,27},{4,28},{5,29},{6,30},{7,31},{8,16},{9,... | collective-permute-start | bytes 125960 | tf_op jit(solution)/shard_map/ppermute | solution.py:65
  6.7 0.0 collective-permute-start.2
  6.7 0.6 %collective-permute-start.1 = (f32[82,128]{1,0:T(8,128)S(1)}, f32[82,128]{1,0:T(8,128)S(1)}, u32[]{:S(2)}, u32[]{:S(2)}) collective-permute-start(f32[82,128]{1,0:T(8,128)S(1)} %pack.1.refs_0_), channel_id=1, source_target_pairs={{0,8},{1,9},{2,10},{3,11},{4,12},{5,13},{6,14},{7,15},{8,0},{9,1},... | collective-permute-start | bytes 125960 | tf_op jit(solution)/shard_map/ppermute | solution.py:65
  7.4 0.7 %copy-done.3 = f32[1,3,256]{2,0,1:T(1,128)S(1)} copy-done((f32[1,3,256]{2,0,1:T(1,128)S(1)}, f32[1,3,256]{2,0,1:T(1,128)}, u32[]{:S(2)}) %copy-start.3) | copy-done | bytes 3096
  8.1 0.0 copy-done.4
  8.1 0.3 layout.1
  8.4 0.4 %collective-permute-done.refs_3_ = f32[82,128]{1,0:T(8,128)S(1)} collective-permute-done((f32[82,128]{1,0:T(8,128)S(1)}, f32[82,128]{1,0:T(8,128)S(1)}, u32[]{:S(2)}, u32[]{:S(2)}) %collective-permute-start) | collective-permute-done | bytes 42016 | tf_op jit(solution)/shard_map/ppermute | solution.py:65
  8.8 2.9 %collective-permute-done.2.refs_2_ = f32[82,128]{1,0:T(8,128)S(1)} collective-permute-done((f32[82,128]{1,0:T(8,128)S(1)}, f32[82,128]{1,0:T(8,128)S(1)}, u32[]{:S(2)}, u32[]{:S(2)}) %collective-permute-start.2) | collective-permute-done | bytes 42016 | tf_op jit(solution)/shard_map/ppermute | solution.py:65
  11.7 0.0 collective-permute-done.1.refs_1_
  11.7 2.5 %collective-permute-start.5 = (f32[328,128]{1,0:T(8,128)S(1)}, f32[328,128]{1,0:T(8,128)S(1)}, u32[]{:S(2)}, u32[]{:S(2)}) collective-permute-start(f32[328,128]{1,0:T(8,128)S(1)} %stack.1.refs_5_), channel_id=1, source_target_pairs={{0,6},{1,7},{2,4},{3,5},{4,2},{5,3},{6,0},{7,1},{8,14},{9,15},{10,... | collective-permute-start | bytes 503816 | tf_op jit(solution)/shard_map/ppermute | solution.py:65
  14.2 0.5 %collective-permute-start.4 = (f32[328,128]{1,0:T(8,128)S(1)}, f32[328,128]{1,0:T(8,128)S(1)}, u32[]{:S(2)}, u32[]{:S(2)}) collective-permute-start(f32[328,128]{1,0:T(8,128)S(1)} %stack.1.refs_5_), channel_id=1, source_target_pairs={{0,4},{1,5},{2,6},{3,7},{4,0},{5,1},{6,2},{7,3},{8,12},{9,13},{10,... | collective-permute-start | bytes 503816 | tf_op jit(solution)/shard_map/ppermute | solution.py:65
  14.7 0.5 %collective-permute-start.3 = (f32[328,128]{1,0:T(8,128)S(1)}, f32[328,128]{1,0:T(8,128)S(1)}, u32[]{:S(2)}, u32[]{:S(2)}) collective-permute-start(f32[328,128]{1,0:T(8,128)S(1)} %stack.1.refs_5_), channel_id=1, source_target_pairs={{0,2},{1,3},{2,0},{3,1},{4,6},{5,7},{6,4},{7,5},{8,10},{9,11},{10,... | collective-permute-start | bytes 503816 | tf_op jit(solution)/shard_map/ppermute | solution.py:65
  15.2 0.0 collective-permute-start.6
  15.2 4.6 %collective-permute-done.5.refs_8_ = f32[328,128]{1,0:T(8,128)S(1)} collective-permute-done((f32[328,128]{1,0:T(8,128)S(1)}, f32[328,128]{1,0:T(8,128)S(1)}, u32[]{:S(2)}, u32[]{:S(2)}) %collective-permute-start.5) | collective-permute-done | bytes 167968 | tf_op jit(solution)/shard_map/ppermute | solution.py:65
  19.8 0.0 collective-permute-start.9
  19.8 1.0 %collective-permute-done.4.refs_7_ = f32[328,128]{1,0:T(8,128)S(1)} collective-permute-done((f32[328,128]{1,0:T(8,128)S(1)}, f32[328,128]{1,0:T(8,128)S(1)}, u32[]{:S(2)}, u32[]{:S(2)}) %collective-permute-start.4) | collective-permute-done | bytes 167968 | tf_op jit(solution)/shard_map/ppermute | solution.py:65
  20.9 0.0 collective-permute-start.8
  20.9 0.1 collective-permute-done.3.refs_6_
  20.9 0.5 %collective-permute-start.7 = (f32[328,128]{1,0:T(8,128)S(1)}, f32[328,128]{1,0:T(8,128)S(1)}, u32[]{:S(2)}, u32[]{:S(2)}) collective-permute-start(f32[328,128]{1,0:T(8,128)S(1)} %collective-permute-done.3.refs_6_), channel_id=1, source_target_pairs={{0,1},{1,0},{2,3},{3,2},{4,5},{5,4},{6,7},{7,6},{8,9},{9,8},{10,11... | collective-permute-start | bytes 503816 | tf_op jit(solution)/shard_map/ppermute | solution.py:65
  21.4 0.0 collective-permute-done.6.refs_9_
  21.4 0.0 collective-permute-done.9.refs_12_
  21.4 0.9 %collective-permute-done.8.refs_11_ = f32[328,128]{1,0:T(8,128)S(1)} collective-permute-done((f32[328,128]{1,0:T(8,128)S(1)}, f32[328,128]{1,0:T(8,128)S(1)}, u32[]{:S(2)}, u32[]{:S(2)}) %collective-permute-start.8) | collective-permute-done | bytes 167968 | tf_op jit(solution)/shard_map/ppermute | solution.py:65
  22.3 0.2 collective-permute-done.7.refs_10_
  22.5 3.4 %render.1 = (f32[3,1,256]{2,1,0:T(1,128)}, f32[32,4,128]{2,1,0:T(4,128)S(1)}, bf16[256,1024]{1,0:T(8,128)(2,1)S(1)}) custom-call(s32[1]{0:T(128)} %bitcast.me_ref.refs_0_, s32[1,128]{1,0:T(1,128)S(1)} %bitcast.11, bf16[2,512,256]{2,1,0:T(8,128)(2,1)S(1)} %get-tuple-element.23.refs_2_, f32[16,256]{1,0:T(8,128)S(1)} %get-tuple-element.24.refs_3_, ...), custom_call_target="tpu_custom_call" | custom-call | tf_op jit(solution)/shard_map/render/pallas_call | solution.py:471
  25.9 0.0 copy-start
  25.9 0.0 copy-start.1
  25.9 10.8 %all_to_all.5 = f32[32,4,128]{2,1,0:T(4,128)S(1)} all-to-all(f32[32,4,128]{2,1,0:T(4,128)S(1)} %get-tuple-element.28), channel_id=1, replica_groups=mesh['dev'=32] {'dev'}, dimensions={0} | all-to-all | bytes 131072 | tf_op jit(solution)/shard_map/all_to_all | solution.py:502
  36.8 0.0 copy-done.2
  36.8 0.0 copy-done
  36.8 0.0 copy-done.1
  36.8 1.1 %update.1 = (f32[9,1024]{1,0:T(8,128)}, f32[9,1024]{1,0:T(8,128)}, f32[9,1024]{1,0:T(8,128)}) custom-call(f32[128,128]{1,0:T(8,128)S(1)} %bitcast.8, bf16[512,128]{1,0:T(8,128)(2,1)S(1)} %get-tuple-element.29.back, bf16[256,1024]{1,0:T(8,128)(2,1)S(1)} %get-tuple-element.30.hot, f32[9,1024]{1,0:T(8,128)S(1)} %copy-done, f32[9,1024]{1,0:T(8,128)S(1)} %copy-done.1, ...), custom_call_target="tpu_custom_call" | custom-call | tf_op jit(solution)/shard_map/update/pallas_call | solution.py:504
  (4 shorter events, 0.0 us)
Async XLA Ops:
  1.6 7.2 %collective-permute-start = (f32[82,128]{1,0:T(8,128)S(1)}, f32[82,128]{1,0:T(8,128)S(1)}, u32[]{:S(2)}, u32[]{:S(2)}) collective-permute-start(f32[82,128]{1,0:T(8,128)S(1)} %pack.1.refs_0_), channel_id=1, source_target_pairs={{0,24},{1,25},{2,26},{3,27},{4,28},{5,29},{6,30},{7,31},{8,16},{9,... | collective-permute-start | bytes 125960 | tf_op jit(solution)/shard_map/ppermute | solution.py:65
  6.7 4.9 %collective-permute-start.2 = (f32[82,128]{1,0:T(8,128)S(1)}, f32[82,128]{1,0:T(8,128)S(1)}, u32[]{:S(2)}, u32[]{:S(2)}) collective-permute-start(f32[82,128]{1,0:T(8,128)S(1)} %pack.1.refs_0_), channel_id=1, source_target_pairs={{0,16},{1,17},{2,18},{3,19},{4,20},{5,21},{6,22},{7,23},{8,24},{9,... | collective-permute-start | bytes 125960 | tf_op jit(solution)/shard_map/ppermute | solution.py:65
  6.7 4.9 %collective-permute-start.1 = (f32[82,128]{1,0:T(8,128)S(1)}, f32[82,128]{1,0:T(8,128)S(1)}, u32[]{:S(2)}, u32[]{:S(2)}) collective-permute-start(f32[82,128]{1,0:T(8,128)S(1)} %pack.1.refs_0_), channel_id=1, source_target_pairs={{0,8},{1,9},{2,10},{3,11},{4,12},{5,13},{6,14},{7,15},{8,0},{9,1},... | collective-permute-start | bytes 125960 | tf_op jit(solution)/shard_map/ppermute | solution.py:65
  7.4 0.7 %copy-start.3 = (f32[1,3,256]{2,0,1:T(1,128)S(1)}, f32[1,3,256]{2,0,1:T(1,128)}, u32[]{:S(2)}) copy-start(f32[1,3,256]{2,0,1:T(1,128)} %param.15) | copy-start | bytes 9220
  7.4 0.7 %copy-start.4 = (s32[128]{0:T(128)S(1)}, s32[128]{0:T(128)}, u32[]{:S(2)}) copy-start(s32[128]{0:T(128)} %param.14) | copy-start | bytes 1540
  11.7 8.1 %collective-permute-start.5 = (f32[328,128]{1,0:T(8,128)S(1)}, f32[328,128]{1,0:T(8,128)S(1)}, u32[]{:S(2)}, u32[]{:S(2)}) collective-permute-start(f32[328,128]{1,0:T(8,128)S(1)} %stack.1.refs_5_), channel_id=1, source_target_pairs={{0,6},{1,7},{2,4},{3,5},{4,2},{5,3},{6,0},{7,1},{8,14},{9,15},{10,... | collective-permute-start | bytes 503816 | tf_op jit(solution)/shard_map/ppermute | solution.py:65
  14.2 6.7 %collective-permute-start.4 = (f32[328,128]{1,0:T(8,128)S(1)}, f32[328,128]{1,0:T(8,128)S(1)}, u32[]{:S(2)}, u32[]{:S(2)}) collective-permute-start(f32[328,128]{1,0:T(8,128)S(1)} %stack.1.refs_5_), channel_id=1, source_target_pairs={{0,4},{1,5},{2,6},{3,7},{4,0},{5,1},{6,2},{7,3},{8,12},{9,13},{10,... | collective-permute-start | bytes 503816 | tf_op jit(solution)/shard_map/ppermute | solution.py:65
  14.7 6.2 %collective-permute-start.3 = (f32[328,128]{1,0:T(8,128)S(1)}, f32[328,128]{1,0:T(8,128)S(1)}, u32[]{:S(2)}, u32[]{:S(2)}) collective-permute-start(f32[328,128]{1,0:T(8,128)S(1)} %stack.1.refs_5_), channel_id=1, source_target_pairs={{0,2},{1,3},{2,0},{3,1},{4,6},{5,7},{6,4},{7,5},{8,10},{9,11},{10,... | collective-permute-start | bytes 503816 | tf_op jit(solution)/shard_map/ppermute | solution.py:65
  15.2 6.1 %collective-permute-start.6 = (f32[328,128]{1,0:T(8,128)S(1)}, f32[328,128]{1,0:T(8,128)S(1)}, u32[]{:S(2)}, u32[]{:S(2)}) collective-permute-start(f32[328,128]{1,0:T(8,128)S(1)} %stack.1.refs_5_), channel_id=1, source_target_pairs={{0,1},{1,0},{2,3},{3,2},{4,5},{5,4},{6,7},{7,6},{8,9},{9,8},{10,11... | collective-permute-start | bytes 503816 | tf_op jit(solution)/shard_map/ppermute | solution.py:65
  19.8 1.6 %collective-permute-start.9 = (f32[328,128]{1,0:T(8,128)S(1)}, f32[328,128]{1,0:T(8,128)S(1)}, u32[]{:S(2)}, u32[]{:S(2)}) collective-permute-start(f32[328,128]{1,0:T(8,128)S(1)} %collective-permute-done.5.refs_8_), channel_id=1, source_target_pairs={{0,1},{1,0},{2,3},{3,2},{4,5},{5,4},{6,7},{7,6},{8,9},{9,8},{10,11... | collective-permute-start | bytes 503816 | tf_op jit(solution)/shard_map/ppermute | solution.py:65
  20.9 1.4 %collective-permute-start.8 = (f32[328,128]{1,0:T(8,128)S(1)}, f32[328,128]{1,0:T(8,128)S(1)}, u32[]{:S(2)}, u32[]{:S(2)}) collective-permute-start(f32[328,128]{1,0:T(8,128)S(1)} %collective-permute-done.4.refs_7_), channel_id=1, source_target_pairs={{0,1},{1,0},{2,3},{3,2},{4,5},{5,4},{6,7},{7,6},{8,9},{9,8},{10,11... | collective-permute-start | bytes 503816 | tf_op jit(solution)/shard_map/ppermute | solution.py:65
  20.9 1.6 %collective-permute-start.7 = (f32[328,128]{1,0:T(8,128)S(1)}, f32[328,128]{1,0:T(8,128)S(1)}, u32[]{:S(2)}, u32[]{:S(2)}) collective-permute-start(f32[328,128]{1,0:T(8,128)S(1)} %collective-permute-done.3.refs_6_), channel_id=1, source_target_pairs={{0,1},{1,0},{2,3},{3,2},{4,5},{5,4},{6,7},{7,6},{8,9},{9,8},{10,11... | collective-permute-start | bytes 503816 | tf_op jit(solution)/shard_map/ppermute | solution.py:65
  22.5 14.3 %copy-start.2 = (f32[9,1024]{1,0:T(8,128)S(1)}, f32[9,1024]{1,0:T(8,128)}, u32[]{:S(2)}) copy-start(f32[9,1024]{1,0:T(8,128)} %second.1) | copy-start | bytes 110596
  25.9 10.8 %copy-start = (f32[9,1024]{1,0:T(8,128)S(1)}, f32[9,1024]{1,0:T(8,128)}, u32[]{:S(2)}) copy-start(f32[9,1024]{1,0:T(8,128)} %params.1) | copy-start | bytes 110596
  25.9 10.8 %copy-start.1 = (f32[9,1024]{1,0:T(8,128)S(1)}, f32[9,1024]{1,0:T(8,128)}, u32[]{:S(2)}) copy-start(f32[9,1024]{1,0:T(8,128)} %moment.1) | copy-start | bytes 110596

commit v6 on v5

--- a/solution.py
+++ b/solution.py
@@ -180,7 +180,7 @@
     narr = 2 << stages(ndev)[-2][1]
     arrays = refs[5 : 5 + narr]
     image, grads, asked = refs[5 + narr : 8 + narr]
-    (column, ids, lists, idrows, table, hots, coef, alpha, trans, logs, weights, colours, backs, dys, dpar, gback, flat) = refs[8 + narr :]
+    (fetched, column, ids, lists, idrows, table, hots, coef, alpha, trans, logs, weights, colours, backs, dys, dpar, gback, flat) = refs[8 + narr :]
     main, tail = nparam * chunks + SUB, SUB * ndev // LANES
     unit = 4 * (main + tail)
     per = arrays[0].shape[0] * 4 // unit
@@ -200,18 +200,18 @@
         idrows[j, :SUB, :] = ref[at + base : at + base + SUB, :]
         at = j % per // 4 * unit + 4 * main + j % 4 * tail
         idrows[j, SUB : SUB + tail, :] = ref[at : at + tail, :]
-    fetched = []
     places = (iota(perm.shape, 0) * LANES + iota(perm.shape, 1)).astype(F32)
     for q in range(KSEG):
         slot = jnp.sum(jnp.where(perm[...] == me * KSEG + q, places, 0.0)).astype(jnp.int32)
         j = position(ndev, (slot >> 2) ^ me)
-        fetched.append([jnp.broadcast_to(idrows[j, SUB + r : SUB + r + 1, :], (SUB, LANES)) for r in range(tail)])
+        fetched[q * tail : (q + 1) * tail, :] = idrows[j, SUB : SUB + tail, :]
         for h in range(halves):
             lists[q * halves + h : q * halves + h + 1, :] = idrows[j, pl.ds((slot & 3) * halves + h, 1), :]
     sub, lane = iota((SUB, LANES), 0), iota((SUB, LANES), 1)
     low_bits = cap.bit_length() - 1
     rank, which = (lane >> low_bits) & (KSEG - 1), lane >> (low_bits + 2)
     kth, share = lane & (cap - 1), SUB // tail
+    asked_row = rank * tail + kth // share
     extra = []
     for g in range(ndev // 4):
         offs = [offset_at(ndev, 4 * g + b) for b in range(4)]
@@ -219,11 +219,11 @@
         owner = off ^ me
         found = jnp.zeros((SUB, LANES), F32)
         source = (kth & (share - 1)) * ndev + owner
-        for r in range(tail):
-            here = jnp.zeros((SUB, LANES), F32)
-            for q in range(KSEG):
-                here = jnp.where(rank == q, pick(fetched[q][r], source), here)
-            found = jnp.where(kth // share == r, here, found)
+        for i in range(KSEG * tail // SUB):
+            here = pick(fetched[i * SUB : (i + 1) * SUB, :], source)
+            found = jnp.where(asked_row == i * SUB + sub, here, found)
+        for step in (4, 2, 1):
+            found = found + pltpu.roll(found, step, 0)
         local = found.astype(jnp.int32)
         inside, chunk = local & (LANES - 1), local >> 7
         got = []
@@ -478,6 +478,7 @@
         in_specs=[SMEM] + [VMEM] * (4 + len(blocks)),
         out_specs=(VMEM, VMEM, VMEM),
         scratch_shapes=[
+            pltpu.VMEM((KSEG * SUB * ndev // LANES, LANES), F32),
             pltpu.VMEM((slots, LANES), F32),
             pltpu.VMEM((SUB, span), F32),
             pltpu.VMEM((SUB, LANES), F32),

time: 38.1 us -> 38.1 us (level)
  no operation moved by 1% of the time
where the time goes in v6:
time: 38.1 us; the launch traced here: 37.8 us
  blocking collectives  10.8 us (28%)
  waiting for transfers between devices  10.1 us (27%)
  starting transfers between devices  9.77 us (26%)
  Pallas kernels  5.79 us (15%)
  local copies, waits for them, and re-layouts  0.7 us (2%)
  between operations  0.69 us (2%)
    all_to_all x1, blocking collectives, per_device(): lax.all_to_all(grads, 'dev', split_axis=0, concat_axis=0, tiled=True)  10.8 us
    ppermute x10, waiting for transfers between devices, pull(): return lax.ppermute(x, 'dev', [(d, d ^ change) for d in range(ndev)])  10.1 us
    ppermute x10, starting transfers between devices, pull(): return lax.ppermute(x, 'dev', [(d, d ^ change) for d in range(ndev)])  9.77 us
    pallas_call x1, Pallas kernels, per_device(): pl.pallas_call(functools.partial(render_kernel, segs, cap, nparam, chunks...  3.37 us
    pallas_call x1, Pallas kernels, per_device(): pl.pallas_call(update_kernel, out_shape=(new, new, new), in_specs=[VMEM]...  1.1 us
    pallas_call x1, Pallas kernels, per_device(): pl.pallas_call(pack_kernel, out_shape=jax.ShapeDtypeStruct((base + SUB +...  0.97 us
  transfers between devices with their start and end apart: 10, of which 7 were waited for; matrix products, arithmetic and copies ran while one was open for 0% of the time, Pallas kernels for 1%

profile of v6, /device:TPU:0, one launch (start us, length us, event | category | flops | bytes accessed | tf_op | source)
XLA Modules:
  0.0 37.8 jit_solution(3943623986164593516)
XLA Ops:
  0.6 1.0 %pack.1.refs_0_ = f32[82,128]{1,0:T(8,128)S(1)} custom-call(s32[4]{0:T(128)} %count_in.1, s32[4,256]{1,0:T(4,128)} %seg_in.1, s32[8,32]{1,0:T(8,128)} %bitcast.12, f32[9,1024]{1,0:T(8,128)} %params.1), custom_call_target="tpu_custom_call" | custom-call | tf_op jit(solution)/shard_map/pack/pallas_call | solution.py:440
  1.6 5.1 %collective-permute-start = (f32[82,128]{1,0:T(8,128)S(1)}, f32[82,128]{1,0:T(8,128)S(1)}, u32[]{:S(2)}, u32[]{:S(2)}) collective-permute-start(f32[82,128]{1,0:T(8,128)S(1)} %pack.1.refs_0_), channel_id=1, source_target_pairs={{0,24},{1,25},{2,26},{3,27},{4,28},{5,29},{6,30},{7,31},{8,16},{9,... | collective-permute-start | bytes 125960 | tf_op jit(solution)/shard_map/ppermute | solution.py:65
  6.7 0.0 collective-permute-start.2
  6.7 0.6 %collective-permute-start.1 = (f32[82,128]{1,0:T(8,128)S(1)}, f32[82,128]{1,0:T(8,128)S(1)}, u32[]{:S(2)}, u32[]{:S(2)}) collective-permute-start(f32[82,128]{1,0:T(8,128)S(1)} %pack.1.refs_0_), channel_id=1, source_target_pairs={{0,8},{1,9},{2,10},{3,11},{4,12},{5,13},{6,14},{7,15},{8,0},{9,1},... | collective-permute-start | bytes 125960 | tf_op jit(solution)/shard_map/ppermute | solution.py:65
  7.4 0.7 %copy-done.3 = f32[1,3,256]{2,0,1:T(1,128)S(1)} copy-done((f32[1,3,256]{2,0,1:T(1,128)S(1)}, f32[1,3,256]{2,0,1:T(1,128)}, u32[]{:S(2)}) %copy-start.3) | copy-done | bytes 3096
  8.1 0.0 copy-done.4
  8.1 0.3 layout.1
  8.4 0.4 %collective-permute-done.refs_3_ = f32[82,128]{1,0:T(8,128)S(1)} collective-permute-done((f32[82,128]{1,0:T(8,128)S(1)}, f32[82,128]{1,0:T(8,128)S(1)}, u32[]{:S(2)}, u32[]{:S(2)}) %collective-permute-start) | collective-permute-done | bytes 42016 | tf_op jit(solution)/shard_map/ppermute | solution.py:65
  8.8 2.9 %collective-permute-done.2.refs_2_ = f32[82,128]{1,0:T(8,128)S(1)} collective-permute-done((f32[82,128]{1,0:T(8,128)S(1)}, f32[82,128]{1,0:T(8,128)S(1)}, u32[]{:S(2)}, u32[]{:S(2)}) %collective-permute-start.2) | collective-permute-done | bytes 42016 | tf_op jit(solution)/shard_map/ppermute | solution.py:65
  11.7 0.0 collective-permute-done.1.refs_1_
  11.7 2.5 %collective-permute-start.5 = (f32[328,128]{1,0:T(8,128)S(1)}, f32[328,128]{1,0:T(8,128)S(1)}, u32[]{:S(2)}, u32[]{:S(2)}) collective-permute-start(f32[328,128]{1,0:T(8,128)S(1)} %stack.1.refs_5_), channel_id=1, source_target_pairs={{0,6},{1,7},{2,4},{3,5},{4,2},{5,3},{6,0},{7,1},{8,14},{9,15},{10,... | collective-permute-start | bytes 503816 | tf_op jit(solution)/shard_map/ppermute | solution.py:65
  14.2 0.5 %collective-permute-start.4 = (f32[328,128]{1,0:T(8,128)S(1)}, f32[328,128]{1,0:T(8,128)S(1)}, u32[]{:S(2)}, u32[]{:S(2)}) collective-permute-start(f32[328,128]{1,0:T(8,128)S(1)} %stack.1.refs_5_), channel_id=1, source_target_pairs={{0,4},{1,5},{2,6},{3,7},{4,0},{5,1},{6,2},{7,3},{8,12},{9,13},{10,... | collective-permute-start | bytes 503816 | tf_op jit(solution)/shard_map/ppermute | solution.py:65
  14.7 0.5 %collective-permute-start.3 = (f32[328,128]{1,0:T(8,128)S(1)}, f32[328,128]{1,0:T(8,128)S(1)}, u32[]{:S(2)}, u32[]{:S(2)}) collective-permute-start(f32[328,128]{1,0:T(8,128)S(1)} %stack.1.refs_5_), channel_id=1, source_target_pairs={{0,2},{1,3},{2,0},{3,1},{4,6},{5,7},{6,4},{7,5},{8,10},{9,11},{10,... | collective-permute-start | bytes 503816 | tf_op jit(solution)/shard_map/ppermute | solution.py:65
  15.2 0.0 collective-permute-start.6
  15.2 4.6 %collective-permute-done.5.refs_8_ = f32[328,128]{1,0:T(8,128)S(1)} collective-permute-done((f32[328,128]{1,0:T(8,128)S(1)}, f32[328,128]{1,0:T(8,128)S(1)}, u32[]{:S(2)}, u32[]{:S(2)}) %collective-permute-start.5) | collective-permute-done | bytes 167968 | tf_op jit(solution)/shard_map/ppermute | solution.py:65
  19.8 0.0 collective-permute-start.9
  19.8 1.0 %collective-permute-done.4.refs_7_ = f32[328,128]{1,0:T(8,128)S(1)} collective-permute-done((f32[328,128]{1,0:T(8,128)S(1)}, f32[328,128]{1,0:T(8,128)S(1)}, u32[]{:S(2)}, u32[]{:S(2)}) %collective-permute-start.4) | collective-permute-done | bytes 167968 | tf_op jit(solution)/shard_map/ppermute | solution.py:65
  20.9 0.0 collective-permute-start.8
  20.9 0.1 collective-permute-done.3.refs_6_
  20.9 0.5 %collective-permute-start.7 = (f32[328,128]{1,0:T(8,128)S(1)}, f32[328,128]{1,0:T(8,128)S(1)}, u32[]{:S(2)}, u32[]{:S(2)}) collective-permute-start(f32[328,128]{1,0:T(8,128)S(1)} %collective-permute-done.3.refs_6_), channel_id=1, source_target_pairs={{0,1},{1,0},{2,3},{3,2},{4,5},{5,4},{6,7},{7,6},{8,9},{9,8},{10,11... | collective-permute-start | bytes 503816 | tf_op jit(solution)/shard_map/ppermute | solution.py:65
  21.4 0.0 collective-permute-done.6.refs_9_
  21.4 0.0 collective-permute-done.9.refs_12_
  21.4 0.9 %collective-permute-done.8.refs_11_ = f32[328,128]{1,0:T(8,128)S(1)} collective-permute-done((f32[328,128]{1,0:T(8,128)S(1)}, f32[328,128]{1,0:T(8,128)S(1)}, u32[]{:S(2)}, u32[]{:S(2)}) %collective-permute-start.8) | collective-permute-done | bytes 167968 | tf_op jit(solution)/shard_map/ppermute | solution.py:65
  22.3 0.2 collective-permute-done.7.refs_10_
  22.5 3.4 %render.1 = (f32[3,1,256]{2,1,0:T(1,128)}, f32[32,4,128]{2,1,0:T(4,128)S(1)}, bf16[256,1024]{1,0:T(8,128)(2,1)S(1)}) custom-call(s32[1]{0:T(128)} %bitcast.me_ref.refs_0_, s32[1,128]{1,0:T(1,128)S(1)} %bitcast.11, bf16[2,512,256]{2,1,0:T(8,128)(2,1)S(1)} %get-tuple-element.23.refs_2_, f32[16,256]{1,0:T(8,128)S(1)} %get-tuple-element.24.refs_3_, ...), custom_call_target="tpu_custom_call" | custom-call | tf_op jit(solution)/shard_map/render/pallas_call | solution.py:471
  25.9 0.0 copy-start
  25.9 0.0 copy-start.1
  25.9 10.8 %all_to_all.5 = f32[32,4,128]{2,1,0:T(4,128)S(1)} all-to-all(f32[32,4,128]{2,1,0:T(4,128)S(1)} %get-tuple-element.28), channel_id=1, replica_groups=mesh['dev'=32] {'dev'}, dimensions={0} | all-to-all | bytes 131072 | tf_op jit(solution)/shard_map/all_to_all | solution.py:503
  36.7 0.0 copy-done.2
  36.7 0.0 copy-done
  36.7 0.0 copy-done.1
  36.7 1.1 %update.1 = (f32[9,1024]{1,0:T(8,128)}, f32[9,1024]{1,0:T(8,128)}, f32[9,1024]{1,0:T(8,128)}) custom-call(f32[128,128]{1,0:T(8,128)S(1)} %bitcast.8, bf16[512,128]{1,0:T(8,128)(2,1)S(1)} %get-tuple-element.29.back, bf16[256,1024]{1,0:T(8,128)(2,1)S(1)} %get-tuple-element.30.hot, f32[9,1024]{1,0:T(8,128)S(1)} %copy-done, f32[9,1024]{1,0:T(8,128)S(1)} %copy-done.1, ...), custom_call_target="tpu_custom_call" | custom-call | tf_op jit(solution)/shard_map/update/pallas_call | solution.py:505
  (4 shorter events, 0.0 us)
Async XLA Ops:
  1.6 7.2 %collective-permute-start = (f32[82,128]{1,0:T(8,128)S(1)}, f32[82,128]{1,0:T(8,128)S(1)}, u32[]{:S(2)}, u32[]{:S(2)}) collective-permute-start(f32[82,128]{1,0:T(8,128)S(1)} %pack.1.refs_0_), channel_id=1, source_target_pairs={{0,24},{1,25},{2,26},{3,27},{4,28},{5,29},{6,30},{7,31},{8,16},{9,... | collective-permute-start | bytes 125960 | tf_op jit(solution)/shard_map/ppermute | solution.py:65
  6.7 4.9 %collective-permute-start.2 = (f32[82,128]{1,0:T(8,128)S(1)}, f32[82,128]{1,0:T(8,128)S(1)}, u32[]{:S(2)}, u32[]{:S(2)}) collective-permute-start(f32[82,128]{1,0:T(8,128)S(1)} %pack.1.refs_0_), channel_id=1, source_target_pairs={{0,16},{1,17},{2,18},{3,19},{4,20},{5,21},{6,22},{7,23},{8,24},{9,... | collective-permute-start | bytes 125960 | tf_op jit(solution)/shard_map/ppermute | solution.py:65
  6.7 4.9 %collective-permute-start.1 = (f32[82,128]{1,0:T(8,128)S(1)}, f32[82,128]{1,0:T(8,128)S(1)}, u32[]{:S(2)}, u32[]{:S(2)}) collective-permute-start(f32[82,128]{1,0:T(8,128)S(1)} %pack.1.refs_0_), channel_id=1, source_target_pairs={{0,8},{1,9},{2,10},{3,11},{4,12},{5,13},{6,14},{7,15},{8,0},{9,1},... | collective-permute-start | bytes 125960 | tf_op jit(solution)/shard_map/ppermute | solution.py:65
  7.4 0.7 %copy-start.3 = (f32[1,3,256]{2,0,1:T(1,128)S(1)}, f32[1,3,256]{2,0,1:T(1,128)}, u32[]{:S(2)}) copy-start(f32[1,3,256]{2,0,1:T(1,128)} %param.15) | copy-start | bytes 9220
  7.4 0.7 %copy-start.4 = (s32[128]{0:T(128)S(1)}, s32[128]{0:T(128)}, u32[]{:S(2)}) copy-start(s32[128]{0:T(128)} %param.14) | copy-start | bytes 1540
  11.7 8.1 %collective-permute-start.5 = (f32[328,128]{1,0:T(8,128)S(1)}, f32[328,128]{1,0:T(8,128)S(1)}, u32[]{:S(2)}, u32[]{:S(2)}) collective-permute-start(f32[328,128]{1,0:T(8,128)S(1)} %stack.1.refs_5_), channel_id=1, source_target_pairs={{0,6},{1,7},{2,4},{3,5},{4,2},{5,3},{6,0},{7,1},{8,14},{9,15},{10,... | collective-permute-start | bytes 503816 | tf_op jit(solution)/shard_map/ppermute | solution.py:65
  14.2 6.7 %collective-permute-start.4 = (f32[328,128]{1,0:T(8,128)S(1)}, f32[328,128]{1,0:T(8,128)S(1)}, u32[]{:S(2)}, u32[]{:S(2)}) collective-permute-start(f32[328,128]{1,0:T(8,128)S(1)} %stack.1.refs_5_), channel_id=1, source_target_pairs={{0,4},{1,5},{2,6},{3,7},{4,0},{5,1},{6,2},{7,3},{8,12},{9,13},{10,... | collective-permute-start | bytes 503816 | tf_op jit(solution)/shard_map/ppermute | solution.py:65
  14.7 6.2 %collective-permute-start.3 = (f32[328,128]{1,0:T(8,128)S(1)}, f32[328,128]{1,0:T(8,128)S(1)}, u32[]{:S(2)}, u32[]{:S(2)}) collective-permute-start(f32[328,128]{1,0:T(8,128)S(1)} %stack.1.refs_5_), channel_id=1, source_target_pairs={{0,2},{1,3},{2,0},{3,1},{4,6},{5,7},{6,4},{7,5},{8,10},{9,11},{10,... | collective-permute-start | bytes 503816 | tf_op jit(solution)/shard_map/ppermute | solution.py:65
  15.2 6.1 %collective-permute-start.6 = (f32[328,128]{1,0:T(8,128)S(1)}, f32[328,128]{1,0:T(8,128)S(1)}, u32[]{:S(2)}, u32[]{:S(2)}) collective-permute-start(f32[328,128]{1,0:T(8,128)S(1)} %stack.1.refs_5_), channel_id=1, source_target_pairs={{0,1},{1,0},{2,3},{3,2},{4,5},{5,4},{6,7},{7,6},{8,9},{9,8},{10,11... | collective-permute-start | bytes 503816 | tf_op jit(solution)/shard_map/ppermute | solution.py:65
  19.8 1.6 %collective-permute-start.9 = (f32[328,128]{1,0:T(8,128)S(1)}, f32[328,128]{1,0:T(8,128)S(1)}, u32[]{:S(2)}, u32[]{:S(2)}) collective-permute-start(f32[328,128]{1,0:T(8,128)S(1)} %collective-permute-done.5.refs_8_), channel_id=1, source_target_pairs={{0,1},{1,0},{2,3},{3,2},{4,5},{5,4},{6,7},{7,6},{8,9},{9,8},{10,11... | collective-permute-start | bytes 503816 | tf_op jit(solution)/shard_map/ppermute | solution.py:65
  20.9 1.4 %collective-permute-start.8 = (f32[328,128]{1,0:T(8,128)S(1)}, f32[328,128]{1,0:T(8,128)S(1)}, u32[]{:S(2)}, u32[]{:S(2)}) collective-permute-start(f32[328,128]{1,0:T(8,128)S(1)} %collective-permute-done.4.refs_7_), channel_id=1, source_target_pairs={{0,1},{1,0},{2,3},{3,2},{4,5},{5,4},{6,7},{7,6},{8,9},{9,8},{10,11... | collective-permute-start | bytes 503816 | tf_op jit(solution)/shard_map/ppermute | solution.py:65
  20.9 1.6 %collective-permute-start.7 = (f32[328,128]{1,0:T(8,128)S(1)}, f32[328,128]{1,0:T(8,128)S(1)}, u32[]{:S(2)}, u32[]{:S(2)}) collective-permute-start(f32[328,128]{1,0:T(8,128)S(1)} %collective-permute-done.3.refs_6_), channel_id=1, source_target_pairs={{0,1},{1,0},{2,3},{3,2},{4,5},{5,4},{6,7},{7,6},{8,9},{9,8},{10,11... | collective-permute-start | bytes 503816 | tf_op jit(solution)/shard_map/ppermute | solution.py:65
  22.5 14.2 %copy-start.2 = (f32[9,1024]{1,0:T(8,128)S(1)}, f32[9,1024]{1,0:T(8,128)}, u32[]{:S(2)}) copy-start(f32[9,1024]{1,0:T(8,128)} %second.1) | copy-start | bytes 110596
  25.9 10.8 %copy-start = (f32[9,1024]{1,0:T(8,128)S(1)}, f32[9,1024]{1,0:T(8,128)}, u32[]{:S(2)}) copy-start(f32[9,1024]{1,0:T(8,128)} %params.1) | copy-start | bytes 110596
  25.9 10.8 %copy-start.1 = (f32[9,1024]{1,0:T(8,128)S(1)}, f32[9,1024]{1,0:T(8,128)}, u32[]{:S(2)}) copy-start(f32[9,1024]{1,0:T(8,128)} %moment.1) | copy-start | bytes 110596
